TPU v7x, 128 devices: a whole 4x4x4 slice. The times are simulated.
128 devices in a mesh: dp: 16 (over y, z), tensor: 8 (over x, core).
Axes of the slice: x: 4, y: 4, z: 4, core: 2. Of those that a mesh axis runs over, the one named last changes fastest.
Arguments:
- queries: bfloat16 [3, 1536, 4096], P(None, 'dp', 'tensor'), may hold values from -88 to 88
- draft_keys: bfloat16 [3, 1536, 1024], P(None, 'dp', 'tensor'), may hold values from -5 to 5
- draft_values: bfloat16 [3, 1536, 1024], P(None, 'dp', 'tensor'), may hold values from -5 to 5
- key_cache: bfloat16 [1536, 256, 1024], P('dp', None, 'tensor'), may hold values from -4 to 4
- value_cache: bfloat16 [1536, 256, 1024], P('dp', None, 'tensor'), may hold values from -5 to 5
- lengths: int32 [1536], P('dp'), may hold values from 2 to 256, as said below
- request_adapter: int32 [1536], P('dp'), may hold values from 0 to 255, as said below
- adapter_page_table: int32 [256], replicated, may hold values from 0 to 255, as said below
- output_weight: bfloat16 [4096, 8192], P('tensor'), may hold values from -0.09375 to 0.09375
- adapter_down: bfloat16 [256, 32, 4096], P('dp', None, 'tensor'), may hold values from -0.09375 to 0.09375
- adapter_up: bfloat16 [256, 32, 8192], P('dp', None, 'tensor'), may hold values from -1 to 1
Outputs:
- layer_out: bfloat16 [3, 1536, 8192], P(None, 'dp', 'tensor')
Inputs may be any that keep to these rules, and one draw needn't show every extreme that they name: A permutation: adapter a's factors are page adapter_page_table[a] of adapter_down and adapter_up, and page p lies with index p // 16 of dp. `request_adapter`: of the 96 requests of one index of dp, at most 12 use adapters whose pages one index of dp holds; one index of dp holds the pages of exactly 12 requests of every index of dp. `lengths`: some request has all 256 positions valid.
All inputs are finite; a program needn't handle non-finite values.
Results may differ from a plain program's by a relative error of at most 0.017.
Values may be sent and summed in bfloat16 or wider, within the bound.
No kernel may reach another device: no remote copies, remote signals or barrier semaphores. Data moves between devices by JAX's collectives and lax.ppermute only.
A program may use at most 192 MiB of HBM per device.

v0:
```python
import math

import jax
import jax.numpy as jnp
from jax import lax
from jax.sharding import PartitionSpec as P

HEAD_SIZE = 128


masked_score = -1e30


def attend(queries, draft_keys, draft_values, key_cache, value_cache, lengths):
    draft_count, total_rows, q_width = queries.shape
    cache_len = key_cache.shape[1]
    kv_count = key_cache.shape[2] // HEAD_SIZE
    group_size = q_width // HEAD_SIZE // kv_count
    score_scale = 1.0 / math.sqrt(HEAD_SIZE)
    grouped = queries.reshape(draft_count, total_rows, kv_count, group_size, HEAD_SIZE)
    keys_cache = key_cache.reshape(total_rows, cache_len, kv_count, HEAD_SIZE)
    vals_cache = value_cache.reshape(total_rows, cache_len, kv_count, HEAD_SIZE)
    keys_new = draft_keys.reshape(draft_count, total_rows, kv_count, HEAD_SIZE)
    vals_new = draft_values.reshape(draft_count, total_rows, kv_count, HEAD_SIZE)
    cache_scores = (
        jnp.einsum("sbkgd,blkd->sbkgl", grouped, keys_cache, preferred_element_type=jnp.float32)
        * score_scale
    )
    fresh_scores = (
        jnp.einsum("sbkgd,tbkd->sbkgt", grouped, keys_new, preferred_element_type=jnp.float32)
        * score_scale
    )
    visible = jnp.arange(cache_len)[None, :] < lengths[:, None]
    cache_scores = jnp.where(visible[None, :, None, None, :], cache_scores, masked_score)
    causal = jnp.arange(draft_count)[:, None] >= jnp.arange(draft_count)[None, :]
    fresh_scores = jnp.where(causal[:, None, None, None, :], fresh_scores, masked_score)
    top_score = jnp.maximum(jnp.max(cache_scores, axis=-1), jnp.max(fresh_scores, axis=-1))[
        ..., None
    ]
    cache_exp = jnp.exp(cache_scores - top_score)
    fresh_exp = jnp.exp(fresh_scores - top_score)
    denom = jnp.sum(cache_exp, axis=-1, keepdims=True) + jnp.sum(fresh_exp, axis=-1, keepdims=True)
    cache_weights = (cache_exp / denom).astype(jnp.bfloat16)
    fresh_weights = (fresh_exp / denom).astype(jnp.bfloat16)
    mixed = jnp.einsum(
        "sbkgl,blkd->sbkgd", cache_weights, vals_cache, preferred_element_type=jnp.float32
    )
    mixed = mixed + jnp.einsum(
        "sbkgt,tbkd->sbkgd", fresh_weights, vals_new, preferred_element_type=jnp.float32
    )
    return mixed.astype(jnp.bfloat16).reshape(draft_count, total_rows, q_width)


def body(
    queries,
    draft_keys,
    draft_values,
    key_cache,
    value_cache,
    lengths,
    request_adapter,
    adapter_page_table,
    output_weight,
    adapter_down,
    adapter_up,
):
    draft_count, total_rows, q_width = queries.shape
    local_model_part = adapter_up.shape[2]
    rank_width = adapter_down.shape[1]
    page_total = adapter_page_table.shape[0]
    attention_out = attend(queries, draft_keys, draft_values, key_cache, value_cache, lengths)
    flat_attn = attention_out.reshape(draft_count * total_rows, q_width)
    base_projection = lax.psum_scatter(
        lax.dot_general(
            output_weight, flat_attn, (((0,), (1,)), ((), ())), preferred_element_type=jnp.float32
        ).astype(jnp.bfloat16),
        "tensor",
        scatter_dimension=0,
        tiled=True,
    ).astype(jnp.float32)
    base_projection = jnp.transpose(base_projection).reshape(
        draft_count, total_rows, local_model_part
    )
    page_match = request_adapter[:, None] == jnp.arange(page_total, dtype=jnp.int32)[None, :]
    page_index = jnp.sum(jnp.where(page_match, adapter_page_table[None, :], 0), axis=1)
    local_rows = lax.all_gather(adapter_down, "dp", axis=0, tiled=True)
    span = local_rows.shape[0]
    selector = (page_index[:, None] == jnp.arange(span)[None, :]).astype(jnp.float32)
    product = lax.dot_general(
        flat_attn,
        local_rows.reshape(span * rank_width, q_width),
        (((1,), (1,)), ((), ())),
        preferred_element_type=jnp.float32,
    )
    product = product.reshape(draft_count, total_rows, span, rank_width)
    partial_value = jnp.sum(product * selector[None, :, :, None], axis=2)
    rank_mixture = lax.psum(partial_value, "tensor").astype(jnp.bfloat16)
    local_rows = lax.all_gather(adapter_up, "dp", axis=0, tiled=True)
    span = local_rows.shape[0]
    selector = (page_index[:, None] == jnp.arange(span)[None, :]).astype(jnp.bfloat16)
    spread = (rank_mixture[:, :, None, :] * selector[None, :, :, None]).reshape(
        draft_count * total_rows, span * rank_width
    )
    adapter_total = jnp.dot(
        spread,
        local_rows.reshape(span * rank_width, local_model_part),
        preferred_element_type=jnp.float32,
    )
    adapter_term = adapter_total.astype(jnp.bfloat16).reshape(
        draft_count, total_rows, local_model_part
    )
    return (base_projection + adapter_term.astype(jnp.float32)).astype(jnp.bfloat16)


def solution(mesh):
    placed = (
        P(None, "dp", "tensor"),
        P(None, "dp", "tensor"),
        P(None, "dp", "tensor"),
        P("dp", None, "tensor"),
        P("dp", None, "tensor"),
        P("dp"),
        P("dp"),
        P(),
        P("tensor", None),
        P("dp", None, "tensor"),
        P("dp", None, "tensor"),
    )
    return jax.shard_map(
        body, mesh=mesh, in_specs=placed, out_specs=P(None, "dp", "tensor"), check_vma=False
    )
```

profile of v0, /device:TPU:0, one launch (start us, length us, event | category | flops | bytes accessed | tf_op | source)
XLA Modules:
  0.0 215.8 jit_solution(13219174629485493423)
XLA Ops:
  7.4 0.0 copy-start
  7.4 0.0 all-gather.3.cloned.1.call-start
  7.4 2.2 copy.45
  9.5 0.0 all-gather.3.cloned.1.call-update
  9.6 0.0 reduce-scatter.2.cloned.1.call-start
  9.6 1.0 reshape.172
  10.7 0.7 iota_compare_fusion.2
  11.4 0.0 slice-start.2
  11.4 3.0 %fusion.41 = (f32[3,96,4]{2,0,1:T(4,128)S(1)}, f32[3,96,1,4,3]{3,4,0,1,2:T(4,128)S(1)}) fusion(bf16[3,96,4,128]{3,2,1,0:T(4,128)(2,1)S(1)} %reshape.172, bf16[3,96,128,1]{2,1,0,3:T(8,128)(2,1)} %bitcast.88, pred[3,3]{1,0:T(4,128)(4,1)S(1)} %iota_compare_fusion.3), kind=kOutput, calls=%fused_computation.49 | convolution fusion | flops 893952 | bytes 387081 | tf_op jit(solution)/shard_map/sbkgd,tbkd->sbkgt/dot_general | solution.py:30
  14.5 0.0 slice-start.3
  14.5 4.9 %bitcast_reduce_fusion = (f32[3,96,4]{2,0,1:T(4,128)S(1)}, f32[96,1,256,3,4]{2,4,3,0,1:T(4,128)S(1)}) fusion(bf16[3,96,4,128]{3,2,1,0:T(4,128)(2,1)S(1)} %reshape.172, bf16[96,256,128]{2,1,0:T(8,128)(2,1)} %param.14, pred[96,256]{1,0:T(8,128)(4,1)S(1)} %iota_compare_fusion.2), kind=kOutput, calls=%fused_computation.21 | convolution fusion | flops 76381056 | bytes 7795200 | tf_op jit(solution)/shard_map/sbkgd,blkd->sbkgl/dot_general | solution.py:26
  19.4 0.1 max.9
  19.4 0.6 fusion.29
  20.0 1.0 fusion.26
  20.9 0.0 slice-start
  20.9 0.1 add.22
  21.0 0.0 slice-done.2
  21.0 0.0 slice-done.3
  21.0 0.0 slice-start.1
  21.0 1.6 fusion.3
  22.7 0.0 copy-done
  22.7 0.6 fusion.21
  23.3 0.1 copy.43
  23.4 0.0 slice-done
  23.4 1.5 slice-done.1
  25.0 4.3 %fusion = bf16[8192,288]{0,1:T(8,128)(2,1)} fusion(bf16[512,8192]{1,0:T(8,128)(2,1)S(1)} %bitcast.85, bf16[36,8,4,128]{3,2,1,0:T(4,128)(2,1)S(1)} %bitcast.83), kind=kOutput, calls=%fused_computation.1 | convolution fusion | flops 2418278400 | bytes 13402112 | tf_op jit(solution)/shard_map/dot_general | solution.py:74
  29.3 0.0 copy-start.2
  29.3 0.0 copy-start.3
  29.3 0.0 reduce-scatter.2.cloned.1.call-update
  29.3 0.0 all-gather.5.cloned.1.call-start
  29.4 0.7 all-gather.5.cloned.1.call-update
  30.1 0.1 reshape.180
  30.2 0.0 copy-done.2
  30.2 0.0 copy-done.3
  30.2 0.2 select_reduce_fusion
  30.4 0.1 fusion.40
  30.5 0.1 copy.47
  30.6 53.1 %all-gather.3.cloned.1.call-done = bf16[256,32,512]{2,0,1:T(8,128)(2,1)} async-done(((bf16[16,32,512]{2,0,1:T(8,128)(2,1)}), bf16[256,32,512]{2,0,1:T(8,128)(2,1)}) %all-gather.3.cloned.1.call-update) | async-done | bytes 8388624 | tf_op jit(solution)/shard_map/all_gather | solution.py:86
  83.8 6.2 %multiply_reduce_fusion = f32[3,96,32]{1,2,0:T(8,128)S(1)} fusion(f32[96,256]{1,0:T(8,128)S(1)} %get-tuple-element.5, bf16[256,32,512]{2,0,1:T(8,128)(2,1)} %all-gather.3.cloned.1.call-done, bf16[3,96,512,1]{2,1,0,3:T(8,128)(2,1)S(1)} %reshape.180), kind=kOutput, calls=%fused_computation.2 | convolution fusion | flops 2420628480 | bytes 8818688 | tf_op jit(solution)/shard_map/dot_general | solution.py:89
  89.9 27.2 %psum.7 = bf16[3,96,32]{1,2,0:T(8,128)(2,1)S(1)} all-reduce(f32[3,96,32]{1,2,0:T(8,128)S(1)} %multiply_reduce_fusion), channel_id=1, replica_groups=mesh['dp'=16,'tensor'=8] {'tensor'}, use_global_device_ids=true, to_apply=%region_7.8 | all-reduce | flops 9216 | bytes 55296 | tf_op jit(solution)/shard_map/psum | solution.py:97
  117.1 6.2 %broadcast_multiply_fusion = bf16[3,96,256,32]{1,0,3,2:T(4,128)(2,1)} fusion(bf16[96,256]{0,1:T(8,128)(2,1)S(1)} %copy.47, bf16[3,96,32]{1,0,2:T(4,128)(2,1)S(1)} %copy.46), kind=kLoop, calls=%fused_computation.9 | loop fusion | flops 2359296 | bytes 4786176 | tf_op jit(solution)/shard_map/mul | solution.py:101
  123.4 17.1 %mul.65 = bf16[288,8192]{0,1:T(8,128)(2,1)} reshape(bf16[3,96,256,32]{1,0,3,2:T(4,128)(2,1)} %broadcast_multiply_fusion) | data formatting | bytes 9437184 | tf_op jit(solution)/shard_map/mul | solution.py:101
  140.5 0.0 reduce-scatter.2.cloned.1.call-done
  140.5 56.5 %all-gather.5.cloned.1.call-done = bf16[256,32,1024]{2,1,0:T(8,128)(2,1)} async-done(((bf16[16,32,1024]{2,1,0:T(8,128)(2,1)}), bf16[256,32,1024]{2,1,0:T(8,128)(2,1)}) %all-gather.5.cloned.1.call-update) | async-done | bytes 16777232 | tf_op jit(solution)/shard_map/all_gather | solution.py:98
  197.0 0.0 copy-start.1
  197.0 11.4 %fusion.11 = bf16[288,1024]{1,0:T(8,128)(2,1)} fusion(bf16[288,8192]{0,1:T(8,128)(2,1)} %mul.65, bf16[8192,1024]{1,0:T(8,128)(2,1)} %bitcast.82, bf16[1024,288]{0,1:T(8,128)(2,1)} %reduce-scatter.2.cloned.1.call-done), kind=kOutput, calls=%fused_computation.13 | convolution fusion | flops 4833312768 | bytes 22675456 | tf_op jit(solution)/shard_map/dot_general | solution.py:104
  208.4 0.0 copy-done.1
  (4 shorter events, 0.0 us)
Async XLA Ops:
  7.4 15.3 %copy-start = (bf16[3,96,128]{2,1,0:T(8,128)(2,1)S(1)}, bf16[3,96,128]{2,1,0:T(8,128)(2,1)}, u32[]{:S(2)}) copy-start(bf16[3,96,128]{2,1,0:T(8,128)(2,1)} %param.13) | copy-start | bytes 221188
  7.4 76.4 %all-gather.3.cloned.1.call-start = ((), (), s32[]{:S(2)}) async-start(), calls=%async_computation.2 | async-start | bytes 8912896 | tf_op jit(solution)/shard_map/all_gather | solution.py:86
  9.6 130.9 %reduce-scatter.2.cloned.1.call-start = ((), (), s32[]{:S(2)}) async-start(), calls=%async_computation.1 | async-start | bytes 5308416 | tf_op jit(solution)/shard_map/reduce_scatter | solution.py:73
  11.4 9.6 %slice-start.2 = ((s8[6291456]{0:T(1024)(128)(4,1)}), s8[4194304]{0:T(1024)(128)(4,1)S(1)}, s32[]{:S(2)}) async-start(s8[6291456]{0:T(1024)(128)(4,1)} %bitcast.86), calls=%async_computation.6 | async-start | bytes 8388608
  14.5 6.5 %slice-start.3 = ((s8[6291456]{0:T(1024)(128)(4,1)}), s8[2097152]{0:T(1024)(128)(4,1)S(1)}, s32[]{:S(2)}) async-start(s8[6291456]{0:T(1024)(128)(4,1)} %bitcast.86), calls=%async_computation.7 | async-start | bytes 4194304
  20.9 2.5 %slice-start = ((s8[8388608]{0:T(1024)(128)(4,1)}), s8[4194304]{0:T(1024)(128)(4,1)S(1)}, s32[]{:S(2)}) async-start(s8[8388608]{0:T(1024)(128)(4,1)} %bitcast.84), calls=%async_computation.4 | async-start | bytes 8388608
  21.0 3.9 %slice-start.1 = ((s8[8388608]{0:T(1024)(128)(4,1)}), s8[4194304]{0:T(1024)(128)(4,1)S(1)}, s32[]{:S(2)}) async-start(s8[8388608]{0:T(1024)(128)(4,1)} %bitcast.84), calls=%async_computation.5 | async-start | bytes 8388608
  29.3 0.9 copy-start.2
  29.3 0.9 copy-start.3
  29.3 167.6 %all-gather.5.cloned.1.call-start = ((), (), s32[]{:S(2)}) async-start(), calls=%async_computation.3 | async-start | bytes 17825792 | tf_op jit(solution)/shard_map/all_gather | solution.py:98
  197.0 11.4 %copy-start.1 = (bf16[3,96,128]{2,1,0:T(8,128)(2,1)S(1)}, bf16[3,96,128]{2,1,0:T(8,128)(2,1)}, u32[]{:S(2)}) copy-start(bf16[3,96,128]{2,1,0:T(8,128)(2,1)} %param.13) | copy-start | bytes 221188
Sparse Core Ops, SparseCore 0:
  10.4 73.3 all-gather.2
  85.9 111.0 all-gather.4
Sparse Core Ops, SparseCore 1:
  29.4 41.7 reduce-scatter.1
where the time goes:
time: 217 us; the launch traced here: 216 us
  waiting for transfers between devices  110 us (51%)
  matrix products  32 us (15%)
  blocking collectives  27.2 us (13%)
  local copies, waits for them, and re-layouts  22.2 us (10%)
  between operations  15 us (7%)
  other arithmetic  8.87 us (4%)
    all_gather x1, waiting for transfers between devices, body(): local_rows = lax.all_gather(adapter_up, 'dp', axis=0, tiled=True)  56.5 us
    all_gather x1, waiting for transfers between devices, body(): local_rows = lax.all_gather(adapter_down, 'dp', axis=0, tiled=True)  53.1 us
    psum x1, blocking collectives, body(): rank_mixture = lax.psum(partial_value, 'tensor').astype(jnp.bfloat16)  27.2 us
    mul x1, local copies, waits for them, and re-layouts, body(): rank_mixture[:, :, None, :] * selector[None, :, :, None]  17.1 us
    dot_general x1, matrix products, body(): jnp.dot(spread, local_rows.reshape(span * rank_width, local_model_part),...  11.4 us
    mul x1, other arithmetic, body(): rank_mixture[:, :, None, :] * selector[None, :, :, None]  6.24 us
    dot_general x1, matrix products, body(): lax.dot_general(flat_attn, local_rows.reshape(span * rank_width, q_width)...  6.16 us
    dot_general x1, matrix products, attend(): jnp.einsum('sbkgd,blkd->sbkgl', grouped, keys_cache, preferred_element_ty...  4.86 us
  transfers between devices with their start and end apart: 3, of which 2 were waited for; matrix products, arithmetic and copies ran while one was open for 22% of the time, Pallas kernels for 0%

commit v1 on v0

v1 whole, which is shorter than its diff:
```python
import functools, math
import jax, jax.numpy as jnp
from jax import lax
from jax.experimental import pallas as pl
from jax.experimental.pallas import tpu as pltpu
from jax.sharding import PartitionSpec as P

LANES = 128
STEP = 16
HALF = 8
VMEM = 63 * 1024 * 1024

def attend_kernel(slots, owner_rows, span, lengths, adapters, table, q, dk, dv, k, v, attn, payload, dest_out, kept):
    step = pl.program_id(0)
    drafts, _, width = q.shape
    cache = k.shape[1]
    heads = width // LANES
    rows = drafts * heads * HALF
    scale = math.log2(math.e) / math.sqrt(LANES)
    qf = q[...].astype(jnp.float32)
    dkf = dk[...].astype(jnp.float32)
    dvf = dv[...].astype(jnp.float32)
    sub = lax.broadcasted_iota(jnp.int32, (rows, cache), 0) % HALF
    lane8 = lax.broadcasted_iota(jnp.int32, (HALF, cache), 1)
    sub8 = lax.broadcasted_iota(jnp.int32, (HALF, cache), 0)
    drow = lax.broadcasted_iota(jnp.int32, (rows, drafts * HALF), 0)
    dlane = lax.broadcasted_iota(jnp.int32, (rows, drafts * HALF), 1)
    fresh_ok = (drow % HALF == dlane % HALF) & (dlane // HALF <= drow // (heads * HALF))
    outs = []
    for h in range(STEP // HALF):
        at = slice(h * HALF, (h + 1) * HALF)
        qb = jnp.concatenate([qf[s, at, g * LANES:(g + 1) * LANES] for s in range(drafts) for g in range(heads)], axis=0).astype(jnp.bfloat16)
        kb = jnp.concatenate([dkf[t, at] for t in range(drafts)], axis=0).astype(jnp.bfloat16)
        vb = jnp.concatenate([dvf[t, at] for t in range(drafts)], axis=0).astype(jnp.bfloat16)
        scores = None
        limit = jnp.zeros((HALF, cache), jnp.int32)
        for r in range(HALF):
            part = lax.dot_general(qb, k[h * HALF + r], (((1,), (1,)), ((), ())), preferred_element_type=jnp.float32)
            scores = part if r == 0 else jnp.where(sub == r, part, scores)
            limit = jnp.where(sub8 == r, lengths[step * STEP + h * HALF + r], limit)
        fresh = lax.dot_general(qb, kb, (((1,), (1,)), ((), ())), preferred_element_type=jnp.float32)
        seen = jnp.concatenate([(lane8 < limit).astype(jnp.int32)] * (drafts * heads), axis=0) > 0
        scores = jnp.where(seen, scores, -1e30)
        fresh = jnp.where(fresh_ok, fresh, -1e30)
        top = jnp.maximum(jnp.max(scores, axis=1, keepdims=True), jnp.max(fresh, axis=1, keepdims=True))
        e = jnp.exp2((scores - top) * scale)
        ef = jnp.exp2((fresh - top) * scale)
        total = jnp.sum(e, axis=1, keepdims=True) + jnp.sum(ef, axis=1, keepdims=True)
        inv = 1.0 / total
        w = e * inv
        wf = (ef * inv).astype(jnp.bfloat16)
        wide = jnp.concatenate([jnp.where(sub == r, w, 0.0).astype(jnp.bfloat16) for r in range(HALF)], axis=1)
        vals = v[h * HALF:(h + 1) * HALF].reshape(HALF * cache, LANES)
        mixed = jnp.dot(wide, vals, preferred_element_type=jnp.float32)
        mixed = mixed + jnp.dot(wf, vb, preferred_element_type=jnp.float32)
        outs.append(mixed)
    for s in range(drafts):
        for g in range(heads):
            at = (s * heads + g) * HALF
            piece = jnp.concatenate([o[at:at + HALF] for o in outs], axis=0).astype(jnp.bfloat16)
            attn[s, :, g * LANES:(g + 1) * LANES] = piece
            kept[s, pl.ds(pl.multiple_of(step * STEP, STEP), STEP), g * LANES:(g + 1) * LANES] = piece

    @pl.when(step == pl.num_programs(0) - 1)
    def _():
        count = adapters.shape[1]
        pages = table.shape[1]
        a = lax.broadcasted_iota(jnp.int32, (count, count), 0)
        b = lax.broadcasted_iota(jnp.int32, (count, count), 1)
        eye = a == b
        to_col = lambda row: jnp.sum(jnp.where(eye, jnp.broadcast_to(row, (count, count)), 0.0), axis=1, keepdims=True)
        to_row = lambda col: jnp.sum(jnp.where(eye, jnp.broadcast_to(col, (count, count)), 0.0), axis=0, keepdims=True)
        acol = to_col(adapters[...].astype(jnp.float32)).astype(jnp.int32)
        hit = acol == lax.broadcasted_iota(jnp.int32, (count, pages), 1)
        page = jnp.sum(jnp.where(hit, jnp.broadcast_to(table[...].astype(jnp.float32), (count, pages)), 0.0), axis=1, keepdims=True)
        prow = to_row(page).astype(jnp.int32)
        pcol = page.astype(jnp.int32)
        orow, ocol = prow // span, pcol // span
        rank = jnp.sum(jnp.where((ocol == orow) & (a < b), 1.0, 0.0), axis=0, keepdims=True).astype(jnp.int32)
        dest = orow * owner_rows + rank
        dest_col = jnp.sum(jnp.where((ocol == orow) & (b < a), 1.0, 0.0), axis=1, keepdims=True).astype(jnp.int32)
        dest_out[...] = jnp.broadcast_to(ocol * owner_rows + dest_col, dest_out.shape)
        place = lax.broadcasted_iota(jnp.int32, (payload.shape[0], count), 0)
        local = jnp.broadcast_to((pcol - ocol * span).astype(jnp.float32), (count, LANES)).astype(jnp.bfloat16)
        acc = None
        for s in range(drafts):
            pick = jnp.where(place == dest + s * slots, 1.0, 0.0).astype(jnp.bfloat16)
            rowsv = jnp.concatenate([kept[s], local], axis=1)
            part = jnp.dot(pick, rowsv, preferred_element_type=jnp.float32)
            acc = part if acc is None else acc + part
        payload[...] = acc.astype(jnp.bfloat16)

def attend(queries, draft_keys, draft_values, key_cache, value_cache, lengths, request_adapter, table, slots, owner_rows, owners, span):
    drafts, rows, width = queries.shape
    cache = key_cache.shape[1]
    return pl.pallas_call(
        functools.partial(attend_kernel, slots, owner_rows, span),
        grid=(rows // STEP,),
        in_specs=[
            pl.BlockSpec(memory_space=pltpu.SMEM),
            pl.BlockSpec((1, rows), lambda i: (0, 0)),
            pl.BlockSpec((1, table.shape[0]), lambda i: (0, 0)),
            pl.BlockSpec((drafts, STEP, width), lambda i: (0, i, 0)),
            pl.BlockSpec((drafts, STEP, LANES), lambda i: (0, i, 0)),
            pl.BlockSpec((drafts, STEP, LANES), lambda i: (0, i, 0)),
            pl.BlockSpec((STEP, cache, LANES), lambda i: (i, 0, 0)),
            pl.BlockSpec((STEP, cache, LANES), lambda i: (i, 0, 0)),
        ],
        out_specs=[
            pl.BlockSpec((drafts, STEP, width), lambda i: (0, i, 0)),
            pl.BlockSpec((owners * owner_rows, width + LANES), lambda i: (0, 0)),
            pl.BlockSpec((rows, LANES), lambda i: (0, 0)),
        ],
        out_shape=[
            jax.ShapeDtypeStruct((drafts, rows, width), jnp.bfloat16),
            jax.ShapeDtypeStruct((owners * owner_rows, width + LANES), jnp.bfloat16),
            jax.ShapeDtypeStruct((rows, LANES), jnp.int32),
        ],
        scratch_shapes=[pltpu.VMEM((drafts, rows, width), jnp.bfloat16)],
        compiler_params=pltpu.CompilerParams(vmem_limit_bytes=VMEM),
        name="attend",
    )(lengths, request_adapter.reshape(1, rows), table.reshape(1, -1), queries, draft_keys, draft_values, key_cache, value_cache)


def base_kernel(attn, weight, out):
    drafts, rows, width = attn.shape
    out[0] = jnp.dot(
        attn[...].reshape(drafts * rows, width), weight[...], preferred_element_type=jnp.float32
    ).astype(jnp.bfloat16)


def project(attn, weight, parts):
    drafts, rows, width = attn.shape
    part = weight.shape[1] // parts
    return pl.pallas_call(
        base_kernel,
        grid=(parts,),
        in_specs=[
            pl.BlockSpec((drafts, rows, width), lambda j: (0, 0, 0)),
            pl.BlockSpec((width, part), lambda j: (0, j)),
        ],
        out_specs=pl.BlockSpec((1, drafts * rows, part), lambda j: (j, 0, 0)),
        out_shape=jax.ShapeDtypeStruct((parts, drafts * rows, part), jnp.bfloat16),
        compiler_params=pltpu.CompilerParams(vmem_limit_bytes=VMEM),
        name="project",
    )(attn, weight)


def down_kernel(arrived, down, mix):
    width = down.shape[1]
    span = down.shape[0] // mix.shape[0]
    product = lax.dot_general(
        down[...], arrived[:, :width], (((1,), (1,)), ((), ())), preferred_element_type=jnp.float32
    )
    ones = jnp.ones((8, LANES), jnp.bfloat16)
    page = lax.dot_general(
        ones, arrived[:, width:], (((1,), (1,)), ((), ())), preferred_element_type=jnp.float32
    )[:1] * (1.0 / LANES)
    rank = mix.shape[0]
    total = jnp.zeros(mix.shape, jnp.float32)
    for p in range(span):
        total = total + jnp.where(page == float(p), product[p * rank:(p + 1) * rank], 0.0)
    mix[...] = total


def down_mix(arrived, down):
    rows = arrived.shape[0]
    span, rank, width = down.shape
    return pl.pallas_call(
        down_kernel,
        out_shape=jax.ShapeDtypeStruct((rank, rows), jnp.float32),
        compiler_params=pltpu.CompilerParams(vmem_limit_bytes=VMEM),
        name="down_mix",
    )(arrived, down.reshape(span * rank, width))


def up_kernel(mine, one, two, three, arrived, up, out):
    rank = mine.shape[0]
    spread_width = up.shape[0]
    mix = (
        mine[...].astype(jnp.float32)
        + one[...].astype(jnp.float32)
        + two[...].astype(jnp.float32)
        + three[...].astype(jnp.float32)
    ).astype(jnp.bfloat16)
    a = lax.broadcasted_iota(jnp.int32, (rank, spread_width), 0)
    b = lax.broadcasted_iota(jnp.int32, (rank, spread_width), 1)
    repeat = jnp.where(b % rank == a, 1.0, 0.0).astype(jnp.bfloat16)
    spread = lax.dot_general(
        mix, repeat, (((0,), (0,)), ((), ())), preferred_element_type=jnp.float32
    )
    meta = arrived[...].astype(jnp.float32)
    pieces = []
    for j in range(spread_width // LANES):
        lane = lax.broadcasted_iota(jnp.int32, meta.shape, 1) + j * LANES
        same = meta == (lane // rank).astype(jnp.float32)
        pieces.append(jnp.where(same, spread[:, j * LANES:(j + 1) * LANES], 0.0).astype(jnp.bfloat16))
    out[...] = jnp.dot(
        jnp.concatenate(pieces, axis=1), up[...], preferred_element_type=jnp.float32
    ).astype(jnp.bfloat16)


def up_terms(mixes, arrived, up):
    rows, full = arrived.shape
    span, rank, width = up.shape
    mix_spec = pl.BlockSpec((rank, rows), lambda i: (0, 0))
    return pl.pallas_call(
        up_kernel,
        grid=(1,),
        in_specs=[mix_spec] * 4
        + [
            pl.BlockSpec((rows, LANES), lambda i: (0, full // LANES - 1)),
            pl.BlockSpec((span * rank, width), lambda i: (0, 0)),
        ],
        out_specs=pl.BlockSpec((rows, width), lambda i: (0, 0)),
        out_shape=jax.ShapeDtypeStruct((rows, width), jnp.bfloat16),
        compiler_params=pltpu.CompilerParams(vmem_limit_bytes=VMEM),
        name="up_terms",
    )(*mixes, arrived, up.reshape(span * rank, width))


def finish_kernel(slots, base, terms, dest, out):
    drafts, rows, width = out.shape
    places = terms.shape[0]
    lane = lax.broadcasted_iota(jnp.int32, (rows, places), 1)
    where_to = dest[:, :1]
    for s in range(drafts):
        pick = jnp.where(lane == where_to + s * slots, 1.0, 0.0).astype(jnp.bfloat16)
        term = jnp.dot(pick, terms[...], preferred_element_type=jnp.float32)
        out[s] = (base[s * rows:(s + 1) * rows].astype(jnp.float32) + term).astype(jnp.bfloat16)


def finish(base, terms, dest, drafts, slots):
    rows = dest.shape[0]
    width = base.shape[1]
    return pl.pallas_call(
        functools.partial(finish_kernel, slots),
        out_shape=jax.ShapeDtypeStruct((drafts, rows, width), jnp.bfloat16),
        compiler_params=pltpu.CompilerParams(vmem_limit_bytes=VMEM),
        name="finish",
    )(base, terms, dest)


def body(
    queries,
    draft_keys,
    draft_values,
    key_cache,
    value_cache,
    lengths,
    request_adapter,
    adapter_page_table,
    output_weight,
    adapter_down,
    adapter_up,
):
    drafts, rows, width = queries.shape
    owners = lax.axis_size("dp")
    parts = lax.axis_size("tensor")
    span, rank, _ = adapter_down.shape
    slots = rows // 8
    owner_rows = -(-drafts * slots // 8) * 8
    attn, payload, dest = attend(
        queries, draft_keys, draft_values, key_cache, value_cache, lengths, request_adapter,
        adapter_page_table, slots, owner_rows, owners, span,
    )
    partial_base = project(attn, output_weight, parts)
    base = lax.psum_scatter(partial_base, "tensor", scatter_dimension=0, tiled=False)
    arrived = lax.all_to_all(
        payload.reshape(owners, owner_rows, -1), "dp", 0, 0, tiled=True
    ).reshape(owners * owner_rows, -1)
    mine = down_mix(arrived, adapter_down)
    chips = parts // 2
    other = lax.ppermute(mine, "tensor", [(i, i ^ 1) for i in range(parts)])
    pair = (mine + other).astype(jnp.bfloat16)
    mixes = [pair] + [
        lax.ppermute(pair, "tensor", [(2 * x + c, 2 * ((x + k) % chips) + c) for x in range(chips) for c in range(2)])
        for k in range(1, chips)
    ]
    terms = up_terms(mixes, arrived, adapter_up)
    terms = lax.all_to_all(
        terms.reshape(owners, owner_rows, -1), "dp", 0, 0, tiled=True
    ).reshape(owners * owner_rows, -1)
    return finish(base, terms, dest, drafts, slots)


def solution(mesh):
    placed = (
        P(None, "dp", "tensor"),
        P(None, "dp", "tensor"),
        P(None, "dp", "tensor"),
        P("dp", None, "tensor"),
        P("dp", None, "tensor"),
        P("dp"),
        P("dp"),
        P(),
        P("tensor", None),
        P("dp", None, "tensor"),
        P("dp", None, "tensor"),
    )
    return jax.shard_map(
        body, mesh=mesh, in_specs=placed, out_specs=P(None, "dp", "tensor"), check_vma=False
    )
```

time: 217 us -> 103 us (0.47)
  waiting for transfers between devices: 110 us -> 4.69 us
  matrix products: 32 us -> 0 us
  Pallas kernels: 0 us -> 30.9 us
  local copies, waits for them, and re-layouts: 22.2 us -> 0.62 us
  blocking collectives: 27.2 us -> 45.9 us
  other arithmetic: 8.87 us -> 0.9 us
  starting transfers between devices: 0.09 us -> 5.66 us
    all_gather x2 -> x0, waiting for transfers between devices: 110 us -> none  [the longest x1 56.5 us: body(): local_rows = lax.all_gather(adapter_up, 'dp', axis=0, tiled=True)]
    all_to_all x0 -> x2, blocking collectives: none -> 45.9 us  [the longest x1 23.4 us: body(): lax.all_to_all(terms.reshape(owners, owner_rows, -1), 'dp', 0, 0, tiled=T...]
    dot_general x7 -> x0, matrix products: 32 us -> none  [the longest x1 11.4 us: body(): jnp.dot(spread, local_rows.reshape(span * rank_width, local_model_part),...]
    pallas_call x0 -> x5, Pallas kernels: none -> 30.9 us  [the longest x1 12.2 us: attend(): pl.pallas_call(functools.partial(attend_kernel, slots, owner_rows, span),...]
    psum x1 -> x0, blocking collectives: 27.2 us -> none  [body(): rank_mixture = lax.psum(partial_value, 'tensor').astype(jnp.bfloat16)]
    mul x1 -> x0, local copies, waits for them, and re-layouts: 17.1 us -> none  [body(): rank_mixture[:, :, None, :] * selector[None, :, :, None]]
    mul x1 -> x0, other arithmetic: 6.24 us -> none  [body(): rank_mixture[:, :, None, :] * selector[None, :, :, None]]
    ppermute x0 -> x4, starting transfers between devices: none -> 5.65 us  [the longest x3 5.65 us: body(): lax.ppermute(pair, 'tensor', [(2 * x + c, 2 * ((x + k) % chips) + c) for...]
  transfers between devices with their start and end apart: 3 -> 5, of which waited for: 2 -> 3; matrix products, arithmetic and copies ran while one was open for 22% -> 1% of each run, Pallas kernels for 0% -> 6%
where the time goes in v1:
time: 103 us; the launch traced here: 102 us
  blocking collectives  45.9 us (45%)
  Pallas kernels  30.9 us (30%)
  between operations  13.4 us (13%)
  starting transfers between devices  5.66 us (5%)
  waiting for transfers between devices  4.69 us (5%)
    all_to_all x1, blocking collectives, body(): lax.all_to_all(terms.reshape(owners, owner_rows, -1), 'dp', 0, 0, tiled=T...  23.4 us
    all_to_all x1, blocking collectives, body(): lax.all_to_all(payload.reshape(owners, owner_rows, -1), 'dp', 0, 0, tiled...  22.5 us
    pallas_call x1, Pallas kernels, attend(): pl.pallas_call(functools.partial(attend_kernel, slots, owner_rows, span),...  12.2 us
    pallas_call x1, Pallas kernels, project(): pl.pallas_call(base_kernel, grid=(parts,), in_specs=[pl.BlockSpec((drafts...  9.29 us
    ppermute x3, starting transfers between devices, body(): lax.ppermute(pair, 'tensor', [(2 * x + c, 2 * ((x + k) % chips) + c) for...  5.65 us
    pallas_call x1, Pallas kernels, up_terms(): pl.pallas_call(up_kernel, grid=(1,), in_specs=[mix_spec] * 4 + [pl.BlockS...  3.59 us
    pallas_call x1, Pallas kernels, finish(): pl.pallas_call(functools.partial(finish_kernel, slots), out_shape=jax.Sha...  3.15 us
    ppermute x3, waiting for transfers between devices, body(): lax.ppermute(pair, 'tensor', [(2 * x + c, 2 * ((x + k) % chips) + c) for...  3.09 us
  transfers between devices with their start and end apart: 5, of which 3 were waited for; matrix products, arithmetic and copies ran while one was open for 1% of the time, Pallas kernels for 6%

profile of v1, /device:TPU:0, one launch (start us, length us, event | category | flops | bytes accessed | tf_op | source)
XLA Modules:
  0.0 102.1 jit_solution(12309153738926806512)
XLA Ops:
  6.5 0.0 reduce-scatter.2.cloned.1.call-start
  6.5 12.2 %attend.1 = (bf16[3,96,512]{2,1,0:T(8,128)(2,1)}, bf16[640,640]{1,0:T(8,128)(2,1)}, s32[96,128]{1,0:T(8,128)}) custom-call(s32[96]{0:T(128)} %lengths.1, s32[1,96]{1,0:T(1,128)} %bitcast.18, s32[1,256]{1,0:T(1,128)} %bitcast.17, bf16[3,96,512]{2,1,0:T(8,128)(2,1)} %q.1, bf16[3,96,128]{2,1,0:T(8,128)(2,1)} %dk.1, bf16[3,96,128]{2,1,0:T(8,128)(2,1)} %dv.1, ...), custom_call_target="tpu_custom_call" | custom-call | tf_op jit(solution)/shard_map/attend/pallas_call | solution.py:96
  18.7 0.0 copy-start
  18.8 9.3 %project.1 = bf16[8,288,1024]{2,1,0:T(8,128)(2,1)} custom-call(bf16[3,96,512]{2,1,0:T(8,128)(2,1)} %get-tuple-element.8.attn, bf16[512,8192]{1,0:T(8,128)(2,1)} %weight.1), custom_call_target="tpu_custom_call" | custom-call | tf_op jit(solution)/shard_map/project/pallas_call | solution.py:135
  28.0 0.0 reduce-scatter.2.cloned.1.call-update
  28.1 0.0 copy-done
  28.1 22.5 %all_to_all.10 = bf16[16,40,640]{2,1,0:T(8,128)(2,1)} all-to-all(bf16[16,40,640]{2,1,0:T(8,128)(2,1)S(1)} %bitcast.14), channel_id=1, replica_groups=mesh['dp'=16,'tensor'=8] {'dp'}, dimensions={0} | all-to-all | bytes 1638400 | tf_op jit(solution)/shard_map/all_to_all | solution.py:269
  50.6 2.6 %down_mix.1 = f32[32,640]{1,0:T(8,128)} custom-call(bf16[640,640]{1,0:T(8,128)(2,1)} %bitcast.9, bf16[512,512]{1,0:T(8,128)(2,1)} %bitcast.16), custom_call_target="tpu_custom_call" | custom-call | tf_op jit(solution)/shard_map/down_mix/pallas_call | solution.py:169
  53.2 0.0 collective-permute-start
  53.2 1.6 %collective-permute-done = f32[32,640]{1,0:T(8,128)S(1)} collective-permute-done((f32[32,640]{1,0:T(8,128)}, f32[32,640]{1,0:T(8,128)S(1)}, u32[]{:S(2)}, u32[]{:S(2)}) %collective-permute-start) | collective-permute-done | bytes 81952 | tf_op jit(solution)/shard_map/ppermute | solution.py:274
  54.8 0.9 add_convert_fusion.mine
  55.7 0.0 copy-start.1
  55.7 1.5 %collective-permute-start.1 = (bf16[32,640]{1,0:T(8,128)(2,1)S(1)}, bf16[32,640]{1,0:T(8,128)(2,1)S(1)}, u32[]{:S(2)}, u32[]{:S(2)}) collective-permute-start(bf16[32,640]{1,0:T(8,128)(2,1)S(1)} %add_convert_fusion.mine), channel_id=1, source_target_pairs={{0,2},{1,3},{2,4},{3,5},{4,6},{5,7},{6,0},{7,1},{8,10},{9,11},{10,... | collective-permute-start | bytes 122888 | tf_op jit(solution)/shard_map/ppermute | solution.py:277
  57.2 2.7 %collective-permute-start.2 = (bf16[32,640]{1,0:T(8,128)(2,1)S(1)}, bf16[32,640]{1,0:T(8,128)(2,1)S(1)}, u32[]{:S(2)}, u32[]{:S(2)}) collective-permute-start(bf16[32,640]{1,0:T(8,128)(2,1)S(1)} %add_convert_fusion.mine), channel_id=1, source_target_pairs={{0,4},{1,5},{2,6},{3,7},{4,0},{5,1},{6,2},{7,3},{8,12},{9,13},{10,... | collective-permute-start | bytes 122888 | tf_op jit(solution)/shard_map/ppermute | solution.py:277
  59.9 1.4 %collective-permute-start.3 = (bf16[32,640]{1,0:T(8,128)(2,1)S(1)}, bf16[32,640]{1,0:T(8,128)(2,1)S(1)}, u32[]{:S(2)}, u32[]{:S(2)}) collective-permute-start(bf16[32,640]{1,0:T(8,128)(2,1)S(1)} %add_convert_fusion.mine), channel_id=1, source_target_pairs={{0,6},{1,7},{2,0},{3,1},{4,2},{5,3},{6,4},{7,5},{8,14},{9,15},{10,... | collective-permute-start | bytes 122888 | tf_op jit(solution)/shard_map/ppermute | solution.py:277
  61.4 0.0 collective-permute-done.1.one
  61.4 0.0 copy-start.2
  61.4 2.2 %collective-permute-done.2.two = bf16[32,640]{1,0:T(8,128)(2,1)S(1)} collective-permute-done((bf16[32,640]{1,0:T(8,128)(2,1)S(1)}, bf16[32,640]{1,0:T(8,128)(2,1)S(1)}, u32[]{:S(2)}, u32[]{:S(2)}) %collective-permute-start.2) | collective-permute-done | bytes 40992 | tf_op jit(solution)/shard_map/ppermute | solution.py:277
  63.6 0.0 copy-start.3
  63.6 0.8 collective-permute-done.3.three
  64.5 0.0 copy-start.4
  64.5 0.0 copy-done.1
  64.5 0.0 copy-done.2
  64.5 0.0 copy-done.3
  64.5 0.6 copy-done.4
  65.1 3.6 %up_terms.1 = bf16[640,1024]{1,0:T(8,128)(2,1)} custom-call(bf16[32,640]{1,0:T(8,128)(2,1)} %copy-done.1, bf16[32,640]{1,0:T(8,128)(2,1)} %copy-done.2, bf16[32,640]{1,0:T(8,128)(2,1)} %copy-done.3, bf16[32,640]{1,0:T(8,128)(2,1)} %copy-done.4, bf16[640,640]{1,0:T(8,128)(2,1)} %bitcast.10, bf16[512,1024]{1,0:T(8,128)(2,1)} %bitcast.13), custom_call_target="tpu_custom_call" | custom-call | tf_op jit(solution)/shard_map/up_terms/pallas_call | solution.py:207
  68.7 23.4 %all_to_all.11 = bf16[16,40,1024]{2,1,0:T(8,128)(2,1)} all-to-all(bf16[16,40,1024]{2,1,0:T(8,128)(2,1)} %bitcast.11), channel_id=1, replica_groups=mesh['dp'=16,'tensor'=8] {'dp'}, dimensions={0} | all-to-all | bytes 2621440 | tf_op jit(solution)/shard_map/all_to_all | solution.py:281
  92.1 0.0 reduce-scatter.2.cloned.1.call-done
  92.1 3.1 %finish.1 = bf16[3,96,1024]{2,1,0:T(8,128)(2,1)} custom-call(bf16[288,1024]{1,0:T(8,128)(2,1)} %bitcast.15, bf16[640,1024]{1,0:T(8,128)(2,1)} %bitcast.12, s32[96,128]{1,0:T(8,128)} %get-tuple-element.10.dest), custom_call_target="tpu_custom_call" | custom-call | tf_op jit(solution)/shard_map/finish/pallas_call | solution.py:236
Async XLA Ops:
  6.5 85.5 %reduce-scatter.2.cloned.1.call-start = ((), (), s32[]{:S(2)}) async-start(), calls=%async_computation.3 | async-start | bytes 5308416 | tf_op jit(solution)/shard_map/reduce_scatter | solution.py:268
  18.7 9.3 %copy-start = (bf16[640,640]{1,0:T(8,128)(2,1)S(1)}, bf16[640,640]{1,0:T(8,128)(2,1)}, u32[]{:S(2)}) copy-start(bf16[640,640]{1,0:T(8,128)(2,1)} %get-tuple-element.9) | copy-start | bytes 2457604
  53.2 1.6 %collective-permute-start = (f32[32,640]{1,0:T(8,128)}, f32[32,640]{1,0:T(8,128)S(1)}, u32[]{:S(2)}, u32[]{:S(2)}) collective-permute-start(f32[32,640]{1,0:T(8,128)} %down_mix.1), channel_id=1, source_target_pairs={{0,1},{1,0},{2,3},{3,2},{4,5},{5,4},{6,7},{7,6},{8,9},{9,8},{10,11... | collective-permute-start | bytes 245768 | tf_op jit(solution)/shard_map/ppermute | solution.py:274
  55.7 8.8 %copy-start.1 = (bf16[32,640]{1,0:T(8,128)(2,1)}, bf16[32,640]{1,0:T(8,128)(2,1)S(1)}, u32[]{:S(2)}) copy-start(bf16[32,640]{1,0:T(8,128)(2,1)S(1)} %add_convert_fusion.mine) | copy-start | bytes 122884
  55.7 5.7 %collective-permute-start.1 = (bf16[32,640]{1,0:T(8,128)(2,1)S(1)}, bf16[32,640]{1,0:T(8,128)(2,1)S(1)}, u32[]{:S(2)}, u32[]{:S(2)}) collective-permute-start(bf16[32,640]{1,0:T(8,128)(2,1)S(1)} %add_convert_fusion.mine), channel_id=1, source_target_pairs={{0,2},{1,3},{2,4},{3,5},{4,6},{5,7},{6,0},{7,1},{8,10},{9,11},{10,... | collective-permute-start | bytes 122888 | tf_op jit(solution)/shard_map/ppermute | solution.py:277
  57.2 6.4 %collective-permute-start.2 = (bf16[32,640]{1,0:T(8,128)(2,1)S(1)}, bf16[32,640]{1,0:T(8,128)(2,1)S(1)}, u32[]{:S(2)}, u32[]{:S(2)}) collective-permute-start(bf16[32,640]{1,0:T(8,128)(2,1)S(1)} %add_convert_fusion.mine), channel_id=1, source_target_pairs={{0,4},{1,5},{2,6},{3,7},{4,0},{5,1},{6,2},{7,3},{8,12},{9,13},{10,... | collective-permute-start | bytes 122888 | tf_op jit(solution)/shard_map/ppermute | solution.py:277
  59.9 4.5 %collective-permute-start.3 = (bf16[32,640]{1,0:T(8,128)(2,1)S(1)}, bf16[32,640]{1,0:T(8,128)(2,1)S(1)}, u32[]{:S(2)}, u32[]{:S(2)}) collective-permute-start(bf16[32,640]{1,0:T(8,128)(2,1)S(1)} %add_convert_fusion.mine), channel_id=1, source_target_pairs={{0,6},{1,7},{2,0},{3,1},{4,2},{5,3},{6,4},{7,5},{8,14},{9,15},{10,... | collective-permute-start | bytes 122888 | tf_op jit(solution)/shard_map/ppermute | solution.py:277
  61.4 3.1 %copy-start.2 = (bf16[32,640]{1,0:T(8,128)(2,1)}, bf16[32,640]{1,0:T(8,128)(2,1)S(1)}, u32[]{:S(2)}) copy-start(bf16[32,640]{1,0:T(8,128)(2,1)S(1)} %collective-permute-done.1.one) | copy-start | bytes 122884
  63.6 0.8 copy-start.3
  64.5 0.6 copy-start.4
Sparse Core Ops, SparseCore 0:
  28.2 42.9 reduce-scatter.1

commit v2 on v1

--- a/solution.py
+++ b/solution.py
@@ -8,6 +8,7 @@
 LANES = 128
 STEP = 16
 HALF = 8
+AHEAD = (2, 1, 3, 0)
 VMEM = 63 * 1024 * 1024
 
 def attend_kernel(slots, owner_rows, span, lengths, adapters, table, q, dk, dv, k, v, attn, payload, dest_out, kept):
@@ -118,32 +119,97 @@
         ],
         scratch_shapes=[pltpu.VMEM((drafts, rows, width), jnp.bfloat16)],
         compiler_params=pltpu.CompilerParams(vmem_limit_bytes=VMEM),
+        cost_estimate=pl.CostEstimate(
+            flops=8 * queries.size * cache, bytes_accessed=4 * key_cache.size, transcendentals=0
+        ),
         name="attend",
     )(lengths, request_adapter.reshape(1, rows), table.reshape(1, -1), queries, draft_keys, draft_values, key_cache, value_cache)
 
 
-def base_kernel(attn, weight, out):
+def fetch_blocks(weight, held, sems, other_core):
+    place = lax.axis_index("tensor")
+    chips, _, part = held.shape
+    core = place % 2
+    core = 1 - core if other_core else core
+    fetches = []
+    for j, ahead in enumerate(AHEAD):
+        block = (place // 2 + ahead) % chips * 2 + core
+        fetches.append(
+            pltpu.make_async_copy(
+                weight.at[:, pl.ds(pl.multiple_of(block * part, part), part)], held.at[j], sems.at[j]
+            )
+        )
+        fetches[-1].start()
+    return fetches
+
+
+def sent_kernel(attn, weight, out, held, sems):
     drafts, rows, width = attn.shape
-    out[0] = jnp.dot(
-        attn[...].reshape(drafts * rows, width), weight[...], preferred_element_type=jnp.float32
-    ).astype(jnp.bfloat16)
-
-
-def project(attn, weight, parts):
+    fetches = fetch_blocks(weight, held, sems, True)
+    flat = attn[...].reshape(drafts * rows, width)
+    for j, fetch in enumerate(fetches):
+        fetch.wait()
+        out[j] = jnp.dot(flat, held[j], preferred_element_type=jnp.float32).astype(jnp.bfloat16)
+
+
+def kept_kernel(attn, weight, other, far_up, far_down, up, down, own, held, sems):
+    drafts, rows, width = attn.shape
+    half = drafts * rows // 2
+    fetches = fetch_blocks(weight, held, sems, False)
+    flat = attn[...].reshape(drafts * rows, width)
+    for j, fetch in enumerate(fetches):
+        fetch.wait()
+        total = jnp.dot(flat, held[j], preferred_element_type=jnp.float32)
+        total = (total + other[j].astype(jnp.float32)).astype(jnp.bfloat16)
+        if j == 0:
+            far_up[...] = total[:half]
+            far_down[...] = total[half:]
+        else:
+            (up, down, own)[j - 1][...] = total
+
+
+def project(attn, weight, other, parts):
     drafts, rows, width = attn.shape
     part = weight.shape[1] // parts
-    return pl.pallas_call(
-        base_kernel,
-        grid=(parts,),
-        in_specs=[
-            pl.BlockSpec((drafts, rows, width), lambda j: (0, 0, 0)),
-            pl.BlockSpec((width, part), lambda j: (0, j)),
-        ],
-        out_specs=pl.BlockSpec((1, drafts * rows, part), lambda j: (j, 0, 0)),
-        out_shape=jax.ShapeDtypeStruct((parts, drafts * rows, part), jnp.bfloat16),
-        compiler_params=pltpu.CompilerParams(vmem_limit_bytes=VMEM),
-        name="project",
-    )(attn, weight)
+    chips = parts // 2
+    full = (drafts * rows, part)
+    half = (drafts * rows // 2, part)
+    shapes = [(chips,) + full] if other is None else [half, half, full, full, full]
+    ins = [attn, weight] + ([] if other is None else [other])
+    vmem = pl.BlockSpec(memory_space=pltpu.VMEM)
+    return pl.pallas_call(
+        sent_kernel if other is None else kept_kernel,
+        in_specs=[vmem, pl.BlockSpec(memory_space=pltpu.HBM)] + [vmem] * (len(ins) - 2),
+        out_specs=[vmem] * len(shapes),
+        out_shape=[jax.ShapeDtypeStruct(s, jnp.bfloat16) for s in shapes],
+        scratch_shapes=[
+            pltpu.VMEM((chips, width, part), jnp.bfloat16),
+            pltpu.SemaphoreType.DMA((chips,)),
+        ],
+        compiler_params=pltpu.CompilerParams(vmem_limit_bytes=VMEM * 8 // 9),
+        cost_estimate=pl.CostEstimate(flops=1, bytes_accessed=1, transcendentals=0),
+        name="project_sent" if other is None else "project_kept",
+    )(*ins)
+
+
+def merge_kernel(up, down, far_up, far_down, up_out, down_out):
+    half = far_up.shape[0]
+    add = lambda a, b: (a.astype(jnp.float32) + b.astype(jnp.float32)).astype(jnp.bfloat16)
+    up_out[:half] = add(up[:half], far_up[...])
+    up_out[half:] = up[half:]
+    down_out[:half] = down[:half]
+    down_out[half:] = add(down[half:], far_down[...])
+
+
+def merge(up, down, far_up, far_down):
+    shape = jax.ShapeDtypeStruct(up.shape, up.dtype)
+    return pl.pallas_call(
+        merge_kernel,
+        out_shape=[shape, shape],
+        compiler_params=pltpu.CompilerParams(vmem_limit_bytes=VMEM // 4),
+        cost_estimate=pl.CostEstimate(flops=0, bytes_accessed=10 * up.size, transcendentals=0),
+        name="merge",
+    )(up, down, far_up, far_down)
 
 
 def down_kernel(arrived, down, mix):
@@ -169,7 +235,8 @@
     return pl.pallas_call(
         down_kernel,
         out_shape=jax.ShapeDtypeStruct((rank, rows), jnp.float32),
-        compiler_params=pltpu.CompilerParams(vmem_limit_bytes=VMEM),
+        compiler_params=pltpu.CompilerParams(vmem_limit_bytes=VMEM // 4),
+        cost_estimate=pl.CostEstimate(flops=2 * rows * down.size, bytes_accessed=2 * (arrived.size + down.size), transcendentals=0),
         name="down_mix",
     )(arrived, down.reshape(span * rank, width))
 
@@ -214,31 +281,37 @@
         ],
         out_specs=pl.BlockSpec((rows, width), lambda i: (0, 0)),
         out_shape=jax.ShapeDtypeStruct((rows, width), jnp.bfloat16),
-        compiler_params=pltpu.CompilerParams(vmem_limit_bytes=VMEM),
+        compiler_params=pltpu.CompilerParams(vmem_limit_bytes=VMEM // 4),
+        cost_estimate=pl.CostEstimate(flops=2 * rows * up.size, bytes_accessed=2 * (up.size + rows * width), transcendentals=0),
         name="up_terms",
     )(*mixes, arrived, up.reshape(span * rank, width))
 
 
-def finish_kernel(slots, base, terms, dest, out):
+def finish_kernel(slots, own, from_below, from_above, terms, dest, out):
     drafts, rows, width = out.shape
     places = terms.shape[0]
     lane = lax.broadcasted_iota(jnp.int32, (rows, places), 1)
     where_to = dest[:, :1]
     for s in range(drafts):
         pick = jnp.where(lane == where_to + s * slots, 1.0, 0.0).astype(jnp.bfloat16)
-        term = jnp.dot(pick, terms[...], preferred_element_type=jnp.float32)
-        out[s] = (base[s * rows:(s + 1) * rows].astype(jnp.float32) + term).astype(jnp.bfloat16)
-
-
-def finish(base, terms, dest, drafts, slots):
+        total = jnp.dot(pick, terms[...], preferred_element_type=jnp.float32)
+        for ref in (own, from_below, from_above):
+            total = total + ref[s * rows:(s + 1) * rows].astype(jnp.float32)
+        out[s] = total.astype(jnp.bfloat16)
+
+
+def finish(own, from_below, from_above, terms, dest, drafts, slots):
     rows = dest.shape[0]
-    width = base.shape[1]
+    width = own.shape[1]
     return pl.pallas_call(
         functools.partial(finish_kernel, slots),
         out_shape=jax.ShapeDtypeStruct((drafts, rows, width), jnp.bfloat16),
-        compiler_params=pltpu.CompilerParams(vmem_limit_bytes=VMEM),
+        compiler_params=pltpu.CompilerParams(vmem_limit_bytes=VMEM // 4),
+        cost_estimate=pl.CostEstimate(
+            flops=2 * terms.size * rows * drafts, bytes_accessed=2 * terms.size, transcendentals=0
+        ),
         name="finish",
-    )(base, terms, dest)
+    )(own, from_below, from_above, terms, dest)
 
 
 def body(
@@ -260,28 +333,36 @@
     span, rank, _ = adapter_down.shape
     slots = rows // 8
     owner_rows = -(-drafts * slots // 8) * 8
+    chips = parts // 2
+    swap = [(i, i ^ 1) for i in range(parts)]
+    shift = lambda k: [
+        (2 * x + c, 2 * ((x + k) % chips) + c) for x in range(chips) for c in range(2)
+    ]
     attn, payload, dest = attend(
         queries, draft_keys, draft_values, key_cache, value_cache, lengths, request_adapter,
         adapter_page_table, slots, owner_rows, owners, span,
     )
-    partial_base = project(attn, output_weight, parts)
-    base = lax.psum_scatter(partial_base, "tensor", scatter_dimension=0, tiled=False)
     arrived = lax.all_to_all(
         payload.reshape(owners, owner_rows, -1), "dp", 0, 0, tiled=True
     ).reshape(owners * owner_rows, -1)
+    (sent,) = project(attn, output_weight, None, parts)
+    other = lax.ppermute(sent, "tensor", swap)
+    far_up, far_down, up, down, own = project(attn, output_weight, other, parts)
+    far_up = lax.ppermute(far_up, "tensor", shift(1))
+    far_down = lax.ppermute(far_down, "tensor", shift(-1))
+    arrived, far_up, far_down = lax.optimization_barrier((arrived, far_up, far_down))
     mine = down_mix(arrived, adapter_down)
-    chips = parts // 2
-    other = lax.ppermute(mine, "tensor", [(i, i ^ 1) for i in range(parts)])
-    pair = (mine + other).astype(jnp.bfloat16)
-    mixes = [pair] + [
-        lax.ppermute(pair, "tensor", [(2 * x + c, 2 * ((x + k) % chips) + c) for x in range(chips) for c in range(2)])
-        for k in range(1, chips)
-    ]
+    pair = (mine + lax.ppermute(mine, "tensor", swap)).astype(jnp.bfloat16)
+    mixes = [pair] + [lax.ppermute(pair, "tensor", shift(k)) for k in range(1, chips)]
     terms = up_terms(mixes, arrived, adapter_up)
+    terms, far_up, far_down = lax.optimization_barrier((terms, far_up, far_down))
+    up, down = merge(up, down, far_up, far_down)
+    from_below = lax.ppermute(up, "tensor", shift(1))
+    from_above = lax.ppermute(down, "tensor", shift(-1))
     terms = lax.all_to_all(
         terms.reshape(owners, owner_rows, -1), "dp", 0, 0, tiled=True
     ).reshape(owners * owner_rows, -1)
-    return finish(base, terms, dest, drafts, slots)
+    return finish(own, from_below, from_above, terms, dest, drafts, slots)
 
 
 def solution(mesh):

time: 103 us -> 84.6 us (0.82)
  blocking collectives: 45.9 us -> 0 us
  waiting for transfers between devices: 4.69 us -> 28.2 us
  starting transfers between devices: 5.66 us -> 26.2 us
  between operations: 13.4 us -> 0.14 us
  Pallas kernels: 30.9 us -> 28.5 us
    all_to_all x2 -> x0, blocking collectives: 45.9 us -> none  [the longest x1 23.4 us: body(): lax.all_to_all(terms.reshape(owners, owner_rows, -1), 'dp', 0, 0, tiled=T...]
    all_to_all x0 -> x2, starting transfers between devices: none -> 15.2 us  [the longest x1 8.17 us: body(): lax.all_to_all(payload.reshape(owners, owner_rows, -1), 'dp', 0, 0, tiled...]
    ppermute x4 -> x9, waiting for transfers between devices: 4.67 us -> 18.6 us  [the longest x1 11.7 us: body(): from_below = lax.ppermute(up, 'tensor', shift(1))]
    all_to_all x0 -> x2, waiting for transfers between devices: none -> 9.59 us  [the longest x1 6.38 us: body(): lax.all_to_all(payload.reshape(owners, owner_rows, -1), 'dp', 0, 0, tiled...]
    ppermute x4 -> x9, starting transfers between devices: 5.65 us -> 11 us  [the longest x3 4.21 us: body(): lax.ppermute(pair, 'tensor', shift(k))]
    pallas_call x1 -> x3, Pallas kernels: 9.29 us -> 11.7 us  [the longest x2 11.5 us: project(): pl.pallas_call(sent_kernel if other is None else kept_kernel, in_specs=[v...]
    pallas_call x1, Pallas kernels: 2.63 us -> 0.72 us  [down_mix(): pl.pallas_call(down_kernel, out_shape=jax.ShapeDtypeStruct((rank, rows),...]
    pallas_call x1, Pallas kernels: 3.59 us -> 2.11 us  [up_terms(): pl.pallas_call(up_kernel, grid=(1,), in_specs=[mix_spec] * 4 + [pl.BlockS...]
  transfers between devices with their start and end apart: 5 -> 11, of which waited for: 3 -> 8; matrix products, arithmetic and copies ran while one was open for 1% -> 0% of each run, Pallas kernels for 6% -> 7%
where the time goes in v2:
time: 84.6 us; the launch traced here: 84.1 us
  Pallas kernels  28.5 us (34%)
  waiting for transfers between devices  28.2 us (33%)
  starting transfers between devices  26.2 us (31%)
  local copies, waits for them, and re-layouts  0.99 us (1%)
    pallas_call x1, Pallas kernels, attend(): pl.pallas_call(functools.partial(attend_kernel, slots, owner_rows, span),...  12.2 us
    ppermute x1, waiting for transfers between devices, body(): from_below = lax.ppermute(up, 'tensor', shift(1))  11.7 us
    pallas_call x2, Pallas kernels, project(): pl.pallas_call(sent_kernel if other is None else kept_kernel, in_specs=[v...  11.5 us
    all_to_all x1, starting transfers between devices, body(): lax.all_to_all(payload.reshape(owners, owner_rows, -1), 'dp', 0, 0, tiled...  8.17 us
    all_to_all x1, starting transfers between devices, body(): lax.all_to_all(terms.reshape(owners, owner_rows, -1), 'dp', 0, 0, tiled=T...  7.08 us
    all_to_all x1, waiting for transfers between devices, body(): lax.all_to_all(payload.reshape(owners, owner_rows, -1), 'dp', 0, 0, tiled...  6.38 us
    ppermute x3, waiting for transfers between devices, body(): lax.ppermute(pair, 'tensor', shift(k))  4.74 us
    ppermute x3, starting transfers between devices, body(): lax.ppermute(pair, 'tensor', shift(k))  4.21 us
  transfers between devices with their start and end apart: 11, of which 8 were waited for; matrix products, arithmetic and copies ran while one was open for 0% of the time, Pallas kernels for 7%

profile of v2, /device:TPU:0, one launch (start us, length us, event | category | flops | bytes accessed | tf_op | source)
XLA Modules:
  0.0 84.1 jit_solution(2610874982049636744)
XLA Ops:
  0.0 12.2 %attend.1 = (bf16[3,96,512]{2,1,0:T(8,128)(2,1)}, bf16[640,640]{1,0:T(8,128)(2,1)}, s32[96,128]{1,0:T(8,128)}) custom-call(s32[96]{0:T(128)} %lengths.1, s32[1,96]{1,0:T(1,128)} %bitcast.14, s32[1,256]{1,0:T(1,128)} %bitcast.13, bf16[3,96,512]{2,1,0:T(8,128)(2,1)} %q.1, bf16[3,96,128]{2,1,0:T(8,128)(2,1)} %dk.1, bf16[3,96,128]{2,1,0:T(8,128)(2,1)} %dv.1, ...), custom_call_target="tpu_custom_call" | custom-call | flops 301989888 | bytes 12582912 | tf_op jit(solution)/shard_map/attend/pallas_call | solution.py:97
  12.2 5.6 %project_sent.1 = bf16[4,288,1024]{2,1,0:T(8,128)(2,1)} custom-call(bf16[3,96,512]{2,1,0:T(8,128)(2,1)} %get-tuple-element.21.attn, bf16[512,8192]{1,0:T(8,128)(2,1)} %weight.3), custom_call_target="tpu_custom_call" | custom-call | flops 1 | bytes 1 | tf_op jit(solution)/shard_map/project_sent/pallas_call | solution.py:180
  17.8 0.1 collective-permute-start
  17.9 8.2 %all-to-all-start = ((bf16[16,40,640]{2,1,0:T(8,128)(2,1)}), bf16[16,40,640]{2,1,0:T(8,128)(2,1)S(1)}, u32[]{:S(2)}, u32[]{:S(2)}) async-start(bf16[16,40,640]{2,1,0:T(8,128)(2,1)} %bitcast.2), calls=%async_computation | async-start | bytes 1638400 | tf_op jit(solution)/shard_map/all_to_all | solution.py:345
  26.1 0.0 copy-start.4
  26.1 0.0 collective-permute-done.other
  26.1 5.9 %project_kept.1 = (bf16[144,1024]{1,0:T(8,128)(2,1)}, bf16[144,1024]{1,0:T(8,128)(2,1)}, bf16[288,1024]{1,0:T(8,128)(2,1)}, bf16[288,1024]{1,0:T(8,128)(2,1)}, bf16[288,1024]{1,0:T(8,128)(2,1)}) custom-call(bf16[3,96,512]{2,1,0:T(8,128)(2,1)} %get-tuple-element.21.attn, bf16[512,8192]{1,0:T(8,128)(2,1)} %weight.3, ...), custom_call_target="tpu_custom_call" | custom-call | flops 1 | bytes 1 | tf_op jit(solution)/shard_map/project_kept/pallas_call | solution.py:180
  32.0 0.0 copy-start
  32.0 1.6 %collective-permute-start.1 = (bf16[144,1024]{1,0:T(8,128)(2,1)}, bf16[144,1024]{1,0:T(8,128)(2,1)S(1)}, u32[]{:S(2)}, u32[]{:S(2)}) collective-permute-start(bf16[144,1024]{1,0:T(8,128)(2,1)} %get-tuple-element.26), channel_id=1, source_target_pairs={{0,2},{1,3},{2,4},{3,5},{4,6},{5,7},{6,0},{7,1},{8,10},{9,11},{10,... | collective-permute-start | bytes 884744 | tf_op jit(solution)/shard_map/ppermute | solution.py:351
  33.6 1.8 %collective-permute-start.2 = (bf16[144,1024]{1,0:T(8,128)(2,1)}, bf16[144,1024]{1,0:T(8,128)(2,1)S(1)}, u32[]{:S(2)}, u32[]{:S(2)}) collective-permute-start(bf16[144,1024]{1,0:T(8,128)(2,1)} %get-tuple-element.27), channel_id=1, source_target_pairs={{0,6},{1,7},{2,0},{3,1},{4,2},{5,3},{6,4},{7,5},{8,14},{9,15},{10,... | collective-permute-start | bytes 884744 | tf_op jit(solution)/shard_map/ppermute | solution.py:352
  35.3 6.4 %all-to-all-done = bf16[16,40,640]{2,1,0:T(8,128)(2,1)S(1)} async-done(((bf16[16,40,640]{2,1,0:T(8,128)(2,1)}), bf16[16,40,640]{2,1,0:T(8,128)(2,1)S(1)}, u32[]{:S(2)}, u32[]{:S(2)}) %all-to-all-start) | async-done | bytes 819232 | tf_op jit(solution)/shard_map/all_to_all | solution.py:345
  41.7 0.9 %collective-permute-done.1.far_up = bf16[144,1024]{1,0:T(8,128)(2,1)S(1)} collective-permute-done((bf16[144,1024]{1,0:T(8,128)(2,1)}, bf16[144,1024]{1,0:T(8,128)(2,1)S(1)}, u32[]{:S(2)}, u32[]{:S(2)}) %collective-permute-start.1) | collective-permute-done | bytes 294944 | tf_op jit(solution)/shard_map/ppermute | solution.py:351
  42.6 0.0 collective-permute-done.2.far_down
  42.6 0.0 copy-start.5
  42.6 0.0 copy-done.4
  42.6 0.7 down_mix.1
  43.4 0.1 collective-permute-start.3
  43.5 1.3 %collective-permute-done.3 = f32[32,640]{1,0:T(8,128)S(1)} collective-permute-done((f32[32,640]{1,0:T(8,128)S(1)}, f32[32,640]{1,0:T(8,128)S(1)}, u32[]{:S(2)}, u32[]{:S(2)}) %collective-permute-start.3) | collective-permute-done | bytes 81952 | tf_op jit(solution)/shard_map/ppermute | solution.py:355
  44.7 3.0 %collective-permute-start.6 = (bf16[32,640]{1,0:T(8,128)(2,1)S(1)}, bf16[32,640]{1,0:T(8,128)(2,1)S(1)}, u32[]{:S(2)}, u32[]{:S(2)}) collective-permute-start(bf16[32,640]{1,0:T(8,128)(2,1)S(1)} %add_convert_fusion.mine), channel_id=1, source_target_pairs={{0,6},{1,7},{2,0},{3,1},{4,2},{5,3},{6,4},{7,5},{8,14},{9,15},{10,... | collective-permute-start | bytes 122888 | tf_op jit(solution)/shard_map/ppermute | solution.py:356
  47.8 0.6 collective-permute-start.5
  48.3 0.6 collective-permute-start.4
  49.0 0.5 collective-permute-done.6.three
  49.4 3.8 %collective-permute-done.5.two = bf16[32,640]{1,0:T(8,128)(2,1)S(1)} collective-permute-done((bf16[32,640]{1,0:T(8,128)(2,1)S(1)}, bf16[32,640]{1,0:T(8,128)(2,1)S(1)}, u32[]{:S(2)}, u32[]{:S(2)}) %collective-permute-start.5) | collective-permute-done | bytes 40992 | tf_op jit(solution)/shard_map/ppermute | solution.py:356
  53.3 0.4 collective-permute-done.4.one
  53.7 0.0 copy-done.5
  53.7 0.0 copy-done
  53.7 0.0 copy-start.2
  53.7 0.0 copy-start.3
  53.7 2.1 %up_terms.1 = bf16[640,1024]{1,0:T(8,128)(2,1)} custom-call(bf16[32,640]{1,0:T(8,128)(2,1)S(1)} %add_convert_fusion.mine, bf16[32,640]{1,0:T(8,128)(2,1)S(1)} %collective-permute-done.4.one, bf16[32,640]{1,0:T(8,128)(2,1)S(1)} %collective-permute-done.5.two, bf16[32,640]{1,0:T(8,128)(2,1)S(1)} %collective-permute-done.6.three, bf16[640,640]{1,0:T(8,128)(2,1)S(1)} %bitcast.9, ...), custom_call_target="tpu_custom_call" | custom-call | flops 671088640 | bytes 2359296 | tf_op jit(solution)/shard_map/up_terms/pallas_call | solution.py:274
  55.8 0.0 copy-start.1
  55.8 0.0 copy-start.7
  55.8 7.1 %all-to-all-start.1 = ((bf16[16,40,1024]{2,1,0:T(8,128)(2,1)}), bf16[16,40,1024]{2,1,0:T(8,128)(2,1)S(1)}, u32[]{:S(2)}, u32[]{:S(2)}) async-start(bf16[16,40,1024]{2,1,0:T(8,128)(2,1)} %bitcast.6), calls=%async_computation.1 | async-start | bytes 2621440 | tf_op jit(solution)/shard_map/all_to_all | solution.py:362
  62.9 0.0 copy-done.2
  62.9 0.0 copy-done.3
  62.9 0.0 copy-start.6
  62.9 1.0 %copy-done.6 = bf16[144,1024]{1,0:T(8,128)(2,1)S(1)} copy-done((bf16[144,1024]{1,0:T(8,128)(2,1)S(1)}, bf16[144,1024]{1,0:T(8,128)(2,1)}, u32[]{:S(2)}) %copy-start.6) | copy-done | bytes 294936
  63.9 0.2 merge.1
  64.1 0.1 collective-permute-start.7
  64.1 3.2 %collective-permute-start.8 = (bf16[288,1024]{1,0:T(8,128)(2,1)S(1)}, bf16[288,1024]{1,0:T(8,128)(2,1)S(1)}, u32[]{:S(2)}, u32[]{:S(2)}) collective-permute-start(bf16[288,1024]{1,0:T(8,128)(2,1)S(1)} %get-tuple-element.34), channel_id=1, source_target_pairs={{0,6},{1,7},{2,0},{3,1},{4,2},{5,3},{6,4},{7,5},{8,14},{9,15},{10,... | collective-permute-start | bytes 1769480 | tf_op jit(solution)/shard_map/ppermute | solution.py:361
  67.4 11.7 %collective-permute-done.7.from_below = bf16[288,1024]{1,0:T(8,128)(2,1)S(1)} collective-permute-done((bf16[288,1024]{1,0:T(8,128)(2,1)S(1)}, bf16[288,1024]{1,0:T(8,128)(2,1)S(1)}, u32[]{:S(2)}, u32[]{:S(2)}) %collective-permute-start.7) | collective-permute-done | bytes 589856 | tf_op jit(solution)/shard_map/ppermute | solution.py:360
  79.0 0.0 collective-permute-done.8.from_above
  79.0 3.2 %all-to-all-done.1 = bf16[16,40,1024]{2,1,0:T(8,128)(2,1)S(1)} async-done(((bf16[16,40,1024]{2,1,0:T(8,128)(2,1)}), bf16[16,40,1024]{2,1,0:T(8,128)(2,1)S(1)}, u32[]{:S(2)}, u32[]{:S(2)}) %all-to-all-start.1) | async-done | bytes 1310752 | tf_op jit(solution)/shard_map/all_to_all | solution.py:362
  82.2 0.0 copy-done.1
  82.2 0.0 copy-done.7
  82.2 1.8 %finish.1 = bf16[3,96,1024]{2,1,0:T(8,128)(2,1)} custom-call(bf16[288,1024]{1,0:T(8,128)(2,1)S(1)} %copy-done.1, bf16[288,1024]{1,0:T(8,128)(2,1)S(1)} %collective-permute-done.7.from_below, bf16[288,1024]{1,0:T(8,128)(2,1)S(1)} %collective-permute-done.8.from_above, bf16[640,1024]{1,0:T(8,128)(2,1)S(1)} %bitcast.10, s32[96,128]{1,0:T(8,128)S(1)} %copy-done.7), custom_call_target="tpu_custom_call" | custom-call | flops 377487360 | bytes 1310720 | tf_op jit(solution)/shard_map/finish/pallas_call | solution.py:306
  (1 shorter events, 0.0 us)
Async XLA Ops:
  17.8 8.3 %collective-permute-start = (bf16[4,288,1024]{2,1,0:T(8,128)(2,1)}, bf16[4,288,1024]{2,1,0:T(8,128)(2,1)}, u32[]{:S(2)}, u32[]{:S(2)}) collective-permute-start(bf16[4,288,1024]{2,1,0:T(8,128)(2,1)} %project_sent.1), channel_id=1, source_target_pairs={{0,1},{1,0},{2,3},{3,2},{4,5},{5,4},{6,7},{7,6},{8,9},{9,8},{10,11... | collective-permute-start | bytes 7077896 | tf_op jit(solution)/shard_map/ppermute | solution.py:349
  17.9 23.8 %all-to-all-start = ((bf16[16,40,640]{2,1,0:T(8,128)(2,1)}), bf16[16,40,640]{2,1,0:T(8,128)(2,1)S(1)}, u32[]{:S(2)}, u32[]{:S(2)}) async-start(bf16[16,40,640]{2,1,0:T(8,128)(2,1)} %bitcast.2), calls=%async_computation | async-start | bytes 1638400 | tf_op jit(solution)/shard_map/all_to_all | solution.py:345
  26.1 16.6 %copy-start.4 = (bf16[16,32,512]{2,1,0:T(8,128)(2,1)S(1)}, bf16[16,32,512]{2,1,0:T(8,128)(2,1)}, u32[]{:S(2)}) copy-start(bf16[16,32,512]{2,1,0:T(8,128)(2,1)} %param.20) | copy-start | bytes 1572868
  32.0 21.7 %copy-start = (bf16[16,32,1024]{2,1,0:T(8,128)(2,1)S(1)}, bf16[16,32,1024]{2,1,0:T(8,128)(2,1)}, u32[]{:S(2)}) copy-start(bf16[16,32,1024]{2,1,0:T(8,128)(2,1)} %param.21) | copy-start | bytes 3145732
  32.0 10.6 %collective-permute-start.1 = (bf16[144,1024]{1,0:T(8,128)(2,1)}, bf16[144,1024]{1,0:T(8,128)(2,1)S(1)}, u32[]{:S(2)}, u32[]{:S(2)}) collective-permute-start(bf16[144,1024]{1,0:T(8,128)(2,1)} %get-tuple-element.26), channel_id=1, source_target_pairs={{0,2},{1,3},{2,4},{3,5},{4,6},{5,7},{6,0},{7,1},{8,10},{9,11},{10,... | collective-permute-start | bytes 884744 | tf_op jit(solution)/shard_map/ppermute | solution.py:351
  33.6 9.1 %collective-permute-start.2 = (bf16[144,1024]{1,0:T(8,128)(2,1)}, bf16[144,1024]{1,0:T(8,128)(2,1)S(1)}, u32[]{:S(2)}, u32[]{:S(2)}) collective-permute-start(bf16[144,1024]{1,0:T(8,128)(2,1)} %get-tuple-element.27), channel_id=1, source_target_pairs={{0,6},{1,7},{2,0},{3,1},{4,2},{5,3},{6,4},{7,5},{8,14},{9,15},{10,... | collective-permute-start | bytes 884744 | tf_op jit(solution)/shard_map/ppermute | solution.py:352
  42.6 11.1 %copy-start.5 = (bf16[144,1024]{1,0:T(8,128)(2,1)}, bf16[144,1024]{1,0:T(8,128)(2,1)S(1)}, u32[]{:S(2)}) copy-start(bf16[144,1024]{1,0:T(8,128)(2,1)S(1)} %collective-permute-done.2.far_down) | copy-start | bytes 884740
  43.4 1.4 %collective-permute-start.3 = (f32[32,640]{1,0:T(8,128)S(1)}, f32[32,640]{1,0:T(8,128)S(1)}, u32[]{:S(2)}, u32[]{:S(2)}) collective-permute-start(f32[32,640]{1,0:T(8,128)S(1)} %down_mix.1), channel_id=1, source_target_pairs={{0,1},{1,0},{2,3},{3,2},{4,5},{5,4},{6,7},{7,6},{8,9},{9,8},{10,11... | collective-permute-start | bytes 245768 | tf_op jit(solution)/shard_map/ppermute | solution.py:355
  44.7 4.7 %collective-permute-start.6 = (bf16[32,640]{1,0:T(8,128)(2,1)S(1)}, bf16[32,640]{1,0:T(8,128)(2,1)S(1)}, u32[]{:S(2)}, u32[]{:S(2)}) collective-permute-start(bf16[32,640]{1,0:T(8,128)(2,1)S(1)} %add_convert_fusion.mine), channel_id=1, source_target_pairs={{0,6},{1,7},{2,0},{3,1},{4,2},{5,3},{6,4},{7,5},{8,14},{9,15},{10,... | collective-permute-start | bytes 122888 | tf_op jit(solution)/shard_map/ppermute | solution.py:356
  47.8 5.5 %collective-permute-start.5 = (bf16[32,640]{1,0:T(8,128)(2,1)S(1)}, bf16[32,640]{1,0:T(8,128)(2,1)S(1)}, u32[]{:S(2)}, u32[]{:S(2)}) collective-permute-start(bf16[32,640]{1,0:T(8,128)(2,1)S(1)} %add_convert_fusion.mine), channel_id=1, source_target_pairs={{0,4},{1,5},{2,6},{3,7},{4,0},{5,1},{6,2},{7,3},{8,12},{9,13},{10,... | collective-permute-start | bytes 122888 | tf_op jit(solution)/shard_map/ppermute | solution.py:356
  48.3 5.3 %collective-permute-start.4 = (bf16[32,640]{1,0:T(8,128)(2,1)S(1)}, bf16[32,640]{1,0:T(8,128)(2,1)S(1)}, u32[]{:S(2)}, u32[]{:S(2)}) collective-permute-start(bf16[32,640]{1,0:T(8,128)(2,1)S(1)} %add_convert_fusion.mine), channel_id=1, source_target_pairs={{0,2},{1,3},{2,4},{3,5},{4,6},{5,7},{6,0},{7,1},{8,10},{9,11},{10,... | collective-permute-start | bytes 122888 | tf_op jit(solution)/shard_map/ppermute | solution.py:356
  53.7 9.2 %copy-start.2 = (bf16[288,1024]{1,0:T(8,128)(2,1)S(1)}, bf16[288,1024]{1,0:T(8,128)(2,1)}, u32[]{:S(2)}) copy-start(bf16[288,1024]{1,0:T(8,128)(2,1)} %get-tuple-element.23.up) | copy-start | bytes 1769476
  53.7 9.2 %copy-start.3 = (bf16[288,1024]{1,0:T(8,128)(2,1)S(1)}, bf16[288,1024]{1,0:T(8,128)(2,1)}, u32[]{:S(2)}) copy-start(bf16[288,1024]{1,0:T(8,128)(2,1)} %get-tuple-element.24.down) | copy-start | bytes 1769476
  55.8 26.4 %copy-start.1 = (bf16[288,1024]{1,0:T(8,128)(2,1)S(1)}, bf16[288,1024]{1,0:T(8,128)(2,1)}, u32[]{:S(2)}) copy-start(bf16[288,1024]{1,0:T(8,128)(2,1)} %get-tuple-element.22.own) | copy-start | bytes 1769476
  55.8 26.4 %copy-start.7 = (s32[96,128]{1,0:T(8,128)S(1)}, s32[96,128]{1,0:T(8,128)}, u32[]{:S(2)}) copy-start(s32[96,128]{1,0:T(8,128)} %get-tuple-element.36.dest) | copy-start | bytes 147460
  55.8 26.4 %all-to-all-start.1 = ((bf16[16,40,1024]{2,1,0:T(8,128)(2,1)}), bf16[16,40,1024]{2,1,0:T(8,128)(2,1)S(1)}, u32[]{:S(2)}, u32[]{:S(2)}) async-start(bf16[16,40,1024]{2,1,0:T(8,128)(2,1)} %bitcast.6), calls=%async_computation.1 | async-start | bytes 2621440 | tf_op jit(solution)/shard_map/all_to_all | solution.py:362
  62.9 1.0 %copy-start.6 = (bf16[144,1024]{1,0:T(8,128)(2,1)S(1)}, bf16[144,1024]{1,0:T(8,128)(2,1)}, u32[]{:S(2)}) copy-start(bf16[144,1024]{1,0:T(8,128)(2,1)} %copy-done.5) | copy-start | bytes 884740
  64.1 15.0 %collective-permute-start.7 = (bf16[288,1024]{1,0:T(8,128)(2,1)S(1)}, bf16[288,1024]{1,0:T(8,128)(2,1)S(1)}, u32[]{:S(2)}, u32[]{:S(2)}) collective-permute-start(bf16[288,1024]{1,0:T(8,128)(2,1)S(1)} %get-tuple-element.33), channel_id=1, source_target_pairs={{0,2},{1,3},{2,4},{3,5},{4,6},{5,7},{6,0},{7,1},{8,10},{9,11},{10,... | collective-permute-start | bytes 1769480 | tf_op jit(solution)/shard_map/ppermute | solution.py:360
  64.1 14.9 %collective-permute-start.8 = (bf16[288,1024]{1,0:T(8,128)(2,1)S(1)}, bf16[288,1024]{1,0:T(8,128)(2,1)S(1)}, u32[]{:S(2)}, u32[]{:S(2)}) collective-permute-start(bf16[288,1024]{1,0:T(8,128)(2,1)S(1)} %get-tuple-element.34), channel_id=1, source_target_pairs={{0,6},{1,7},{2,0},{3,1},{4,2},{5,3},{6,4},{7,5},{8,14},{9,15},{10,... | collective-permute-start | bytes 1769480 | tf_op jit(solution)/shard_map/ppermute | solution.py:361

commit v3 on v1

v3 whole, which is shorter than its diff:
```python
import functools, math
import jax, jax.numpy as jnp
from jax import lax
from jax.experimental import pallas as pl
from jax.experimental.pallas import tpu as pltpu
from jax.sharding import PartitionSpec as P

LANES = 128
STEP = 16
HALF = 8
AHEAD_COPIES = 3
PIECES = 8
IN_FLIGHT = 4
AHEAD = (2, 1, 3, 0)
VMEM = 63 * 1024 * 1024

def attend_kernel(
    slots, owner_rows, span, lengths, adapters_hbm, table_hbm, q_hbm, dk_hbm, dv_hbm, k_hbm, v_hbm,
    attn, payload, dest_out, adapters, table, q, dk, dv, k, v, scores, weights, small_sems, sems,
):
    drafts, count, width = q.shape
    cache = k.shape[1]
    heads = width // LANES
    rows = drafts * heads * HALF
    scale = math.log2(math.e) / math.sqrt(LANES)
    small = [
        pltpu.make_async_copy(a, b, small_sems.at[n])
        for n, (a, b) in enumerate(
            ((q_hbm, q), (dk_hbm, dk), (dv_hbm, dv), (adapters_hbm, adapters), (table_hbm, table))
        )
    ]

    steps = count // STEP
    flow = [(0, 0), (0, 1), (0, 2)] + [p for j in range(steps - 3) for p in ((1, j), (0, j + 3))] + [(1, j) for j in range(steps - 3, steps)]

    def fetch(at):
        n, j = flow[at]
        here = pl.ds(j * STEP, STEP)
        return pltpu.make_async_copy((k_hbm, v_hbm)[n].at[here], (k, v)[n].at[here], sems.at[n, j])

    def arrive(at):
        fetch(at).wait()
        if at + AHEAD_COPIES < len(flow):
            fetch(at + AHEAD_COPIES).start()

    for copy in small:
        copy.start()
    for at in range(AHEAD_COPIES):
        fetch(at).start()

    sub = lax.broadcasted_iota(jnp.int32, (rows, cache), 0) % HALF
    lane8 = lax.broadcasted_iota(jnp.int32, (HALF, cache), 1)
    sub8 = lax.broadcasted_iota(jnp.int32, (HALF, cache), 0)
    drow = lax.broadcasted_iota(jnp.int32, (rows, drafts * HALF), 0)
    dlane = lax.broadcasted_iota(jnp.int32, (rows, drafts * HALF), 1)
    fresh_ok = (drow % HALF == dlane % HALF) & (dlane // HALF <= drow // (heads * HALF))
    for copy in small[:3]:
        copy.wait()

    def places():
        for copy in small[3:]:
            copy.wait()
        pages = table.shape[1]
        a = lax.broadcasted_iota(jnp.int32, (count, count), 0)
        b = lax.broadcasted_iota(jnp.int32, (count, count), 1)
        eye = a == b
        to_col = lambda row: jnp.sum(jnp.where(eye, jnp.broadcast_to(row, (count, count)), 0.0), axis=1, keepdims=True)
        to_row = lambda col: jnp.sum(jnp.where(eye, jnp.broadcast_to(col, (count, count)), 0.0), axis=0, keepdims=True)
        acol = to_col(adapters[...].astype(jnp.float32)).astype(jnp.int32)
        hit = acol == lax.broadcasted_iota(jnp.int32, (count, pages), 1)
        page = jnp.sum(jnp.where(hit, jnp.broadcast_to(table[...].astype(jnp.float32), (count, pages)), 0.0), axis=1, keepdims=True)
        prow = to_row(page).astype(jnp.int32)
        pcol = page.astype(jnp.int32)
        orow, ocol = prow // span, pcol // span
        rank = jnp.sum(jnp.where((ocol == orow) & (a < b), 1.0, 0.0), axis=0, keepdims=True).astype(jnp.int32)
        rank_col = jnp.sum(jnp.where((ocol == orow) & (b < a), 1.0, 0.0), axis=1, keepdims=True).astype(jnp.int32)
        dest_out[...] = jnp.broadcast_to(ocol * owner_rows + rank_col, dest_out.shape)
        dest = orow * owner_rows + rank
        local = jnp.broadcast_to((pcol - ocol * span).astype(jnp.float32), (count, LANES)).astype(jnp.bfloat16)
        return dest, local

    def score(j, carry):
        base = j * STEP
        here = pl.ds(base, STEP)
        qf = q[:, here].astype(jnp.float32)
        dkf = dk[:, here].astype(jnp.float32)
        arrive(flow.index((0, j)))
        for h in range(STEP // HALF):
            at = slice(h * HALF, (h + 1) * HALF)
            qb = jnp.concatenate([qf[s, at, g * LANES:(g + 1) * LANES] for s in range(drafts) for g in range(heads)], axis=0).astype(jnp.bfloat16)
            kb = jnp.concatenate([dkf[t, at] for t in range(drafts)], axis=0).astype(jnp.bfloat16)
            part = None
            limit = jnp.zeros((HALF, cache), jnp.int32)
            for r in range(HALF):
                one = lax.dot_general(qb, k[base + h * HALF + r], (((1,), (1,)), ((), ())), preferred_element_type=jnp.float32)
                part = one if r == 0 else jnp.where(sub == r, one, part)
                limit = jnp.where(sub8 == r, lengths[base + h * HALF + r], limit)
            seen = jnp.concatenate([(lane8 < limit).astype(jnp.int32)] * (drafts * heads), axis=0) > 0
            fresh = lax.dot_general(qb, kb, (((1,), (1,)), ((), ())), preferred_element_type=jnp.float32)
            scores[j, h, :, :cache] = jnp.where(seen, part, -1e30)
            scores[j, h, :, cache:cache + drafts * HALF] = jnp.where(fresh_ok, fresh, -1e30)
        return carry

    def soften(j, carry):
        for h in range(STEP // HALF):
            part = scores[j, h, :, :cache]
            fresh = scores[j, h, :, cache:cache + drafts * HALF]
            top = jnp.maximum(jnp.max(part, axis=1, keepdims=True), jnp.max(fresh, axis=1, keepdims=True))
            e = jnp.exp2((part - top) * scale)
            ef = jnp.exp2((fresh - top) * scale)
            inv = 1.0 / (jnp.sum(e, axis=1, keepdims=True) + jnp.sum(ef, axis=1, keepdims=True))
            weights[j, h, :, :cache] = (e * inv).astype(jnp.bfloat16)
            weights[j, h, :, cache:cache + drafts * HALF] = (ef * inv).astype(jnp.bfloat16)
        return carry

    keep = [jnp.where(sub == r, 1.0, 0.0).astype(jnp.bfloat16) for r in range(HALF)]

    def mix(j, carry):
        base = j * STEP
        here = pl.ds(base, STEP)
        dvf = dv[:, here].astype(jnp.float32)
        arrive(flow.index((1, j)))
        outs = []
        for h in range(STEP // HALF):
            at = slice(h * HALF, (h + 1) * HALF)
            vb = jnp.concatenate([dvf[t, at] for t in range(drafts)], axis=0).astype(jnp.bfloat16)
            w = weights[j, h, :, :cache]
            wf = weights[j, h, :, cache:cache + drafts * HALF]
            wide = jnp.concatenate([w * keep[r] for r in range(HALF)], axis=1)
            vals = v[pl.ds(base + h * HALF, HALF)].reshape(HALF * cache, LANES)
            mixed = jnp.dot(wide, vals, preferred_element_type=jnp.float32)
            mixed = mixed + jnp.dot(wf, vb, preferred_element_type=jnp.float32)
            outs.append(mixed)
        for s in range(drafts):
            for g in range(heads):
                at = (s * heads + g) * HALF
                piece = jnp.concatenate([o[at:at + HALF] for o in outs], axis=0).astype(jnp.bfloat16)
                attn[s, here, g * LANES:(g + 1) * LANES] = piece
        return carry

    for j in range(steps + 2):
        if j < steps:
            score(j, 0)
        if j == 1:
            dest, local = places()
        if 1 <= j <= steps:
            soften(j - 1, 0)
        if j >= 2:
            mix(j - 2, 0)

    place = lax.broadcasted_iota(jnp.int32, (payload.shape[0], count), 0)
    acc = None
    for s in range(drafts):
        pick = jnp.where(place == dest + s * slots, 1.0, 0.0).astype(jnp.bfloat16)
        part = jnp.dot(pick, jnp.concatenate([attn[s], local], axis=1), preferred_element_type=jnp.float32)
        acc = part if acc is None else acc + part
    payload[...] = acc.astype(jnp.bfloat16)


def attend(queries, draft_keys, draft_values, key_cache, value_cache, lengths, request_adapter, table, slots, owner_rows, owners, span):
    drafts, rows, width = queries.shape
    cache = key_cache.shape[1]
    vmem = pl.BlockSpec(memory_space=pltpu.VMEM)
    hbm = pl.BlockSpec(memory_space=pltpu.HBM)
    return pl.pallas_call(
        functools.partial(attend_kernel, slots, owner_rows, span),
        in_specs=[pl.BlockSpec(memory_space=pltpu.SMEM)] + [hbm] * 7,
        out_specs=[vmem] * 3,
        out_shape=[
            jax.ShapeDtypeStruct((drafts, rows, width), jnp.bfloat16),
            jax.ShapeDtypeStruct((owners * owner_rows, width + LANES), jnp.bfloat16),
            jax.ShapeDtypeStruct((rows, LANES), jnp.int32),
        ],
        scratch_shapes=[
            pltpu.VMEM((1, rows), jnp.int32),
            pltpu.VMEM((1, table.shape[0]), jnp.int32),
            pltpu.VMEM(queries.shape, jnp.bfloat16),
            pltpu.VMEM(draft_keys.shape, jnp.bfloat16),
            pltpu.VMEM(draft_values.shape, jnp.bfloat16),
            pltpu.VMEM(key_cache.shape, jnp.bfloat16),
            pltpu.VMEM(value_cache.shape, jnp.bfloat16),
            pltpu.VMEM((rows // STEP, STEP // HALF, drafts * width // LANES * HALF, cache + LANES), jnp.float32),
            pltpu.VMEM((rows // STEP, STEP // HALF, drafts * width // LANES * HALF, cache + LANES), jnp.bfloat16),
            pltpu.SemaphoreType.DMA((5,)),
            pltpu.SemaphoreType.DMA((2, rows // STEP)),
        ],
        compiler_params=pltpu.CompilerParams(vmem_limit_bytes=VMEM),
        cost_estimate=pl.CostEstimate(
            flops=8 * queries.size * cache, bytes_accessed=4 * key_cache.size, transcendentals=0
        ),
        name="attend",
    )(lengths, request_adapter.reshape(1, rows), table.reshape(1, -1), queries, draft_keys, draft_values, key_cache, value_cache)


def project_kernel(first, attn, attn_other, weight, weight_other, *refs):
    outs, (flat, held, done, sems, in_sems, out_sems) = refs[:-6], refs[-6:]
    _, half, width = flat.shape
    half = half // 2
    place = lax.axis_index("tensor")
    chips = lax.axis_size("tensor") // 2
    blocks, sources, _, part = held.shape
    flow = [(j, n) for j in range(blocks) for n in range(sources)]
    piece = width // PIECES

    def fetch(at, s=None):
        j, n = flow[at]
        block = (place // 2 + AHEAD[first + j]) % chips * 2 + place % 2
        here = pl.ds(pl.multiple_of(block * part, part), part)
        w, to = (weight, weight_other)[n], held.at[j, n]
        if s is None:
            return pltpu.make_async_copy(w.at[:, here], to, sems.at[j, n])
        down = pl.ds(s * piece, piece)
        return pltpu.make_async_copy(w.at[down, here], to.at[down], sems.at[j, n])

    def begin(at):
        for s in range(PIECES):
            fetch(at, s).start()

    ins = [pltpu.make_async_copy(a, flat.at[n], in_sems.at[n]) for n, a in enumerate((attn, attn_other))]
    for copy in ins:
        copy.start()
    for at in range(min(IN_FLIGHT, len(flow))):
        begin(at)
    for copy in ins:
        copy.wait()
    stores = []
    for j in range(blocks):
        total = None
        for n in range(sources):
            at = j * sources + n
            fetch(at).wait()
            if at + IN_FLIGHT < len(flow):
                begin(at + IN_FLIGHT)
            part_sum = jnp.dot(flat[n], held[j, n], preferred_element_type=jnp.float32)
            total = part_sum if total is None else total + part_sum
        done[j] = total.astype(jnp.bfloat16)
        for n in range(2):
            at = 2 * j + n
            stores.append(pltpu.make_async_copy(done.at[j, pl.ds(n * half, half)], outs[at], out_sems.at[at]))
            stores[-1].start()
    for store in stores:
        store.wait()


def project(attn, attn_other, weight, weight_other, parts, first, blocks):
    rows, width = attn.shape
    part = weight.shape[1] // parts
    hbm = pl.BlockSpec(memory_space=pltpu.HBM)
    half = jax.ShapeDtypeStruct((rows // 2, part), jnp.bfloat16)
    return pl.pallas_call(
        functools.partial(project_kernel, first),
        in_specs=[hbm] * 4,
        out_specs=[hbm] * (2 * blocks),
        out_shape=[half] * (2 * blocks),
        scratch_shapes=[
            pltpu.VMEM((2, rows, width), jnp.bfloat16),
            pltpu.VMEM((blocks, 2, width, part), jnp.bfloat16),
            pltpu.VMEM((blocks, rows, part), jnp.bfloat16),
            pltpu.SemaphoreType.DMA((blocks, 2)),
            pltpu.SemaphoreType.DMA((2,)),
            pltpu.SemaphoreType.DMA((2 * blocks,)),
        ],
        compiler_params=pltpu.CompilerParams(vmem_limit_bytes=VMEM),
        cost_estimate=pl.CostEstimate(
            flops=4 * rows * width * part * blocks,
            bytes_accessed=4 * width * part * blocks,
            transcendentals=0,
        ),
        name="project",
    )(attn, attn_other, weight, weight_other)


def merge_kernel(up, down, far_up, far_down, up_out, down_out):
    for a, b, out in ((up, far_up, up_out), (down, far_down, down_out)):
        out[...] = (a[...].astype(jnp.float32) + b[...].astype(jnp.float32)).astype(jnp.bfloat16)


def merge(up, down, far_up, far_down):
    shape = jax.ShapeDtypeStruct(up.shape, up.dtype)
    return pl.pallas_call(
        merge_kernel,
        out_shape=[shape, shape],
        compiler_params=pltpu.CompilerParams(vmem_limit_bytes=VMEM // 4),
        cost_estimate=pl.CostEstimate(flops=0, bytes_accessed=12 * up.size, transcendentals=0),
        name="merge",
    )(up, down, far_up, far_down)


def down_kernel(arrived, down, mix):
    width = down.shape[1]
    span = down.shape[0] // mix.shape[0]
    product = lax.dot_general(
        down[...], arrived[:, :width], (((1,), (1,)), ((), ())), preferred_element_type=jnp.float32
    )
    ones = jnp.ones((8, LANES), jnp.bfloat16)
    page = lax.dot_general(
        ones, arrived[:, width:], (((1,), (1,)), ((), ())), preferred_element_type=jnp.float32
    )[:1] * (1.0 / LANES)
    rank = mix.shape[0]
    total = jnp.zeros(mix.shape, jnp.float32)
    for p in range(span):
        total = total + jnp.where(page == float(p), product[p * rank:(p + 1) * rank], 0.0)
    mix[...] = total


def down_mix(arrived, down):
    rows = arrived.shape[0]
    span, rank, width = down.shape
    return pl.pallas_call(
        down_kernel,
        out_shape=jax.ShapeDtypeStruct((rank, rows), jnp.float32),
        compiler_params=pltpu.CompilerParams(vmem_limit_bytes=VMEM // 4),
        cost_estimate=pl.CostEstimate(flops=2 * rows * down.size, bytes_accessed=2 * (arrived.size + down.size), transcendentals=0),
        name="down_mix",
    )(arrived, down.reshape(span * rank, width))


def up_kernel(mine, one, two, three, arrived, up, out):
    rank = mine.shape[0]
    spread_width = up.shape[0]
    mix = (
        mine[...].astype(jnp.float32)
        + one[...].astype(jnp.float32)
        + two[...].astype(jnp.float32)
        + three[...].astype(jnp.float32)
    ).astype(jnp.bfloat16)
    a = lax.broadcasted_iota(jnp.int32, (rank, spread_width), 0)
    b = lax.broadcasted_iota(jnp.int32, (rank, spread_width), 1)
    repeat = jnp.where(b % rank == a, 1.0, 0.0).astype(jnp.bfloat16)
    spread = lax.dot_general(
        mix, repeat, (((0,), (0,)), ((), ())), preferred_element_type=jnp.float32
    )
    meta = arrived[...].astype(jnp.float32)
    pieces = []
    for j in range(spread_width // LANES):
        lane = lax.broadcasted_iota(jnp.int32, meta.shape, 1) + j * LANES
        same = meta == (lane // rank).astype(jnp.float32)
        pieces.append(jnp.where(same, spread[:, j * LANES:(j + 1) * LANES], 0.0).astype(jnp.bfloat16))
    out[...] = jnp.dot(
        jnp.concatenate(pieces, axis=1), up[...], preferred_element_type=jnp.float32
    ).astype(jnp.bfloat16)


def up_terms(mixes, arrived, up):
    rows, full = arrived.shape
    span, rank, width = up.shape
    mix_spec = pl.BlockSpec((rank, rows), lambda i: (0, 0))
    return pl.pallas_call(
        up_kernel,
        grid=(1,),
        in_specs=[mix_spec] * 4
        + [
            pl.BlockSpec((rows, LANES), lambda i: (0, full // LANES - 1)),
            pl.BlockSpec((span * rank, width), lambda i: (0, 0)),
        ],
        out_specs=pl.BlockSpec((rows, width), lambda i: (0, 0)),
        out_shape=jax.ShapeDtypeStruct((rows, width), jnp.bfloat16),
        compiler_params=pltpu.CompilerParams(vmem_limit_bytes=VMEM // 4),
        cost_estimate=pl.CostEstimate(flops=2 * rows * up.size, bytes_accessed=2 * (up.size + rows * width), transcendentals=0),
        name="up_terms",
    )(*mixes, arrived, up.reshape(span * rank, width))


def finish_kernel(slots, *refs):
    halves, (terms, dest, out) = refs[:6], refs[6:]
    drafts, rows, width = out.shape
    places = terms.shape[0]
    lane = lax.broadcasted_iota(jnp.int32, (rows, places), 1)
    where_to = dest[:, :1]
    total = []
    for n in range(2):
        a, b, c = halves[n::2]
        total.append(a[...].astype(jnp.float32) + b[...].astype(jnp.float32) + c[...].astype(jnp.float32))
    total = jnp.concatenate(total, axis=0)
    for s in range(drafts):
        pick = jnp.where(lane == where_to + s * slots, 1.0, 0.0).astype(jnp.bfloat16)
        term = jnp.dot(pick, terms[...], preferred_element_type=jnp.float32)
        out[s] = (total[s * rows:(s + 1) * rows] + term).astype(jnp.bfloat16)


def finish(halves, terms, dest, drafts, slots):
    rows = dest.shape[0]
    width = terms.shape[1]
    return pl.pallas_call(
        functools.partial(finish_kernel, slots),
        out_shape=jax.ShapeDtypeStruct((drafts, rows, width), jnp.bfloat16),
        compiler_params=pltpu.CompilerParams(vmem_limit_bytes=VMEM // 4),
        cost_estimate=pl.CostEstimate(
            flops=2 * terms.size * rows * drafts, bytes_accessed=2 * terms.size, transcendentals=0
        ),
        name="finish",
    )(*halves, terms, dest)


def body(
    queries,
    draft_keys,
    draft_values,
    key_cache,
    value_cache,
    lengths,
    request_adapter,
    adapter_page_table,
    output_weight,
    adapter_down,
    adapter_up,
):
    drafts, rows, width = queries.shape
    owners = lax.axis_size("dp")
    parts = lax.axis_size("tensor")
    span, rank, _ = adapter_down.shape
    slots = rows // 8
    owner_rows = -(-drafts * slots // 8) * 8
    chips = parts // 2
    swap = [(i, i ^ 1) for i in range(parts)]
    shift = lambda k: [
        (2 * x + c, 2 * ((x + k) % chips) + c) for x in range(chips) for c in range(2)
    ]
    weight_other = lax.ppermute(output_weight, "tensor", swap)
    attn, payload, dest = attend(
        queries, draft_keys, draft_values, key_cache, value_cache, lengths, request_adapter,
        adapter_page_table, slots, owner_rows, owners, span,
    )
    arrived = lax.all_to_all(
        payload.reshape(owners, owner_rows, -1), "dp", 0, 0, tiled=True
    ).reshape(owners * owner_rows, -1)
    attn = attn.reshape(drafts * rows, width)
    attn_other = lax.ppermute(attn, "tensor", swap)
    blocks = project(attn, attn_other, output_weight, weight_other, parts, 0, chips)
    far_up, far_down, up, near_up, near_down, down, own_top, own_bottom = blocks
    far_up = lax.ppermute(far_up, "tensor", shift(1))
    far_down = lax.ppermute(far_down, "tensor", shift(-1))
    mine = down_mix(arrived, adapter_down)
    mine, far_up, far_down = lax.optimization_barrier((mine, far_up, far_down))
    pair = (mine + lax.ppermute(mine, "tensor", swap)).astype(jnp.bfloat16)
    mixes = [pair] + [lax.ppermute(pair, "tensor", shift(k)) for k in range(1, chips)]
    terms = up_terms(mixes, arrived, adapter_up)
    terms, up, down, near_up, near_down = lax.optimization_barrier(
        (terms, up, down, near_up, near_down)
    )
    from_below = lax.ppermute(near_up, "tensor", shift(1))
    from_above = lax.ppermute(near_down, "tensor", shift(-1))
    up, down = merge(up, down, far_up, far_down)
    up = lax.ppermute(up, "tensor", shift(1))
    down = lax.ppermute(down, "tensor", shift(-1))
    terms = lax.all_to_all(
        terms.reshape(owners, owner_rows, -1), "dp", 0, 0, tiled=True
    ).reshape(owners * owner_rows, -1)
    halves = (own_top, own_bottom, up, from_below, from_above, down)
    return finish(halves, terms, dest, drafts, slots)


def solution(mesh):
    placed = (
        P(None, "dp", "tensor"),
        P(None, "dp", "tensor"),
        P(None, "dp", "tensor"),
        P("dp", None, "tensor"),
        P("dp", None, "tensor"),
        P("dp"),
        P("dp"),
        P(),
        P("tensor", None),
        P("dp", None, "tensor"),
        P("dp", None, "tensor"),
    )
    return jax.shard_map(
        body, mesh=mesh, in_specs=placed, out_specs=P(None, "dp", "tensor"), check_vma=False
    )
```

time: 103 us -> 77.8 us (0.76)
  blocking collectives: 45.9 us -> 0 us
  starting transfers between devices: 5.66 us -> 29.8 us
  waiting for transfers between devices: 4.69 us -> 21.1 us
  between operations: 13.4 us -> 0.14 us
  Pallas kernels: 30.9 us -> 20.2 us
  local copies, waits for them, and re-layouts: 0.62 us -> 5.99 us
    all_to_all x2 -> x0, blocking collectives: 45.9 us -> none  [the longest x1 23.4 us: body(): lax.all_to_all(terms.reshape(owners, owner_rows, -1), 'dp', 0, 0, tiled=T...]
    all_to_all x0 -> x2, starting transfers between devices: none -> 15.1 us  [the longest x1 8.13 us: body(): lax.all_to_all(payload.reshape(owners, owner_rows, -1), 'dp', 0, 0, tiled...]
    ppermute x4 -> x12, waiting for transfers between devices: 4.67 us -> 16.4 us  [the longest x1 4.55 us: body(): down = lax.ppermute(down, 'tensor', shift(-1))]
    ppermute x4 -> x12, starting transfers between devices: 5.65 us -> 14.8 us  [the longest x3 5.35 us: body(): lax.ppermute(pair, 'tensor', shift(k))]
    unnamed x10 -> x26, local copies, waits for them, and re-layouts: 0.62 us -> 5.99 us
    all_to_all x0 -> x2, waiting for transfers between devices: none -> 4.75 us  [the longest x1 4.19 us: body(): lax.all_to_all(payload.reshape(owners, owner_rows, -1), 'dp', 0, 0, tiled...]
    pallas_call x1, Pallas kernels: 3.59 us -> 1.04 us  [up_terms(): pl.pallas_call(up_kernel, grid=(1,), in_specs=[mix_spec] * 4 + [pl.BlockS...]
    pallas_call x1, Pallas kernels: 12.2 us -> 9.72 us  [attend(): pl.pallas_call(functools.partial(attend_kernel, slots, owner_rows, span),...]
  transfers between devices with their start and end apart: 5 -> 14, of which waited for: 3 -> 10; matrix products, arithmetic and copies ran while one was open for 1% -> 0% of each run, Pallas kernels for 6% -> 23%
where the time goes in v3:
time: 77.8 us; the launch traced here: 77.3 us
  starting transfers between devices  29.8 us (38%)
  waiting for transfers between devices  21.1 us (27%)
  Pallas kernels  20.2 us (26%)
  local copies, waits for them, and re-layouts  5.99 us (8%)
    pallas_call x1, Pallas kernels, attend(): pl.pallas_call(functools.partial(attend_kernel, slots, owner_rows, span),...  9.72 us
    all_to_all x1, starting transfers between devices, body(): lax.all_to_all(payload.reshape(owners, owner_rows, -1), 'dp', 0, 0, tiled...  8.13 us
    all_to_all x1, starting transfers between devices, body(): lax.all_to_all(terms.reshape(owners, owner_rows, -1), 'dp', 0, 0, tiled=T...  6.93 us
    pallas_call x1, Pallas kernels, project(): pl.pallas_call(functools.partial(project_kernel, first), in_specs=[hbm] *...  6.86 us
    unnamed x26, local copies, waits for them, and re-layouts  5.99 us
    ppermute x3, starting transfers between devices, body(): lax.ppermute(pair, 'tensor', shift(k))  5.35 us
    ppermute x1, waiting for transfers between devices, body(): down = lax.ppermute(down, 'tensor', shift(-1))  4.55 us
    all_to_all x1, waiting for transfers between devices, body(): lax.all_to_all(payload.reshape(owners, owner_rows, -1), 'dp', 0, 0, tiled...  4.19 us
  transfers between devices with their start and end apart: 14, of which 10 were waited for; matrix products, arithmetic and copies ran while one was open for 0% of the time, Pallas kernels for 23%

profile of v3, /device:TPU:0, one launch (start us, length us, event | category | flops | bytes accessed | tf_op | source)
XLA Modules:
  0.0 77.3 jit_solution(10912024876032969271)
XLA Ops:
  0.0 0.0 collective-permute-start.1
  0.0 9.7 %attend.1 = (bf16[3,96,512]{2,1,0:T(8,128)(2,1)}, bf16[640,640]{1,0:T(8,128)(2,1)}, s32[96,128]{1,0:T(8,128)}) custom-call(s32[96]{0:T(128)} %lengths.1, s32[1,96]{1,0:T(1,128)} %bitcast.19, s32[1,256]{1,0:T(1,128)} %bitcast.18, bf16[3,96,512]{2,1,0:T(8,128)(2,1)} %q_hbm.1, bf16[3,96,128]{2,1,0:T(8,128)(2,1)} %dk_hbm.1, bf16[3,96,128]{2,1,0:T(8,128)(2,1)} %dv_hbm.1, ...), custom_call_target="tpu_custom_call" | custom-call | flops 301989888 | bytes 12582912 | tf_op jit(solution)/shard_map/attend/pallas_call | solution.py:165
  9.7 0.6 collective-permute-start
  10.3 8.1 %all-to-all-start = ((bf16[16,40,640]{2,1,0:T(8,128)(2,1)}), bf16[16,40,640]{2,1,0:T(8,128)(2,1)S(1)}, u32[]{:S(2)}, u32[]{:S(2)}) async-start(bf16[16,40,640]{2,1,0:T(8,128)(2,1)} %bitcast.15), calls=%async_computation | async-start | bytes 1638400 | tf_op jit(solution)/shard_map/all_to_all | solution.py:424
  18.5 0.0 collective-permute-done.attn_other
  18.5 0.0 copy-start.12
  18.5 0.7 copy-done.12
  19.2 0.0 collective-permute-done.1.weight_other
  19.2 0.0 copy-start.11
  19.2 6.9 %project.1 = (bf16[144,1024]{1,0:T(8,128)(2,1)}, bf16[144,1024]{1,0:T(8,128)(2,1)}, bf16[144,1024]{1,0:T(8,128)(2,1)}, bf16[144,1024]{1,0:T(8,128)(2,1)}, bf16[1...) custom-call(bf16[288,512]{1,0:T(8,128)(2,1)} %bitcast.17, ...), custom_call_target="tpu_custom_call" | custom-call | flops 2415919104 | bytes 8388608 | tf_op jit(solution)/shard_map/project/pallas_call | solution.py:250
  26.1 1.6 %collective-permute-start.2 = (bf16[144,1024]{1,0:T(8,128)(2,1)}, bf16[144,1024]{1,0:T(8,128)(2,1)S(1)}, u32[]{:S(2)}, u32[]{:S(2)}) collective-permute-start(bf16[144,1024]{1,0:T(8,128)(2,1)} %get-tuple-element.30), channel_id=1, source_target_pairs={{0,2},{1,3},{2,4},{3,5},{4,6},{5,7},{6,0},{7,1},{8,10},{9,11},{10,... | collective-permute-start | bytes 884744 | tf_op jit(solution)/shard_map/ppermute | solution.py:431
  27.6 1.7 %collective-permute-start.3 = (bf16[144,1024]{1,0:T(8,128)(2,1)}, bf16[144,1024]{1,0:T(8,128)(2,1)S(1)}, u32[]{:S(2)}, u32[]{:S(2)}) collective-permute-start(bf16[144,1024]{1,0:T(8,128)(2,1)} %get-tuple-element.31), channel_id=1, source_target_pairs={{0,6},{1,7},{2,0},{3,1},{4,2},{5,3},{6,4},{7,5},{8,14},{9,15},{10,... | collective-permute-start | bytes 884744 | tf_op jit(solution)/shard_map/ppermute | solution.py:432
  29.4 4.2 %all-to-all-done = bf16[16,40,640]{2,1,0:T(8,128)(2,1)S(1)} async-done(((bf16[16,40,640]{2,1,0:T(8,128)(2,1)}), bf16[16,40,640]{2,1,0:T(8,128)(2,1)S(1)}, u32[]{:S(2)}, u32[]{:S(2)}) %all-to-all-start) | async-done | bytes 819232 | tf_op jit(solution)/shard_map/all_to_all | solution.py:424
  33.5 0.0 copy-start.2
  33.5 1.0 %copy-done.2 = bf16[16,32,512]{2,1,0:T(8,128)(2,1)S(1)} copy-done((bf16[16,32,512]{2,1,0:T(8,128)(2,1)S(1)}, bf16[16,32,512]{2,1,0:T(8,128)(2,1)}, u32[]{:S(2)}) %copy-start.2) | copy-done | bytes 524312
  34.6 0.0 copy-start.5
  34.6 0.0 copy-start.6
  34.6 0.0 copy-start.3
  34.6 0.0 copy-start.4
  34.6 0.7 down_mix.1
  35.3 0.9 %collective-permute-done.2.far_up = bf16[144,1024]{1,0:T(8,128)(2,1)S(1)} collective-permute-done((bf16[144,1024]{1,0:T(8,128)(2,1)}, bf16[144,1024]{1,0:T(8,128)(2,1)S(1)}, u32[]{:S(2)}, u32[]{:S(2)}) %collective-permute-start.2) | collective-permute-done | bytes 294944 | tf_op jit(solution)/shard_map/ppermute | solution.py:431
  36.2 0.0 copy-start.7
  36.2 0.0 collective-permute-done.3.far_down
  36.2 0.0 copy-start.9
  36.2 0.1 collective-permute-start.4
  36.3 1.3 %collective-permute-done.4 = f32[32,640]{1,0:T(8,128)S(1)} collective-permute-done((f32[32,640]{1,0:T(8,128)S(1)}, f32[32,640]{1,0:T(8,128)S(1)}, u32[]{:S(2)}, u32[]{:S(2)}) %collective-permute-start.4) | collective-permute-done | bytes 81952 | tf_op jit(solution)/shard_map/ppermute | solution.py:435
  37.6 1.5 %collective-permute-start.5 = (bf16[32,640]{1,0:T(8,128)(2,1)S(1)}, bf16[32,640]{1,0:T(8,128)(2,1)S(1)}, u32[]{:S(2)}, u32[]{:S(2)}) collective-permute-start(bf16[32,640]{1,0:T(8,128)(2,1)S(1)} %add_convert_fusion.mine), channel_id=1, source_target_pairs={{0,2},{1,3},{2,4},{3,5},{4,6},{5,7},{6,0},{7,1},{8,10},{9,11},{10,... | collective-permute-start | bytes 122888 | tf_op jit(solution)/shard_map/ppermute | solution.py:436
  39.1 2.9 %collective-permute-start.6 = (bf16[32,640]{1,0:T(8,128)(2,1)S(1)}, bf16[32,640]{1,0:T(8,128)(2,1)S(1)}, u32[]{:S(2)}, u32[]{:S(2)}) collective-permute-start(bf16[32,640]{1,0:T(8,128)(2,1)S(1)} %add_convert_fusion.mine), channel_id=1, source_target_pairs={{0,4},{1,5},{2,6},{3,7},{4,0},{5,1},{6,2},{7,3},{8,12},{9,13},{10,... | collective-permute-start | bytes 122888 | tf_op jit(solution)/shard_map/ppermute | solution.py:436
  42.0 0.9 %collective-permute-start.7 = (bf16[32,640]{1,0:T(8,128)(2,1)S(1)}, bf16[32,640]{1,0:T(8,128)(2,1)S(1)}, u32[]{:S(2)}, u32[]{:S(2)}) collective-permute-start(bf16[32,640]{1,0:T(8,128)(2,1)S(1)} %add_convert_fusion.mine), channel_id=1, source_target_pairs={{0,6},{1,7},{2,0},{3,1},{4,2},{5,3},{6,4},{7,5},{8,14},{9,15},{10,... | collective-permute-start | bytes 122888 | tf_op jit(solution)/shard_map/ppermute | solution.py:436
  42.9 0.0 collective-permute-done.5.one
  42.9 1.6 %collective-permute-done.6.two = bf16[32,640]{1,0:T(8,128)(2,1)S(1)} collective-permute-done((bf16[32,640]{1,0:T(8,128)(2,1)S(1)}, bf16[32,640]{1,0:T(8,128)(2,1)S(1)}, u32[]{:S(2)}, u32[]{:S(2)}) %collective-permute-start.6) | collective-permute-done | bytes 40992 | tf_op jit(solution)/shard_map/ppermute | solution.py:436
  44.6 1.4 %collective-permute-done.7.three = bf16[32,640]{1,0:T(8,128)(2,1)S(1)} collective-permute-done((bf16[32,640]{1,0:T(8,128)(2,1)S(1)}, bf16[32,640]{1,0:T(8,128)(2,1)S(1)}, u32[]{:S(2)}, u32[]{:S(2)}) %collective-permute-start.7) | collective-permute-done | bytes 40992 | tf_op jit(solution)/shard_map/ppermute | solution.py:436
  46.0 0.0 copy-start.1
  46.0 1.2 %copy-done.1 = bf16[16,32,1024]{2,1,0:T(8,128)(2,1)S(1)} copy-done((bf16[16,32,1024]{2,1,0:T(8,128)(2,1)S(1)}, bf16[16,32,1024]{2,1,0:T(8,128)(2,1)}, u32[]{:S(2)}) %copy-start.1) | copy-done | bytes 1048600
  47.2 1.0 %up_terms.1 = bf16[640,1024]{1,0:T(8,128)(2,1)S(1)} custom-call(bf16[32,640]{1,0:T(8,128)(2,1)S(1)} %add_convert_fusion.mine, bf16[32,640]{1,0:T(8,128)(2,1)S(1)} %collective-permute-done.5.one, bf16[32,640]{1,0:T(8,128)(2,1)S(1)} %collective-permute-done.6.two, bf16[32,640]{1,0:T(8,128)(2,1)S(1)} %collective-permute-done.7.three, ...), custom_call_target="tpu_custom_call" | custom-call | flops 671088640 | bytes 2359296 | tf_op jit(solution)/shard_map/up_terms/pallas_call | solution.py:348
  48.3 0.0 copy-start
  48.3 1.1 %copy-done = bf16[640,1024]{1,0:T(8,128)(2,1)} copy-done((bf16[640,1024]{1,0:T(8,128)(2,1)}, bf16[640,1024]{1,0:T(8,128)(2,1)S(1)}, u32[]{:S(2)}) %copy-start) | copy-done | bytes 1310744
  49.3 0.0 copy-done.7
  49.4 0.0 copy-done.9
  49.4 6.9 %all-to-all-start.1 = ((bf16[16,40,1024]{2,1,0:T(8,128)(2,1)}), bf16[16,40,1024]{2,1,0:T(8,128)(2,1)S(1)}, u32[]{:S(2)}, u32[]{:S(2)}) async-start(bf16[16,40,1024]{2,1,0:T(8,128)(2,1)} %bitcast.12), calls=%async_computation.1 | async-start | bytes 2621440 | tf_op jit(solution)/shard_map/all_to_all | solution.py:446
  56.3 0.0 copy-done.5
  56.3 0.0 copy-done.6
  56.3 0.0 copy-start.8
  56.3 1.0 %copy-done.8 = bf16[144,1024]{1,0:T(8,128)(2,1)S(1)} copy-done((bf16[144,1024]{1,0:T(8,128)(2,1)S(1)}, bf16[144,1024]{1,0:T(8,128)(2,1)}, u32[]{:S(2)}) %copy-start.8) | copy-done | bytes 294936
  57.3 0.0 copy-start.10
  57.3 1.0 %copy-done.10 = bf16[144,1024]{1,0:T(8,128)(2,1)S(1)} copy-done((bf16[144,1024]{1,0:T(8,128)(2,1)S(1)}, bf16[144,1024]{1,0:T(8,128)(2,1)}, u32[]{:S(2)}) %copy-start.10) | copy-done | bytes 294936
  58.2 0.1 merge.1
  58.4 2.2 %collective-permute-start.11 = (bf16[144,1024]{1,0:T(8,128)(2,1)S(1)}, bf16[144,1024]{1,0:T(8,128)(2,1)S(1)}, u32[]{:S(2)}, u32[]{:S(2)}) collective-permute-start(bf16[144,1024]{1,0:T(8,128)(2,1)S(1)} %get-tuple-element.44), channel_id=1, source_target_pairs={{0,6},{1,7},{2,0},{3,1},{4,2},{5,3},{6,4},{7,5},{8,14},{9,15},{10,... | collective-permute-start | bytes 884744 | tf_op jit(solution)/shard_map/ppermute | solution.py:445
  60.6 0.0 collective-permute-start.8
  60.6 3.2 %collective-permute-start.10 = (bf16[144,1024]{1,0:T(8,128)(2,1)}, bf16[144,1024]{1,0:T(8,128)(2,1)S(1)}, u32[]{:S(2)}, u32[]{:S(2)}) collective-permute-start(bf16[144,1024]{1,0:T(8,128)(2,1)} %get-tuple-element.43), channel_id=1, source_target_pairs={{0,6},{1,7},{2,0},{3,1},{4,2},{5,3},{6,4},{7,5},{8,14},{9,15},{10,... | collective-permute-start | bytes 884744 | tf_op jit(solution)/shard_map/ppermute | solution.py:442
  63.8 0.0 collective-permute-start.9
  63.8 4.6 %collective-permute-done.11.refs_5_ = bf16[144,1024]{1,0:T(8,128)(2,1)S(1)} collective-permute-done((bf16[144,1024]{1,0:T(8,128)(2,1)S(1)}, bf16[144,1024]{1,0:T(8,128)(2,1)S(1)}, u32[]{:S(2)}, u32[]{:S(2)}) %collective-permute-start.11) | collective-permute-done | bytes 294944 | tf_op jit(solution)/shard_map/ppermute | solution.py:445
  68.4 3.4 %collective-permute-done.8.refs_2_ = bf16[144,1024]{1,0:T(8,128)(2,1)S(1)} collective-permute-done((bf16[144,1024]{1,0:T(8,128)(2,1)S(1)}, bf16[144,1024]{1,0:T(8,128)(2,1)S(1)}, u32[]{:S(2)}, u32[]{:S(2)}) %collective-permute-start.8) | collective-permute-done | bytes 294944 | tf_op jit(solution)/shard_map/ppermute | solution.py:444
  71.8 0.3 collective-permute-done.10.refs_4_
  72.1 2.9 %collective-permute-done.9.refs_3_ = bf16[144,1024]{1,0:T(8,128)(2,1)S(1)} collective-permute-done((bf16[144,1024]{1,0:T(8,128)(2,1)}, bf16[144,1024]{1,0:T(8,128)(2,1)S(1)}, u32[]{:S(2)}, u32[]{:S(2)}) %collective-permute-start.9) | collective-permute-done | bytes 294944 | tf_op jit(solution)/shard_map/ppermute | solution.py:441
  75.0 0.6 all-to-all-done.1
  75.6 0.0 copy-done.11
  75.6 0.0 copy-done.3
  75.6 0.0 copy-done.4
  75.6 1.7 %finish.1 = bf16[3,96,1024]{2,1,0:T(8,128)(2,1)} custom-call(bf16[144,1024]{1,0:T(8,128)(2,1)S(1)} %copy-done.3, bf16[144,1024]{1,0:T(8,128)(2,1)S(1)} %copy-done.4, bf16[144,1024]{1,0:T(8,128)(2,1)S(1)} %collective-permute-done.8.refs_2_, bf16[144,1024]{1,0:T(8,128)(2,1)S(1)} %collective-permute-done.9.refs_3_, ...), custom_call_target="tpu_custom_call" | custom-call | flops 377487360 | bytes 1310720 | tf_op jit(solution)/shard_map/finish/pallas_call | solution.py:384
  (1 shorter events, 0.0 us)
Async XLA Ops:
  0.0 19.2 %collective-permute-start.1 = (bf16[512,8192]{1,0:T(8,128)(2,1)}, bf16[512,8192]{1,0:T(8,128)(2,1)}, u32[]{:S(2)}, u32[]{:S(2)}) collective-permute-start(bf16[512,8192]{1,0:T(8,128)(2,1)} %weight.1), channel_id=1, source_target_pairs={{0,1},{1,0},{2,3},{3,2},{4,5},{5,4},{6,7},{7,6},{8,9},{9,8},{10,11... | collective-permute-start | bytes 25165832 | tf_op jit(solution)/shard_map/ppermute | solution.py:419
  9.7 8.7 %collective-permute-start = (bf16[288,512]{1,0:T(8,128)(2,1)}, bf16[288,512]{1,0:T(8,128)(2,1)S(1)}, u32[]{:S(2)}, u32[]{:S(2)}) collective-permute-start(bf16[288,512]{1,0:T(8,128)(2,1)} %bitcast.16), channel_id=1, source_target_pairs={{0,1},{1,0},{2,3},{3,2},{4,5},{5,4},{6,7},{7,6},{8,9},{9,8},{10,11... | collective-permute-start | bytes 884744 | tf_op jit(solution)/shard_map/ppermute | solution.py:428
  10.3 23.2 %all-to-all-start = ((bf16[16,40,640]{2,1,0:T(8,128)(2,1)}), bf16[16,40,640]{2,1,0:T(8,128)(2,1)S(1)}, u32[]{:S(2)}, u32[]{:S(2)}) async-start(bf16[16,40,640]{2,1,0:T(8,128)(2,1)} %bitcast.15), calls=%async_computation | async-start | bytes 1638400 | tf_op jit(solution)/shard_map/all_to_all | solution.py:424
  18.5 0.7 copy-start.12
  19.2 56.4 %copy-start.11 = (s32[96,128]{1,0:T(8,128)S(1)}, s32[96,128]{1,0:T(8,128)}, u32[]{:S(2)}) copy-start(s32[96,128]{1,0:T(8,128)} %get-tuple-element.46.refs_7_) | copy-start | bytes 147460
  26.1 10.1 %collective-permute-start.2 = (bf16[144,1024]{1,0:T(8,128)(2,1)}, bf16[144,1024]{1,0:T(8,128)(2,1)S(1)}, u32[]{:S(2)}, u32[]{:S(2)}) collective-permute-start(bf16[144,1024]{1,0:T(8,128)(2,1)} %get-tuple-element.30), channel_id=1, source_target_pairs={{0,2},{1,3},{2,4},{3,5},{4,6},{5,7},{6,0},{7,1},{8,10},{9,11},{10,... | collective-permute-start | bytes 884744 | tf_op jit(solution)/shard_map/ppermute | solution.py:431
  27.6 8.6 %collective-permute-start.3 = (bf16[144,1024]{1,0:T(8,128)(2,1)}, bf16[144,1024]{1,0:T(8,128)(2,1)S(1)}, u32[]{:S(2)}, u32[]{:S(2)}) collective-permute-start(bf16[144,1024]{1,0:T(8,128)(2,1)} %get-tuple-element.31), channel_id=1, source_target_pairs={{0,6},{1,7},{2,0},{3,1},{4,2},{5,3},{6,4},{7,5},{8,14},{9,15},{10,... | collective-permute-start | bytes 884744 | tf_op jit(solution)/shard_map/ppermute | solution.py:432
  33.5 1.0 %copy-start.2 = (bf16[16,32,512]{2,1,0:T(8,128)(2,1)S(1)}, bf16[16,32,512]{2,1,0:T(8,128)(2,1)}, u32[]{:S(2)}) copy-start(bf16[16,32,512]{2,1,0:T(8,128)(2,1)} %param.20) | copy-start | bytes 1572868
  34.6 21.7 %copy-start.5 = (bf16[144,1024]{1,0:T(8,128)(2,1)S(1)}, bf16[144,1024]{1,0:T(8,128)(2,1)}, u32[]{:S(2)}) copy-start(bf16[144,1024]{1,0:T(8,128)(2,1)} %get-tuple-element.37.up) | copy-start | bytes 884740
  34.6 21.7 %copy-start.6 = (bf16[144,1024]{1,0:T(8,128)(2,1)S(1)}, bf16[144,1024]{1,0:T(8,128)(2,1)}, u32[]{:S(2)}) copy-start(bf16[144,1024]{1,0:T(8,128)(2,1)} %get-tuple-element.38.down) | copy-start | bytes 884740
  34.6 41.0 %copy-start.3 = (bf16[144,1024]{1,0:T(8,128)(2,1)S(1)}, bf16[144,1024]{1,0:T(8,128)(2,1)}, u32[]{:S(2)}) copy-start(bf16[144,1024]{1,0:T(8,128)(2,1)} %get-tuple-element.27.refs_0_) | copy-start | bytes 884740
  34.6 41.0 %copy-start.4 = (bf16[144,1024]{1,0:T(8,128)(2,1)S(1)}, bf16[144,1024]{1,0:T(8,128)(2,1)}, u32[]{:S(2)}) copy-start(bf16[144,1024]{1,0:T(8,128)(2,1)} %get-tuple-element.28.refs_1_) | copy-start | bytes 884740
  36.2 13.2 %copy-start.7 = (bf16[144,1024]{1,0:T(8,128)(2,1)}, bf16[144,1024]{1,0:T(8,128)(2,1)S(1)}, u32[]{:S(2)}) copy-start(bf16[144,1024]{1,0:T(8,128)(2,1)S(1)} %collective-permute-done.2.far_up) | copy-start | bytes 884740
  36.2 13.1 %copy-start.9 = (bf16[144,1024]{1,0:T(8,128)(2,1)}, bf16[144,1024]{1,0:T(8,128)(2,1)S(1)}, u32[]{:S(2)}) copy-start(bf16[144,1024]{1,0:T(8,128)(2,1)S(1)} %collective-permute-done.3.far_down) | copy-start | bytes 884740
  36.2 1.4 %collective-permute-start.4 = (f32[32,640]{1,0:T(8,128)S(1)}, f32[32,640]{1,0:T(8,128)S(1)}, u32[]{:S(2)}, u32[]{:S(2)}) collective-permute-start(f32[32,640]{1,0:T(8,128)S(1)} %down_mix.1), channel_id=1, source_target_pairs={{0,1},{1,0},{2,3},{3,2},{4,5},{5,4},{6,7},{7,6},{8,9},{9,8},{10,11... | collective-permute-start | bytes 245768 | tf_op jit(solution)/shard_map/ppermute | solution.py:435
  37.6 5.4 %collective-permute-start.5 = (bf16[32,640]{1,0:T(8,128)(2,1)S(1)}, bf16[32,640]{1,0:T(8,128)(2,1)S(1)}, u32[]{:S(2)}, u32[]{:S(2)}) collective-permute-start(bf16[32,640]{1,0:T(8,128)(2,1)S(1)} %add_convert_fusion.mine), channel_id=1, source_target_pairs={{0,2},{1,3},{2,4},{3,5},{4,6},{5,7},{6,0},{7,1},{8,10},{9,11},{10,... | collective-permute-start | bytes 122888 | tf_op jit(solution)/shard_map/ppermute | solution.py:436
  39.1 5.5 %collective-permute-start.6 = (bf16[32,640]{1,0:T(8,128)(2,1)S(1)}, bf16[32,640]{1,0:T(8,128)(2,1)S(1)}, u32[]{:S(2)}, u32[]{:S(2)}) collective-permute-start(bf16[32,640]{1,0:T(8,128)(2,1)S(1)} %add_convert_fusion.mine), channel_id=1, source_target_pairs={{0,4},{1,5},{2,6},{3,7},{4,0},{5,1},{6,2},{7,3},{8,12},{9,13},{10,... | collective-permute-start | bytes 122888 | tf_op jit(solution)/shard_map/ppermute | solution.py:436
  42.0 4.0 %collective-permute-start.7 = (bf16[32,640]{1,0:T(8,128)(2,1)S(1)}, bf16[32,640]{1,0:T(8,128)(2,1)S(1)}, u32[]{:S(2)}, u32[]{:S(2)}) collective-permute-start(bf16[32,640]{1,0:T(8,128)(2,1)S(1)} %add_convert_fusion.mine), channel_id=1, source_target_pairs={{0,6},{1,7},{2,0},{3,1},{4,2},{5,3},{6,4},{7,5},{8,14},{9,15},{10,... | collective-permute-start | bytes 122888 | tf_op jit(solution)/shard_map/ppermute | solution.py:436
  46.0 1.2 %copy-start.1 = (bf16[16,32,1024]{2,1,0:T(8,128)(2,1)S(1)}, bf16[16,32,1024]{2,1,0:T(8,128)(2,1)}, u32[]{:S(2)}) copy-start(bf16[16,32,1024]{2,1,0:T(8,128)(2,1)} %param.21) | copy-start | bytes 3145732
  48.3 1.1 %copy-start = (bf16[640,1024]{1,0:T(8,128)(2,1)}, bf16[640,1024]{1,0:T(8,128)(2,1)S(1)}, u32[]{:S(2)}) copy-start(bf16[640,1024]{1,0:T(8,128)(2,1)S(1)} %up_terms.1) | copy-start | bytes 3932164
  49.4 26.2 %all-to-all-start.1 = ((bf16[16,40,1024]{2,1,0:T(8,128)(2,1)}), bf16[16,40,1024]{2,1,0:T(8,128)(2,1)S(1)}, u32[]{:S(2)}, u32[]{:S(2)}) async-start(bf16[16,40,1024]{2,1,0:T(8,128)(2,1)} %bitcast.12), calls=%async_computation.1 | async-start | bytes 2621440 | tf_op jit(solution)/shard_map/all_to_all | solution.py:446
  56.3 1.0 %copy-start.8 = (bf16[144,1024]{1,0:T(8,128)(2,1)S(1)}, bf16[144,1024]{1,0:T(8,128)(2,1)}, u32[]{:S(2)}) copy-start(bf16[144,1024]{1,0:T(8,128)(2,1)} %copy-done.7) | copy-start | bytes 884740
  57.3 1.0 %copy-start.10 = (bf16[144,1024]{1,0:T(8,128)(2,1)S(1)}, bf16[144,1024]{1,0:T(8,128)(2,1)}, u32[]{:S(2)}) copy-start(bf16[144,1024]{1,0:T(8,128)(2,1)} %copy-done.9) | copy-start | bytes 884740
  58.4 10.0 %collective-permute-start.11 = (bf16[144,1024]{1,0:T(8,128)(2,1)S(1)}, bf16[144,1024]{1,0:T(8,128)(2,1)S(1)}, u32[]{:S(2)}, u32[]{:S(2)}) collective-permute-start(bf16[144,1024]{1,0:T(8,128)(2,1)S(1)} %get-tuple-element.44), channel_id=1, source_target_pairs={{0,6},{1,7},{2,0},{3,1},{4,2},{5,3},{6,4},{7,5},{8,14},{9,15},{10,... | collective-permute-start | bytes 884744 | tf_op jit(solution)/shard_map/ppermute | solution.py:445
  60.6 11.2 %collective-permute-start.8 = (bf16[144,1024]{1,0:T(8,128)(2,1)S(1)}, bf16[144,1024]{1,0:T(8,128)(2,1)S(1)}, u32[]{:S(2)}, u32[]{:S(2)}) collective-permute-start(bf16[144,1024]{1,0:T(8,128)(2,1)S(1)} %get-tuple-element.41), channel_id=1, source_target_pairs={{0,2},{1,3},{2,4},{3,5},{4,6},{5,7},{6,0},{7,1},{8,10},{9,11},{10,... | collective-permute-start | bytes 884744 | tf_op jit(solution)/shard_map/ppermute | solution.py:444
  60.6 11.5 %collective-permute-start.10 = (bf16[144,1024]{1,0:T(8,128)(2,1)}, bf16[144,1024]{1,0:T(8,128)(2,1)S(1)}, u32[]{:S(2)}, u32[]{:S(2)}) collective-permute-start(bf16[144,1024]{1,0:T(8,128)(2,1)} %get-tuple-element.43), channel_id=1, source_target_pairs={{0,6},{1,7},{2,0},{3,1},{4,2},{5,3},{6,4},{7,5},{8,14},{9,15},{10,... | collective-permute-start | bytes 884744 | tf_op jit(solution)/shard_map/ppermute | solution.py:442
  63.8 11.2 %collective-permute-start.9 = (bf16[144,1024]{1,0:T(8,128)(2,1)}, bf16[144,1024]{1,0:T(8,128)(2,1)S(1)}, u32[]{:S(2)}, u32[]{:S(2)}) collective-permute-start(bf16[144,1024]{1,0:T(8,128)(2,1)} %get-tuple-element.42), channel_id=1, source_target_pairs={{0,2},{1,3},{2,4},{3,5},{4,6},{5,7},{6,0},{7,1},{8,10},{9,11},{10,... | collective-permute-start | bytes 884744 | tf_op jit(solution)/shard_map/ppermute | solution.py:441

commit v4 on v3

--- a/solution.py
+++ b/solution.py
@@ -192,10 +192,9 @@
     )(lengths, request_adapter.reshape(1, rows), table.reshape(1, -1), queries, draft_keys, draft_values, key_cache, value_cache)
 
 
-def project_kernel(first, attn, attn_other, weight, weight_other, *refs):
+def project_kernel(first, cuts, attn, attn_other, weight, weight_other, *refs):
     outs, (flat, held, done, sems, in_sems, out_sems) = refs[:-6], refs[-6:]
-    _, half, width = flat.shape
-    half = half // 2
+    _, rows, width = flat.shape
     place = lax.axis_index("tensor")
     chips = lax.axis_size("tensor") // 2
     blocks, sources, _, part = held.shape
@@ -234,36 +233,37 @@
             part_sum = jnp.dot(flat[n], held[j, n], preferred_element_type=jnp.float32)
             total = part_sum if total is None else total + part_sum
         done[j] = total.astype(jnp.bfloat16)
-        for n in range(2):
-            at = 2 * j + n
-            stores.append(pltpu.make_async_copy(done.at[j, pl.ds(n * half, half)], outs[at], out_sems.at[at]))
+        for n in range(cuts):
+            at = cuts * j + n
+            here = pl.ds(n * (rows // cuts), rows // cuts)
+            stores.append(pltpu.make_async_copy(done.at[j, here], outs[at], out_sems.at[at]))
             stores[-1].start()
     for store in stores:
         store.wait()
 
 
-def project(attn, attn_other, weight, weight_other, parts, first, blocks):
+def project(attn, attn_other, weight, weight_other, parts, first, blocks, cuts=2):
     rows, width = attn.shape
     part = weight.shape[1] // parts
     hbm = pl.BlockSpec(memory_space=pltpu.HBM)
-    half = jax.ShapeDtypeStruct((rows // 2, part), jnp.bfloat16)
-    return pl.pallas_call(
-        functools.partial(project_kernel, first),
+    piece = jax.ShapeDtypeStruct((rows // cuts, part), jnp.bfloat16)
+    return pl.pallas_call(
+        functools.partial(project_kernel, first, cuts),
         in_specs=[hbm] * 4,
-        out_specs=[hbm] * (2 * blocks),
-        out_shape=[half] * (2 * blocks),
+        out_specs=[hbm] * (cuts * blocks),
+        out_shape=[piece] * (cuts * blocks),
         scratch_shapes=[
             pltpu.VMEM((2, rows, width), jnp.bfloat16),
             pltpu.VMEM((blocks, 2, width, part), jnp.bfloat16),
             pltpu.VMEM((blocks, rows, part), jnp.bfloat16),
             pltpu.SemaphoreType.DMA((blocks, 2)),
             pltpu.SemaphoreType.DMA((2,)),
-            pltpu.SemaphoreType.DMA((2 * blocks,)),
+            pltpu.SemaphoreType.DMA((cuts * blocks,)),
         ],
-        compiler_params=pltpu.CompilerParams(vmem_limit_bytes=VMEM),
+        compiler_params=pltpu.CompilerParams(vmem_limit_bytes=VMEM * 8 // 9),
         cost_estimate=pl.CostEstimate(
-            flops=4 * rows * width * part * blocks,
-            bytes_accessed=4 * width * part * blocks,
+            flops=16 * rows * width * part * blocks,
+            bytes_accessed=16 * width * part * blocks,
             transcendentals=0,
         ),
         name="project",
@@ -361,24 +361,37 @@
     )(*mixes, arrived, up.reshape(span * rank, width))
 
 
-def finish_kernel(slots, *refs):
-    halves, (terms, dest, out) = refs[:6], refs[6:]
+def gather_kernel(own, *refs):
+    parts, out = refs[:4], refs[4]
+    half = parts[0].shape[0]
+    for n in range(2):
+        here = slice(n * half, (n + 1) * half)
+        a, b = parts[n::2]
+        out[here] = own[here].astype(jnp.float32) + a[...].astype(jnp.float32) + b[...].astype(jnp.float32)
+
+
+def gather_base(own, parts):
+    return pl.pallas_call(
+        gather_kernel,
+        out_shape=jax.ShapeDtypeStruct(own.shape, jnp.float32),
+        compiler_params=pltpu.CompilerParams(vmem_limit_bytes=VMEM // 4),
+        cost_estimate=pl.CostEstimate(flops=0, bytes_accessed=10 * own.size, transcendentals=0),
+        name="gather_base",
+    )(own, *parts)
+
+
+def finish_kernel(slots, base, terms, dest, out):
     drafts, rows, width = out.shape
     places = terms.shape[0]
     lane = lax.broadcasted_iota(jnp.int32, (rows, places), 1)
     where_to = dest[:, :1]
-    total = []
-    for n in range(2):
-        a, b, c = halves[n::2]
-        total.append(a[...].astype(jnp.float32) + b[...].astype(jnp.float32) + c[...].astype(jnp.float32))
-    total = jnp.concatenate(total, axis=0)
     for s in range(drafts):
         pick = jnp.where(lane == where_to + s * slots, 1.0, 0.0).astype(jnp.bfloat16)
         term = jnp.dot(pick, terms[...], preferred_element_type=jnp.float32)
-        out[s] = (total[s * rows:(s + 1) * rows] + term).astype(jnp.bfloat16)
-
-
-def finish(halves, terms, dest, drafts, slots):
+        out[s] = (base[s * rows:(s + 1) * rows] + term).astype(jnp.bfloat16)
+
+
+def finish(base, terms, dest, drafts, slots):
     rows = dest.shape[0]
     width = terms.shape[1]
     return pl.pallas_call(
@@ -389,7 +402,7 @@
             flops=2 * terms.size * rows * drafts, bytes_accessed=2 * terms.size, transcendentals=0
         ),
         name="finish",
-    )(*halves, terms, dest)
+    )(base, terms, dest)
 
 
 def body(
@@ -426,28 +439,31 @@
     ).reshape(owners * owner_rows, -1)
     attn = attn.reshape(drafts * rows, width)
     attn_other = lax.ppermute(attn, "tensor", swap)
-    blocks = project(attn, attn_other, output_weight, weight_other, parts, 0, chips)
-    far_up, far_down, up, near_up, near_down, down, own_top, own_bottom = blocks
+    weights = (output_weight, weight_other, parts)
+    far_up, far_down = project(attn, attn_other, *weights, 0, 1)
     far_up = lax.ppermute(far_up, "tensor", shift(1))
     far_down = lax.ppermute(far_down, "tensor", shift(-1))
+    up, near_up, near_down, down = project(attn, attn_other, *weights, 1, 2)
+    arrived, up = lax.optimization_barrier((arrived, up))
     mine = down_mix(arrived, adapter_down)
     mine, far_up, far_down = lax.optimization_barrier((mine, far_up, far_down))
     pair = (mine + lax.ppermute(mine, "tensor", swap)).astype(jnp.bfloat16)
     mixes = [pair] + [lax.ppermute(pair, "tensor", shift(k)) for k in range(1, chips)]
     terms = up_terms(mixes, arrived, adapter_up)
-    terms, up, down, near_up, near_down = lax.optimization_barrier(
-        (terms, up, down, near_up, near_down)
+    terms, up, down, near_up, near_down, attn = lax.optimization_barrier(
+        (terms, up, down, near_up, near_down, attn)
     )
     from_below = lax.ppermute(near_up, "tensor", shift(1))
     from_above = lax.ppermute(near_down, "tensor", shift(-1))
     up, down = merge(up, down, far_up, far_down)
     up = lax.ppermute(up, "tensor", shift(1))
     down = lax.ppermute(down, "tensor", shift(-1))
+    (own,) = project(attn, attn_other, *weights, 3, 1, cuts=1)
     terms = lax.all_to_all(
         terms.reshape(owners, owner_rows, -1), "dp", 0, 0, tiled=True
     ).reshape(owners * owner_rows, -1)
-    halves = (own_top, own_bottom, up, from_below, from_above, down)
-    return finish(halves, terms, dest, drafts, slots)
+    base = gather_base(own, (up, from_below, from_above, down))
+    return finish(base, terms, dest, drafts, slots)
 
 
 def solution(mesh):

time: 77.8 us -> 73.6 us (0.946)
  Pallas kernels: 20.2 us -> 26.6 us
  waiting for transfers between devices: 21.1 us -> 15.8 us
  local copies, waits for them, and re-layouts: 5.99 us -> 1.79 us
  starting transfers between devices: 29.8 us -> 28.8 us
    pallas_call x1 -> x4, Pallas kernels: 6.86 us -> 12.2 us  [the longest x3 12 us: project(): pl.pallas_call(functools.partial(project_kernel, first, cuts), in_specs=[...]
    ppermute x1, waiting for transfers between devices: 4.55 us -> 0.01 us  [body(): down = lax.ppermute(down, 'tensor', shift(-1))]
    unnamed x26 -> x14, local copies, waits for them, and re-layouts: 5.99 us -> 1.79 us
    all_to_all x1, waiting for transfers between devices: 0.56 us -> 2.74 us  [body(): lax.all_to_all(terms.reshape(owners, owner_rows, -1), 'dp', 0, 0, tiled=T...]
    ppermute x1, waiting for transfers between devices: 3.37 us -> 1.21 us  [body(): up = lax.ppermute(up, 'tensor', shift(1))]
    all_to_all x1, waiting for transfers between devices: 4.19 us -> 2.51 us  [body(): lax.all_to_all(payload.reshape(owners, owner_rows, -1), 'dp', 0, 0, tiled...]
    all_to_all x1, starting transfers between devices: 6.93 us -> 5.5 us  [body(): lax.all_to_all(terms.reshape(owners, owner_rows, -1), 'dp', 0, 0, tiled=T...]
    ppermute x3, waiting for transfers between devices: 3.06 us -> 4.32 us  [body(): lax.ppermute(pair, 'tensor', shift(k))]
  transfers between devices with their start and end apart: 14 -> 14, of which waited for: 10 -> 8; matrix products, arithmetic and copies ran while one was open for 0% -> 0% of each run, Pallas kernels for 23% -> 31%
where the time goes in v4:
time: 73.6 us; the launch traced here: 73.2 us
  starting transfers between devices  28.8 us (39%)
  Pallas kernels  26.6 us (36%)
  waiting for transfers between devices  15.8 us (21%)
  local copies, waits for them, and re-layouts  1.79 us (2%)
    pallas_call x3, Pallas kernels, project(): pl.pallas_call(functools.partial(project_kernel, first, cuts), in_specs=[...  12 us
    pallas_call x1, Pallas kernels, attend(): pl.pallas_call(functools.partial(attend_kernel, slots, owner_rows, span),...  9.72 us
    all_to_all x1, starting transfers between devices, body(): lax.all_to_all(payload.reshape(owners, owner_rows, -1), 'dp', 0, 0, tiled...  8.13 us
    all_to_all x1, starting transfers between devices, body(): lax.all_to_all(terms.reshape(owners, owner_rows, -1), 'dp', 0, 0, tiled=T...  5.5 us
    ppermute x3, starting transfers between devices, body(): lax.ppermute(pair, 'tensor', shift(k))  4.52 us
    ppermute x3, waiting for transfers between devices, body(): lax.ppermute(pair, 'tensor', shift(k))  4.32 us
    ppermute x1, waiting for transfers between devices, body(): from_below = lax.ppermute(near_up, 'tensor', shift(1))  3.73 us
    ppermute x1, starting transfers between devices, body(): from_above = lax.ppermute(near_down, 'tensor', shift(-1))  3.23 us
  transfers between devices with their start and end apart: 14, of which 8 were waited for; matrix products, arithmetic and copies ran while one was open for 0% of the time, Pallas kernels for 31%

profile of v4, /device:TPU:0, one launch (start us, length us, event | category | flops | bytes accessed | tf_op | source)
XLA Modules:
  0.0 73.2 jit_solution(4074391940700623254)
XLA Ops:
  0.0 0.0 collective-permute-start.1
  0.0 9.7 %attend.1 = (bf16[3,96,512]{2,1,0:T(8,128)(2,1)}, bf16[640,640]{1,0:T(8,128)(2,1)}, s32[96,128]{1,0:T(8,128)}) custom-call(s32[96]{0:T(128)} %lengths.1, s32[1,96]{1,0:T(1,128)} %bitcast.20, s32[1,256]{1,0:T(1,128)} %bitcast.19, bf16[3,96,512]{2,1,0:T(8,128)(2,1)} %q_hbm.1, bf16[3,96,128]{2,1,0:T(8,128)(2,1)} %dk_hbm.1, bf16[3,96,128]{2,1,0:T(8,128)(2,1)} %dv_hbm.1, ...), custom_call_target="tpu_custom_call" | custom-call | flops 301989888 | bytes 12582912 | tf_op jit(solution)/shard_map/attend/pallas_call | solution.py:165
  9.7 0.6 collective-permute-start
  10.3 8.1 %all-to-all-start = ((bf16[16,40,640]{2,1,0:T(8,128)(2,1)}), bf16[16,40,640]{2,1,0:T(8,128)(2,1)S(1)}, u32[]{:S(2)}, u32[]{:S(2)}) async-start(bf16[16,40,640]{2,1,0:T(8,128)(2,1)} %bitcast.18), calls=%async_computation | async-start | bytes 1638400 | tf_op jit(solution)/shard_map/all_to_all | solution.py:437
  18.5 0.0 collective-permute-done.attn_other
  18.5 0.0 copy-start.6
  18.5 0.0 collective-permute-done.1.weight_other
  18.5 0.7 copy-done.6
  19.2 3.5 %project.4 = (bf16[144,1024]{1,0:T(8,128)(2,1)}, bf16[144,1024]{1,0:T(8,128)(2,1)}) custom-call(bf16[288,512]{1,0:T(8,128)(2,1)} %bitcast.15, bf16[288,512]{1,0:T(8,128)(2,1)} %copy-done.6, bf16[512,8192]{1,0:T(8,128)(2,1)} %weight.5, bf16[512,8192]{1,0:T(8,128)(2,1)} %collective-permute-done.1.weight_other), custom_call_target="tpu_custom_call" | custom-call | flops 2415919104 | bytes 8388608 | tf_op jit(solution)/shard_map/project/pallas_call | solution.py:250
  22.7 1.6 %collective-permute-start.2 = (bf16[144,1024]{1,0:T(8,128)(2,1)}, bf16[144,1024]{1,0:T(8,128)(2,1)S(1)}, u32[]{:S(2)}, u32[]{:S(2)}) collective-permute-start(bf16[144,1024]{1,0:T(8,128)(2,1)} %get-tuple-element.31), channel_id=1, source_target_pairs={{0,2},{1,3},{2,4},{3,5},{4,6},{5,7},{6,0},{7,1},{8,10},{9,11},{10,... | collective-permute-start | bytes 884744 | tf_op jit(solution)/shard_map/ppermute | solution.py:444
  24.2 0.0 copy-start.2
  24.2 0.0 copy-start.1
  24.2 1.7 %collective-permute-start.3 = (bf16[144,1024]{1,0:T(8,128)(2,1)}, bf16[144,1024]{1,0:T(8,128)(2,1)S(1)}, u32[]{:S(2)}, u32[]{:S(2)}) collective-permute-start(bf16[144,1024]{1,0:T(8,128)(2,1)} %get-tuple-element.32), channel_id=1, source_target_pairs={{0,6},{1,7},{2,0},{3,1},{4,2},{5,3},{6,4},{7,5},{8,14},{9,15},{10,... | collective-permute-start | bytes 884744 | tf_op jit(solution)/shard_map/ppermute | solution.py:445
  26.0 5.0 %project.3 = (bf16[144,1024]{1,0:T(8,128)(2,1)}, bf16[144,1024]{1,0:T(8,128)(2,1)}, bf16[144,1024]{1,0:T(8,128)(2,1)}, bf16[144,1024]{1,0:T(8,128)(2,1)}) custom-call(bf16[288,512]{1,0:T(8,128)(2,1)} %bitcast.16, bf16[288,512]{1,0:T(8,128)(2,1)} %copy-done.6, bf16[512,8192]{1,0:T(8,128)(2,1)} %weight.5, bf16[512,8192]{1,0:T(8,128)(2,1)} %collective-permute-done.1.weight_other), custom_call_target="tpu_custom_call" | custom-call | flops 4831838208 | bytes 16777216 | tf_op jit(solution)/shard_map/project/pallas_call | solution.py:250
  31.0 0.0 copy-start.3
  31.0 2.5 %all-to-all-done = bf16[16,40,640]{2,1,0:T(8,128)(2,1)S(1)} async-done(((bf16[16,40,640]{2,1,0:T(8,128)(2,1)}), bf16[16,40,640]{2,1,0:T(8,128)(2,1)S(1)}, u32[]{:S(2)}, u32[]{:S(2)}) %all-to-all-start) | async-done | bytes 819232 | tf_op jit(solution)/shard_map/all_to_all | solution.py:437
  33.5 0.0 copy-done.2
  33.6 0.7 down_mix.1
  34.3 0.0 copy-start.4
  34.3 0.0 collective-permute-done.2.far_up
  34.3 0.0 collective-permute-done.3.far_down
  34.3 0.1 collective-permute-start.4
  34.4 1.3 %collective-permute-done.4 = f32[32,640]{1,0:T(8,128)S(1)} collective-permute-done((f32[32,640]{1,0:T(8,128)S(1)}, f32[32,640]{1,0:T(8,128)S(1)}, u32[]{:S(2)}, u32[]{:S(2)}) %collective-permute-start.4) | collective-permute-done | bytes 81952 | tf_op jit(solution)/shard_map/ppermute | solution.py:450
  35.7 2.8 %collective-permute-start.7 = (bf16[32,640]{1,0:T(8,128)(2,1)S(1)}, bf16[32,640]{1,0:T(8,128)(2,1)S(1)}, u32[]{:S(2)}, u32[]{:S(2)}) collective-permute-start(bf16[32,640]{1,0:T(8,128)(2,1)S(1)} %add_convert_fusion.mine), channel_id=1, source_target_pairs={{0,6},{1,7},{2,0},{3,1},{4,2},{5,3},{6,4},{7,5},{8,14},{9,15},{10,... | collective-permute-start | bytes 122888 | tf_op jit(solution)/shard_map/ppermute | solution.py:451
  38.5 0.8 %collective-permute-start.6 = (bf16[32,640]{1,0:T(8,128)(2,1)S(1)}, bf16[32,640]{1,0:T(8,128)(2,1)S(1)}, u32[]{:S(2)}, u32[]{:S(2)}) collective-permute-start(bf16[32,640]{1,0:T(8,128)(2,1)S(1)} %add_convert_fusion.mine), channel_id=1, source_target_pairs={{0,4},{1,5},{2,6},{3,7},{4,0},{5,1},{6,2},{7,3},{8,12},{9,13},{10,... | collective-permute-start | bytes 122888 | tf_op jit(solution)/shard_map/ppermute | solution.py:451
  39.3 0.9 %collective-permute-start.5 = (bf16[32,640]{1,0:T(8,128)(2,1)S(1)}, bf16[32,640]{1,0:T(8,128)(2,1)S(1)}, u32[]{:S(2)}, u32[]{:S(2)}) collective-permute-start(bf16[32,640]{1,0:T(8,128)(2,1)S(1)} %add_convert_fusion.mine), channel_id=1, source_target_pairs={{0,2},{1,3},{2,4},{3,5},{4,6},{5,7},{6,0},{7,1},{8,10},{9,11},{10,... | collective-permute-start | bytes 122888 | tf_op jit(solution)/shard_map/ppermute | solution.py:451
  40.2 0.3 collective-permute-done.7.three
  40.5 3.5 %collective-permute-done.6.two = bf16[32,640]{1,0:T(8,128)(2,1)S(1)} collective-permute-done((bf16[32,640]{1,0:T(8,128)(2,1)S(1)}, bf16[32,640]{1,0:T(8,128)(2,1)S(1)}, u32[]{:S(2)}, u32[]{:S(2)}) %collective-permute-start.6) | collective-permute-done | bytes 40992 | tf_op jit(solution)/shard_map/ppermute | solution.py:451
  44.0 0.5 collective-permute-done.5.one
  44.5 0.0 copy-done.1
  44.5 2.2 %up_terms.1 = bf16[640,1024]{1,0:T(8,128)(2,1)} custom-call(bf16[32,640]{1,0:T(8,128)(2,1)S(1)} %add_convert_fusion.mine, bf16[32,640]{1,0:T(8,128)(2,1)S(1)} %collective-permute-done.5.one, bf16[32,640]{1,0:T(8,128)(2,1)S(1)} %collective-permute-done.6.two, bf16[32,640]{1,0:T(8,128)(2,1)S(1)} %collective-permute-done.7.three, ...), custom_call_target="tpu_custom_call" | custom-call | flops 671088640 | bytes 2359296 | tf_op jit(solution)/shard_map/up_terms/pallas_call | solution.py:348
  46.7 5.5 %all-to-all-start.1 = ((bf16[16,40,1024]{2,1,0:T(8,128)(2,1)}), bf16[16,40,1024]{2,1,0:T(8,128)(2,1)S(1)}, u32[]{:S(2)}, u32[]{:S(2)}) async-start(bf16[16,40,1024]{2,1,0:T(8,128)(2,1)} %bitcast.7), calls=%async_computation.1 | async-start | bytes 2621440 | tf_op jit(solution)/shard_map/all_to_all | solution.py:462
  52.2 0.0 copy-done.3
  52.2 0.0 copy-done.4
  52.2 0.1 merge.1
  52.4 0.3 collective-permute-start.8
  52.6 0.0 copy-start.5
  52.6 3.2 %collective-permute-start.11 = (bf16[144,1024]{1,0:T(8,128)(2,1)S(1)}, bf16[144,1024]{1,0:T(8,128)(2,1)S(1)}, u32[]{:S(2)}, u32[]{:S(2)}) collective-permute-start(bf16[144,1024]{1,0:T(8,128)(2,1)S(1)} %get-tuple-element.46), channel_id=1, source_target_pairs={{0,6},{1,7},{2,0},{3,1},{4,2},{5,3},{6,4},{7,5},{8,14},{9,15},{10,... | collective-permute-start | bytes 884744 | tf_op jit(solution)/shard_map/ppermute | solution.py:460
  55.8 0.0 collective-permute-start.9
  55.9 3.2 %collective-permute-start.10 = (bf16[144,1024]{1,0:T(8,128)(2,1)}, bf16[144,1024]{1,0:T(8,128)(2,1)S(1)}, u32[]{:S(2)}, u32[]{:S(2)}) collective-permute-start(bf16[144,1024]{1,0:T(8,128)(2,1)} %get-tuple-element.45), channel_id=1, source_target_pairs={{0,6},{1,7},{2,0},{3,1},{4,2},{5,3},{6,4},{7,5},{8,14},{9,15},{10,... | collective-permute-start | bytes 884744 | tf_op jit(solution)/shard_map/ppermute | solution.py:457
  59.1 3.5 %project.5.own = bf16[288,1024]{1,0:T(8,128)(2,1)} custom-call(bf16[288,512]{1,0:T(8,128)(2,1)} %bitcast.17, bf16[288,512]{1,0:T(8,128)(2,1)} %copy-done.6, bf16[512,8192]{1,0:T(8,128)(2,1)} %weight.5, bf16[512,8192]{1,0:T(8,128)(2,1)} %collective-permute-done.1.weight_other), custom_call_target="tpu_custom_call" | custom-call | flops 2415919104 | bytes 8388608 | tf_op jit(solution)/shard_map/project/pallas_call | solution.py:250
  62.6 1.2 %collective-permute-done.8.refs_0_ = bf16[144,1024]{1,0:T(8,128)(2,1)S(1)} collective-permute-done((bf16[144,1024]{1,0:T(8,128)(2,1)S(1)}, bf16[144,1024]{1,0:T(8,128)(2,1)S(1)}, u32[]{:S(2)}, u32[]{:S(2)}) %collective-permute-start.8) | collective-permute-done | bytes 294944 | tf_op jit(solution)/shard_map/ppermute | solution.py:459
  63.8 0.0 collective-permute-done.11.refs_3_
  63.8 3.7 %collective-permute-done.9.refs_1_ = bf16[144,1024]{1,0:T(8,128)(2,1)S(1)} collective-permute-done((bf16[144,1024]{1,0:T(8,128)(2,1)}, bf16[144,1024]{1,0:T(8,128)(2,1)S(1)}, u32[]{:S(2)}, u32[]{:S(2)}) %collective-permute-start.9) | collective-permute-done | bytes 294944 | tf_op jit(solution)/shard_map/ppermute | solution.py:456
  67.5 0.0 collective-permute-done.10.refs_2_
  67.5 0.0 copy-start
  67.5 1.1 %copy-done = bf16[288,1024]{1,0:T(8,128)(2,1)S(1)} copy-done((bf16[288,1024]{1,0:T(8,128)(2,1)S(1)}, bf16[288,1024]{1,0:T(8,128)(2,1)}, u32[]{:S(2)}) %copy-start) | copy-done | bytes 589848
  68.6 0.2 gather_base.1.base
  68.8 2.7 %all-to-all-done.1 = bf16[16,40,1024]{2,1,0:T(8,128)(2,1)S(1)} async-done(((bf16[16,40,1024]{2,1,0:T(8,128)(2,1)}), bf16[16,40,1024]{2,1,0:T(8,128)(2,1)S(1)}, u32[]{:S(2)}, u32[]{:S(2)}) %all-to-all-start.1) | async-done | bytes 1310752 | tf_op jit(solution)/shard_map/all_to_all | solution.py:462
  71.5 0.0 copy-done.5
  71.5 1.7 %finish.1 = bf16[3,96,1024]{2,1,0:T(8,128)(2,1)} custom-call(f32[288,1024]{1,0:T(8,128)S(1)} %gather_base.1.base, bf16[640,1024]{1,0:T(8,128)(2,1)S(1)} %bitcast.11, s32[96,128]{1,0:T(8,128)S(1)} %copy-done.5), custom_call_target="tpu_custom_call" | custom-call | flops 377487360 | bytes 1310720 | tf_op jit(solution)/shard_map/finish/pallas_call | solution.py:397
  (1 shorter events, 0.0 us)
Async XLA Ops:
  0.0 18.5 %collective-permute-start.1 = (bf16[512,8192]{1,0:T(8,128)(2,1)}, bf16[512,8192]{1,0:T(8,128)(2,1)}, u32[]{:S(2)}, u32[]{:S(2)}) collective-permute-start(bf16[512,8192]{1,0:T(8,128)(2,1)} %weight.5), channel_id=1, source_target_pairs={{0,1},{1,0},{2,3},{3,2},{4,5},{5,4},{6,7},{7,6},{8,9},{9,8},{10,11... | collective-permute-start | bytes 25165832 | tf_op jit(solution)/shard_map/ppermute | solution.py:432
  9.7 8.7 %collective-permute-start = (bf16[288,512]{1,0:T(8,128)(2,1)}, bf16[288,512]{1,0:T(8,128)(2,1)S(1)}, u32[]{:S(2)}, u32[]{:S(2)}) collective-permute-start(bf16[288,512]{1,0:T(8,128)(2,1)} %bitcast.14), channel_id=1, source_target_pairs={{0,1},{1,0},{2,3},{3,2},{4,5},{5,4},{6,7},{7,6},{8,9},{9,8},{10,11... | collective-permute-start | bytes 884744 | tf_op jit(solution)/shard_map/ppermute | solution.py:441
  10.3 23.2 %all-to-all-start = ((bf16[16,40,640]{2,1,0:T(8,128)(2,1)}), bf16[16,40,640]{2,1,0:T(8,128)(2,1)S(1)}, u32[]{:S(2)}, u32[]{:S(2)}) async-start(bf16[16,40,640]{2,1,0:T(8,128)(2,1)} %bitcast.18), calls=%async_computation | async-start | bytes 1638400 | tf_op jit(solution)/shard_map/all_to_all | solution.py:437
  18.5 0.7 copy-start.6
  22.7 11.6 %collective-permute-start.2 = (bf16[144,1024]{1,0:T(8,128)(2,1)}, bf16[144,1024]{1,0:T(8,128)(2,1)S(1)}, u32[]{:S(2)}, u32[]{:S(2)}) collective-permute-start(bf16[144,1024]{1,0:T(8,128)(2,1)} %get-tuple-element.31), channel_id=1, source_target_pairs={{0,2},{1,3},{2,4},{3,5},{4,6},{5,7},{6,0},{7,1},{8,10},{9,11},{10,... | collective-permute-start | bytes 884744 | tf_op jit(solution)/shard_map/ppermute | solution.py:444
  24.2 9.3 %copy-start.2 = (bf16[16,32,512]{2,1,0:T(8,128)(2,1)S(1)}, bf16[16,32,512]{2,1,0:T(8,128)(2,1)}, u32[]{:S(2)}) copy-start(bf16[16,32,512]{2,1,0:T(8,128)(2,1)} %param.20) | copy-start | bytes 1572868
  24.2 20.3 %copy-start.1 = (bf16[16,32,1024]{2,1,0:T(8,128)(2,1)S(1)}, bf16[16,32,1024]{2,1,0:T(8,128)(2,1)}, u32[]{:S(2)}) copy-start(bf16[16,32,1024]{2,1,0:T(8,128)(2,1)} %param.21) | copy-start | bytes 3145732
  24.2 10.1 %collective-permute-start.3 = (bf16[144,1024]{1,0:T(8,128)(2,1)}, bf16[144,1024]{1,0:T(8,128)(2,1)S(1)}, u32[]{:S(2)}, u32[]{:S(2)}) collective-permute-start(bf16[144,1024]{1,0:T(8,128)(2,1)} %get-tuple-element.32), channel_id=1, source_target_pairs={{0,6},{1,7},{2,0},{3,1},{4,2},{5,3},{6,4},{7,5},{8,14},{9,15},{10,... | collective-permute-start | bytes 884744 | tf_op jit(solution)/shard_map/ppermute | solution.py:445
  31.0 21.2 %copy-start.3 = (bf16[144,1024]{1,0:T(8,128)(2,1)S(1)}, bf16[144,1024]{1,0:T(8,128)(2,1)}, u32[]{:S(2)}) copy-start(bf16[144,1024]{1,0:T(8,128)(2,1)} %get-tuple-element.39.up) | copy-start | bytes 884740
  34.3 17.9 %copy-start.4 = (bf16[144,1024]{1,0:T(8,128)(2,1)S(1)}, bf16[144,1024]{1,0:T(8,128)(2,1)}, u32[]{:S(2)}) copy-start(bf16[144,1024]{1,0:T(8,128)(2,1)} %get-tuple-element.40.down) | copy-start | bytes 884740
  34.3 1.4 %collective-permute-start.4 = (f32[32,640]{1,0:T(8,128)S(1)}, f32[32,640]{1,0:T(8,128)S(1)}, u32[]{:S(2)}, u32[]{:S(2)}) collective-permute-start(f32[32,640]{1,0:T(8,128)S(1)} %down_mix.1), channel_id=1, source_target_pairs={{0,1},{1,0},{2,3},{3,2},{4,5},{5,4},{6,7},{7,6},{8,9},{9,8},{10,11... | collective-permute-start | bytes 245768 | tf_op jit(solution)/shard_map/ppermute | solution.py:450
  35.7 4.8 %collective-permute-start.7 = (bf16[32,640]{1,0:T(8,128)(2,1)S(1)}, bf16[32,640]{1,0:T(8,128)(2,1)S(1)}, u32[]{:S(2)}, u32[]{:S(2)}) collective-permute-start(bf16[32,640]{1,0:T(8,128)(2,1)S(1)} %add_convert_fusion.mine), channel_id=1, source_target_pairs={{0,6},{1,7},{2,0},{3,1},{4,2},{5,3},{6,4},{7,5},{8,14},{9,15},{10,... | collective-permute-start | bytes 122888 | tf_op jit(solution)/shard_map/ppermute | solution.py:451
  38.5 5.5 %collective-permute-start.6 = (bf16[32,640]{1,0:T(8,128)(2,1)S(1)}, bf16[32,640]{1,0:T(8,128)(2,1)S(1)}, u32[]{:S(2)}, u32[]{:S(2)}) collective-permute-start(bf16[32,640]{1,0:T(8,128)(2,1)S(1)} %add_convert_fusion.mine), channel_id=1, source_target_pairs={{0,4},{1,5},{2,6},{3,7},{4,0},{5,1},{6,2},{7,3},{8,12},{9,13},{10,... | collective-permute-start | bytes 122888 | tf_op jit(solution)/shard_map/ppermute | solution.py:451
  39.3 5.2 %collective-permute-start.5 = (bf16[32,640]{1,0:T(8,128)(2,1)S(1)}, bf16[32,640]{1,0:T(8,128)(2,1)S(1)}, u32[]{:S(2)}, u32[]{:S(2)}) collective-permute-start(bf16[32,640]{1,0:T(8,128)(2,1)S(1)} %add_convert_fusion.mine), channel_id=1, source_target_pairs={{0,2},{1,3},{2,4},{3,5},{4,6},{5,7},{6,0},{7,1},{8,10},{9,11},{10,... | collective-permute-start | bytes 122888 | tf_op jit(solution)/shard_map/ppermute | solution.py:451
  46.7 24.8 %all-to-all-start.1 = ((bf16[16,40,1024]{2,1,0:T(8,128)(2,1)}), bf16[16,40,1024]{2,1,0:T(8,128)(2,1)S(1)}, u32[]{:S(2)}, u32[]{:S(2)}) async-start(bf16[16,40,1024]{2,1,0:T(8,128)(2,1)} %bitcast.7), calls=%async_computation.1 | async-start | bytes 2621440 | tf_op jit(solution)/shard_map/all_to_all | solution.py:462
  52.4 11.4 %collective-permute-start.8 = (bf16[144,1024]{1,0:T(8,128)(2,1)S(1)}, bf16[144,1024]{1,0:T(8,128)(2,1)S(1)}, u32[]{:S(2)}, u32[]{:S(2)}) collective-permute-start(bf16[144,1024]{1,0:T(8,128)(2,1)S(1)} %get-tuple-element.43), channel_id=1, source_target_pairs={{0,2},{1,3},{2,4},{3,5},{4,6},{5,7},{6,0},{7,1},{8,10},{9,11},{10,... | collective-permute-start | bytes 884744 | tf_op jit(solution)/shard_map/ppermute | solution.py:459
  52.6 18.9 %copy-start.5 = (s32[96,128]{1,0:T(8,128)S(1)}, s32[96,128]{1,0:T(8,128)}, u32[]{:S(2)}) copy-start(s32[96,128]{1,0:T(8,128)} %get-tuple-element.48.dest) | copy-start | bytes 147460
  52.6 11.1 %collective-permute-start.11 = (bf16[144,1024]{1,0:T(8,128)(2,1)S(1)}, bf16[144,1024]{1,0:T(8,128)(2,1)S(1)}, u32[]{:S(2)}, u32[]{:S(2)}) collective-permute-start(bf16[144,1024]{1,0:T(8,128)(2,1)S(1)} %get-tuple-element.46), channel_id=1, source_target_pairs={{0,6},{1,7},{2,0},{3,1},{4,2},{5,3},{6,4},{7,5},{8,14},{9,15},{10,... | collective-permute-start | bytes 884744 | tf_op jit(solution)/shard_map/ppermute | solution.py:460
  55.8 11.7 %collective-permute-start.9 = (bf16[144,1024]{1,0:T(8,128)(2,1)}, bf16[144,1024]{1,0:T(8,128)(2,1)S(1)}, u32[]{:S(2)}, u32[]{:S(2)}) collective-permute-start(bf16[144,1024]{1,0:T(8,128)(2,1)} %get-tuple-element.44), channel_id=1, source_target_pairs={{0,2},{1,3},{2,4},{3,5},{4,6},{5,7},{6,0},{7,1},{8,10},{9,11},{10,... | collective-permute-start | bytes 884744 | tf_op jit(solution)/shard_map/ppermute | solution.py:456
  55.9 11.7 %collective-permute-start.10 = (bf16[144,1024]{1,0:T(8,128)(2,1)}, bf16[144,1024]{1,0:T(8,128)(2,1)S(1)}, u32[]{:S(2)}, u32[]{:S(2)}) collective-permute-start(bf16[144,1024]{1,0:T(8,128)(2,1)} %get-tuple-element.45), channel_id=1, source_target_pairs={{0,6},{1,7},{2,0},{3,1},{4,2},{5,3},{6,4},{7,5},{8,14},{9,15},{10,... | collective-permute-start | bytes 884744 | tf_op jit(solution)/shard_map/ppermute | solution.py:457
  67.5 1.1 %copy-start = (bf16[288,1024]{1,0:T(8,128)(2,1)S(1)}, bf16[288,1024]{1,0:T(8,128)(2,1)}, u32[]{:S(2)}) copy-start(bf16[288,1024]{1,0:T(8,128)(2,1)} %project.5.own) | copy-start | bytes 1769476

commit v5 on v4

--- a/solution.py
+++ b/solution.py
@@ -74,7 +74,8 @@
         orow, ocol = prow // span, pcol // span
         rank = jnp.sum(jnp.where((ocol == orow) & (a < b), 1.0, 0.0), axis=0, keepdims=True).astype(jnp.int32)
         rank_col = jnp.sum(jnp.where((ocol == orow) & (b < a), 1.0, 0.0), axis=1, keepdims=True).astype(jnp.int32)
-        dest_out[...] = jnp.broadcast_to(ocol * owner_rows + rank_col, dest_out.shape)
+        last = payload.shape[0] // owner_rows - 1
+        dest_out[...] = jnp.broadcast_to((last - ocol) * owner_rows + rank_col, dest_out.shape)
         dest = orow * owner_rows + rank
         local = jnp.broadcast_to((pcol - ocol * span).astype(jnp.float32), (count, LANES)).astype(jnp.bfloat16)
         return dest, local
@@ -315,7 +316,7 @@
     )(arrived, down.reshape(span * rank, width))
 
 
-def up_kernel(mine, one, two, three, arrived, up, out):
+def up_kernel(owner_rows, mine, one, two, three, arrived, up, out):
     rank = mine.shape[0]
     spread_width = up.shape[0]
     mix = (
@@ -336,17 +337,17 @@
         lane = lax.broadcasted_iota(jnp.int32, meta.shape, 1) + j * LANES
         same = meta == (lane // rank).astype(jnp.float32)
         pieces.append(jnp.where(same, spread[:, j * LANES:(j + 1) * LANES], 0.0).astype(jnp.bfloat16))
-    out[...] = jnp.dot(
-        jnp.concatenate(pieces, axis=1), up[...], preferred_element_type=jnp.float32
-    ).astype(jnp.bfloat16)
-
-
-def up_terms(mixes, arrived, up):
+    terms = jnp.dot(jnp.concatenate(pieces, axis=1), up[...], preferred_element_type=jnp.float32)
+    blocks = [terms[at:at + owner_rows] for at in range(0, terms.shape[0], owner_rows)]
+    out[...] = jnp.concatenate(blocks[::-1], axis=0).astype(jnp.bfloat16)
+
+
+def up_terms(mixes, arrived, up, owner_rows):
     rows, full = arrived.shape
     span, rank, width = up.shape
     mix_spec = pl.BlockSpec((rank, rows), lambda i: (0, 0))
     return pl.pallas_call(
-        up_kernel,
+        functools.partial(up_kernel, owner_rows),
         grid=(1,),
         in_specs=[mix_spec] * 4
         + [
@@ -361,22 +362,26 @@
     )(*mixes, arrived, up.reshape(span * rank, width))
 
 
+def widen_kernel(own, out):
+    out[...] = own[...].astype(jnp.float32)
+
+
 def gather_kernel(own, *refs):
     parts, out = refs[:4], refs[4]
     half = parts[0].shape[0]
     for n in range(2):
         here = slice(n * half, (n + 1) * half)
         a, b = parts[n::2]
-        out[here] = own[here].astype(jnp.float32) + a[...].astype(jnp.float32) + b[...].astype(jnp.float32)
+        out[here] = own[here] + a[...].astype(jnp.float32) + b[...].astype(jnp.float32)
 
 
 def gather_base(own, parts):
     return pl.pallas_call(
-        gather_kernel,
+        gather_kernel if parts else widen_kernel,
         out_shape=jax.ShapeDtypeStruct(own.shape, jnp.float32),
         compiler_params=pltpu.CompilerParams(vmem_limit_bytes=VMEM // 4),
         cost_estimate=pl.CostEstimate(flops=0, bytes_accessed=10 * own.size, transcendentals=0),
-        name="gather_base",
+        name="gather_base" if parts else "widen",
     )(own, *parts)
 
 
@@ -449,7 +454,7 @@
     mine, far_up, far_down = lax.optimization_barrier((mine, far_up, far_down))
     pair = (mine + lax.ppermute(mine, "tensor", swap)).astype(jnp.bfloat16)
     mixes = [pair] + [lax.ppermute(pair, "tensor", shift(k)) for k in range(1, chips)]
-    terms = up_terms(mixes, arrived, adapter_up)
+    terms = up_terms(mixes, arrived, adapter_up, owner_rows)
     terms, up, down, near_up, near_down, attn = lax.optimization_barrier(
         (terms, up, down, near_up, near_down, attn)
     )
@@ -460,9 +465,10 @@
     down = lax.ppermute(down, "tensor", shift(-1))
     (own,) = project(attn, attn_other, *weights, 3, 1, cuts=1)
     terms = lax.all_to_all(
-        terms.reshape(owners, owner_rows, -1), "dp", 0, 0, tiled=True
+        terms.reshape(owners, owner_rows, -1), "dp", 0, 0, tiled=True,
+        axis_index_groups=[list(range(owners))[::-1]],
     ).reshape(owners * owner_rows, -1)
-    base = gather_base(own, (up, from_below, from_above, down))
+    base = gather_base(gather_base(own, ()), (up, from_below, from_above, down))
     return finish(base, terms, dest, drafts, slots)
 
 

time: 73.6 us -> 71.5 us (0.971)
  waiting for transfers between devices: 15.8 us -> 12 us
  starting transfers between devices: 28.8 us -> 30.5 us
    all_to_all x1, waiting for transfers between devices: 2.74 us -> 0.13 us  [body(): lax.all_to_all(terms.reshape(owners, owner_rows, -1), 'dp', 0, 0, tiled=T...]
    all_to_all x1, starting transfers between devices: 5.5 us -> 7.19 us  [body(): lax.all_to_all(terms.reshape(owners, owner_rows, -1), 'dp', 0, 0, tiled=T...]
    ppermute x1, waiting for transfers between devices: 1.21 us -> 0.06 us  [body(): up = lax.ppermute(up, 'tensor', shift(1))]
    pallas_call x2 -> x3, Pallas kernels: 2.35 us -> 2.39 us  [the longest x1 2.15 us: up_terms(): pl.pallas_call(functools.partial(up_kernel, owner_rows), grid=(1,), in_sp...]
  transfers between devices with their start and end apart: 14 -> 14, of which waited for: 8 -> 8; matrix products, arithmetic and copies ran while one was open for 0% -> 0% of each run, Pallas kernels for 31% -> 32%
where the time goes in v5:
time: 71.5 us; the launch traced here: 71.1 us
  starting transfers between devices  30.5 us (43%)
  Pallas kernels  26.6 us (37%)
  waiting for transfers between devices  12 us (17%)
  local copies, waits for them, and re-layouts  1.79 us (3%)
    pallas_call x3, Pallas kernels, project(): pl.pallas_call(functools.partial(project_kernel, first, cuts), in_specs=[...  12 us
    pallas_call x1, Pallas kernels, attend(): pl.pallas_call(functools.partial(attend_kernel, slots, owner_rows, span),...  9.72 us
    all_to_all x1, starting transfers between devices, body(): lax.all_to_all(payload.reshape(owners, owner_rows, -1), 'dp', 0, 0, tiled...  8.13 us
    all_to_all x1, starting transfers between devices, body(): lax.all_to_all(terms.reshape(owners, owner_rows, -1), 'dp', 0, 0, tiled=T...  7.19 us
    ppermute x3, starting transfers between devices, body(): lax.ppermute(pair, 'tensor', shift(k))  4.52 us
    ppermute x3, waiting for transfers between devices, body(): lax.ppermute(pair, 'tensor', shift(k))  4.32 us
    ppermute x1, waiting for transfers between devices, body(): from_below = lax.ppermute(near_up, 'tensor', shift(1))  3.66 us
    ppermute x1, starting transfers between devices, body(): from_above = lax.ppermute(near_down, 'tensor', shift(-1))  3.23 us
  transfers between devices with their start and end apart: 14, of which 8 were waited for; matrix products, arithmetic and copies ran while one was open for 0% of the time, Pallas kernels for 32%

profile of v5, /device:TPU:0, one launch (start us, length us, event | category | flops | bytes accessed | tf_op | source)
XLA Modules:
  0.0 71.1 jit_solution(5916707304094808548)
XLA Ops:
  0.0 0.0 collective-permute-start.1
  0.0 9.7 %attend.1 = (bf16[3,96,512]{2,1,0:T(8,128)(2,1)}, bf16[640,640]{1,0:T(8,128)(2,1)}, s32[96,128]{1,0:T(8,128)}) custom-call(s32[96]{0:T(128)} %lengths.1, s32[1,96]{1,0:T(1,128)} %bitcast.20, s32[1,256]{1,0:T(1,128)} %bitcast.19, bf16[3,96,512]{2,1,0:T(8,128)(2,1)} %q_hbm.1, bf16[3,96,128]{2,1,0:T(8,128)(2,1)} %dk_hbm.1, bf16[3,96,128]{2,1,0:T(8,128)(2,1)} %dv_hbm.1, ...), custom_call_target="tpu_custom_call" | custom-call | flops 301989888 | bytes 12582912 | tf_op jit(solution)/shard_map/attend/pallas_call | solution.py:166
  9.7 0.6 collective-permute-start
  10.3 8.1 %all-to-all-start = ((bf16[16,40,640]{2,1,0:T(8,128)(2,1)}), bf16[16,40,640]{2,1,0:T(8,128)(2,1)S(1)}, u32[]{:S(2)}, u32[]{:S(2)}) async-start(bf16[16,40,640]{2,1,0:T(8,128)(2,1)} %bitcast.18), calls=%async_computation | async-start | bytes 1638400 | tf_op jit(solution)/shard_map/all_to_all | solution.py:442
  18.5 0.0 collective-permute-done.attn_other
  18.5 0.0 copy-start.6
  18.5 0.0 collective-permute-done.1.weight_other
  18.5 0.7 copy-done.6
  19.2 3.5 %project.4 = (bf16[144,1024]{1,0:T(8,128)(2,1)}, bf16[144,1024]{1,0:T(8,128)(2,1)}) custom-call(bf16[288,512]{1,0:T(8,128)(2,1)} %bitcast.15, bf16[288,512]{1,0:T(8,128)(2,1)} %copy-done.6, bf16[512,8192]{1,0:T(8,128)(2,1)} %weight.5, bf16[512,8192]{1,0:T(8,128)(2,1)} %collective-permute-done.1.weight_other), custom_call_target="tpu_custom_call" | custom-call | flops 2415919104 | bytes 8388608 | tf_op jit(solution)/shard_map/project/pallas_call | solution.py:251
  22.7 1.6 %collective-permute-start.2 = (bf16[144,1024]{1,0:T(8,128)(2,1)}, bf16[144,1024]{1,0:T(8,128)(2,1)S(1)}, u32[]{:S(2)}, u32[]{:S(2)}) collective-permute-start(bf16[144,1024]{1,0:T(8,128)(2,1)} %get-tuple-element.31), channel_id=1, source_target_pairs={{0,2},{1,3},{2,4},{3,5},{4,6},{5,7},{6,0},{7,1},{8,10},{9,11},{10,... | collective-permute-start | bytes 884744 | tf_op jit(solution)/shard_map/ppermute | solution.py:449
  24.2 0.0 copy-start.2
  24.2 0.0 copy-start.1
  24.2 1.7 %collective-permute-start.3 = (bf16[144,1024]{1,0:T(8,128)(2,1)}, bf16[144,1024]{1,0:T(8,128)(2,1)S(1)}, u32[]{:S(2)}, u32[]{:S(2)}) collective-permute-start(bf16[144,1024]{1,0:T(8,128)(2,1)} %get-tuple-element.32), channel_id=1, source_target_pairs={{0,6},{1,7},{2,0},{3,1},{4,2},{5,3},{6,4},{7,5},{8,14},{9,15},{10,... | collective-permute-start | bytes 884744 | tf_op jit(solution)/shard_map/ppermute | solution.py:450
  26.0 5.0 %project.3 = (bf16[144,1024]{1,0:T(8,128)(2,1)}, bf16[144,1024]{1,0:T(8,128)(2,1)}, bf16[144,1024]{1,0:T(8,128)(2,1)}, bf16[144,1024]{1,0:T(8,128)(2,1)}) custom-call(bf16[288,512]{1,0:T(8,128)(2,1)} %bitcast.16, bf16[288,512]{1,0:T(8,128)(2,1)} %copy-done.6, bf16[512,8192]{1,0:T(8,128)(2,1)} %weight.5, bf16[512,8192]{1,0:T(8,128)(2,1)} %collective-permute-done.1.weight_other), custom_call_target="tpu_custom_call" | custom-call | flops 4831838208 | bytes 16777216 | tf_op jit(solution)/shard_map/project/pallas_call | solution.py:251
  31.0 0.0 copy-start.3
  31.0 2.5 %all-to-all-done = bf16[16,40,640]{2,1,0:T(8,128)(2,1)S(1)} async-done(((bf16[16,40,640]{2,1,0:T(8,128)(2,1)}), bf16[16,40,640]{2,1,0:T(8,128)(2,1)S(1)}, u32[]{:S(2)}, u32[]{:S(2)}) %all-to-all-start) | async-done | bytes 819232 | tf_op jit(solution)/shard_map/all_to_all | solution.py:442
  33.5 0.0 copy-done.2
  33.6 0.7 %down_mix.1 = f32[32,640]{1,0:T(8,128)S(1)} custom-call(bf16[640,640]{1,0:T(8,128)(2,1)S(1)} %bitcast.9, bf16[512,512]{1,0:T(8,128)(2,1)S(1)} %bitcast.13), custom_call_target="tpu_custom_call" | custom-call | flops 335544320 | bytes 1343488 | tf_op jit(solution)/shard_map/down_mix/pallas_call | solution.py:310
  34.3 0.0 copy-start.4
  34.3 0.0 collective-permute-done.2.far_up
  34.3 0.0 collective-permute-done.3.far_down
  34.3 0.1 collective-permute-start.4
  34.4 1.3 %collective-permute-done.4 = f32[32,640]{1,0:T(8,128)S(1)} collective-permute-done((f32[32,640]{1,0:T(8,128)S(1)}, f32[32,640]{1,0:T(8,128)S(1)}, u32[]{:S(2)}, u32[]{:S(2)}) %collective-permute-start.4) | collective-permute-done | bytes 81952 | tf_op jit(solution)/shard_map/ppermute | solution.py:455
  35.7 2.8 %collective-permute-start.7 = (bf16[32,640]{1,0:T(8,128)(2,1)S(1)}, bf16[32,640]{1,0:T(8,128)(2,1)S(1)}, u32[]{:S(2)}, u32[]{:S(2)}) collective-permute-start(bf16[32,640]{1,0:T(8,128)(2,1)S(1)} %add_convert_fusion.mine), channel_id=1, source_target_pairs={{0,6},{1,7},{2,0},{3,1},{4,2},{5,3},{6,4},{7,5},{8,14},{9,15},{10,... | collective-permute-start | bytes 122888 | tf_op jit(solution)/shard_map/ppermute | solution.py:456
  38.5 0.8 %collective-permute-start.6 = (bf16[32,640]{1,0:T(8,128)(2,1)S(1)}, bf16[32,640]{1,0:T(8,128)(2,1)S(1)}, u32[]{:S(2)}, u32[]{:S(2)}) collective-permute-start(bf16[32,640]{1,0:T(8,128)(2,1)S(1)} %add_convert_fusion.mine), channel_id=1, source_target_pairs={{0,4},{1,5},{2,6},{3,7},{4,0},{5,1},{6,2},{7,3},{8,12},{9,13},{10,... | collective-permute-start | bytes 122888 | tf_op jit(solution)/shard_map/ppermute | solution.py:456
  39.3 0.9 %collective-permute-start.5 = (bf16[32,640]{1,0:T(8,128)(2,1)S(1)}, bf16[32,640]{1,0:T(8,128)(2,1)S(1)}, u32[]{:S(2)}, u32[]{:S(2)}) collective-permute-start(bf16[32,640]{1,0:T(8,128)(2,1)S(1)} %add_convert_fusion.mine), channel_id=1, source_target_pairs={{0,2},{1,3},{2,4},{3,5},{4,6},{5,7},{6,0},{7,1},{8,10},{9,11},{10,... | collective-permute-start | bytes 122888 | tf_op jit(solution)/shard_map/ppermute | solution.py:456
  40.2 0.3 collective-permute-done.7.three
  40.5 3.5 %collective-permute-done.6.two = bf16[32,640]{1,0:T(8,128)(2,1)S(1)} collective-permute-done((bf16[32,640]{1,0:T(8,128)(2,1)S(1)}, bf16[32,640]{1,0:T(8,128)(2,1)S(1)}, u32[]{:S(2)}, u32[]{:S(2)}) %collective-permute-start.6) | collective-permute-done | bytes 40992 | tf_op jit(solution)/shard_map/ppermute | solution.py:456
  44.0 0.5 collective-permute-done.5.one
  44.5 0.0 copy-done.1
  44.5 2.2 %up_terms.1 = bf16[640,1024]{1,0:T(8,128)(2,1)} custom-call(bf16[32,640]{1,0:T(8,128)(2,1)S(1)} %add_convert_fusion.mine, bf16[32,640]{1,0:T(8,128)(2,1)S(1)} %collective-permute-done.5.one, bf16[32,640]{1,0:T(8,128)(2,1)S(1)} %collective-permute-done.6.two, bf16[32,640]{1,0:T(8,128)(2,1)S(1)} %collective-permute-done.7.three, ...), custom_call_target="tpu_custom_call" | custom-call | flops 671088640 | bytes 2359296 | tf_op jit(solution)/shard_map/up_terms/pallas_call | solution.py:349
  46.7 7.2 %all-to-all-start.1 = ((bf16[16,40,1024]{2,1,0:T(8,128)(2,1)}), bf16[16,40,1024]{2,1,0:T(8,128)(2,1)S(1)}, u32[]{:S(2)}, u32[]{:S(2)}) async-start(bf16[16,40,1024]{2,1,0:T(8,128)(2,1)} %bitcast.7), calls=%async_computation.1 | async-start | bytes 2621440 | tf_op jit(solution)/shard_map/all_to_all | solution.py:467
  53.9 0.0 copy-done.3
  53.9 0.0 copy-done.4
  53.9 0.1 merge.1
  54.0 0.3 collective-permute-start.8
  54.3 0.0 copy-start.5
  54.3 3.2 %collective-permute-start.11 = (bf16[144,1024]{1,0:T(8,128)(2,1)S(1)}, bf16[144,1024]{1,0:T(8,128)(2,1)S(1)}, u32[]{:S(2)}, u32[]{:S(2)}) collective-permute-start(bf16[144,1024]{1,0:T(8,128)(2,1)S(1)} %get-tuple-element.46), channel_id=1, source_target_pairs={{0,6},{1,7},{2,0},{3,1},{4,2},{5,3},{6,4},{7,5},{8,14},{9,15},{10,... | collective-permute-start | bytes 884744 | tf_op jit(solution)/shard_map/ppermute | solution.py:465
  57.5 0.0 collective-permute-start.9
  57.5 3.2 %collective-permute-start.10 = (bf16[144,1024]{1,0:T(8,128)(2,1)}, bf16[144,1024]{1,0:T(8,128)(2,1)S(1)}, u32[]{:S(2)}, u32[]{:S(2)}) collective-permute-start(bf16[144,1024]{1,0:T(8,128)(2,1)} %get-tuple-element.45), channel_id=1, source_target_pairs={{0,6},{1,7},{2,0},{3,1},{4,2},{5,3},{6,4},{7,5},{8,14},{9,15},{10,... | collective-permute-start | bytes 884744 | tf_op jit(solution)/shard_map/ppermute | solution.py:462
  60.8 3.5 %project.5.own = bf16[288,1024]{1,0:T(8,128)(2,1)} custom-call(bf16[288,512]{1,0:T(8,128)(2,1)} %bitcast.17, bf16[288,512]{1,0:T(8,128)(2,1)} %copy-done.6, bf16[512,8192]{1,0:T(8,128)(2,1)} %weight.5, bf16[512,8192]{1,0:T(8,128)(2,1)} %collective-permute-done.1.weight_other), custom_call_target="tpu_custom_call" | custom-call | flops 2415919104 | bytes 8388608 | tf_op jit(solution)/shard_map/project/pallas_call | solution.py:251
  64.2 0.0 copy-start
  64.2 1.1 %copy-done = bf16[288,1024]{1,0:T(8,128)(2,1)S(1)} copy-done((bf16[288,1024]{1,0:T(8,128)(2,1)S(1)}, bf16[288,1024]{1,0:T(8,128)(2,1)}, u32[]{:S(2)}) %copy-start) | copy-done | bytes 589848
  65.3 0.1 widen.1.own
  65.4 0.1 collective-permute-done.8.refs_0_
  65.4 0.0 collective-permute-done.11.refs_3_
  65.4 3.7 %collective-permute-done.9.refs_1_ = bf16[144,1024]{1,0:T(8,128)(2,1)S(1)} collective-permute-done((bf16[144,1024]{1,0:T(8,128)(2,1)}, bf16[144,1024]{1,0:T(8,128)(2,1)S(1)}, u32[]{:S(2)}, u32[]{:S(2)}) %collective-permute-start.9) | collective-permute-done | bytes 294944 | tf_op jit(solution)/shard_map/ppermute | solution.py:461
  69.1 0.0 collective-permute-done.10.refs_2_
  69.1 0.2 gather_base.1.base
  69.3 0.1 all-to-all-done.1
  69.4 0.0 copy-done.5
  69.4 1.7 %finish.1 = bf16[3,96,1024]{2,1,0:T(8,128)(2,1)} custom-call(f32[288,1024]{1,0:T(8,128)S(1)} %gather_base.1.base, bf16[640,1024]{1,0:T(8,128)(2,1)S(1)} %bitcast.11, s32[96,128]{1,0:T(8,128)S(1)} %copy-done.5), custom_call_target="tpu_custom_call" | custom-call | flops 377487360 | bytes 1310720 | tf_op jit(solution)/shard_map/finish/pallas_call | solution.py:402
  (1 shorter events, 0.0 us)
Async XLA Ops:
  0.0 18.5 %collective-permute-start.1 = (bf16[512,8192]{1,0:T(8,128)(2,1)}, bf16[512,8192]{1,0:T(8,128)(2,1)}, u32[]{:S(2)}, u32[]{:S(2)}) collective-permute-start(bf16[512,8192]{1,0:T(8,128)(2,1)} %weight.5), channel_id=1, source_target_pairs={{0,1},{1,0},{2,3},{3,2},{4,5},{5,4},{6,7},{7,6},{8,9},{9,8},{10,11... | collective-permute-start | bytes 25165832 | tf_op jit(solution)/shard_map/ppermute | solution.py:437
  9.7 8.7 %collective-permute-start = (bf16[288,512]{1,0:T(8,128)(2,1)}, bf16[288,512]{1,0:T(8,128)(2,1)S(1)}, u32[]{:S(2)}, u32[]{:S(2)}) collective-permute-start(bf16[288,512]{1,0:T(8,128)(2,1)} %bitcast.14), channel_id=1, source_target_pairs={{0,1},{1,0},{2,3},{3,2},{4,5},{5,4},{6,7},{7,6},{8,9},{9,8},{10,11... | collective-permute-start | bytes 884744 | tf_op jit(solution)/shard_map/ppermute | solution.py:446
  10.3 23.2 %all-to-all-start = ((bf16[16,40,640]{2,1,0:T(8,128)(2,1)}), bf16[16,40,640]{2,1,0:T(8,128)(2,1)S(1)}, u32[]{:S(2)}, u32[]{:S(2)}) async-start(bf16[16,40,640]{2,1,0:T(8,128)(2,1)} %bitcast.18), calls=%async_computation | async-start | bytes 1638400 | tf_op jit(solution)/shard_map/all_to_all | solution.py:442
  18.5 0.7 %copy-start.6 = (bf16[288,512]{1,0:T(8,128)(2,1)}, bf16[288,512]{1,0:T(8,128)(2,1)S(1)}, u32[]{:S(2)}) copy-start(bf16[288,512]{1,0:T(8,128)(2,1)S(1)} %collective-permute-done.attn_other) | copy-start | bytes 884740
  22.7 11.6 %collective-permute-start.2 = (bf16[144,1024]{1,0:T(8,128)(2,1)}, bf16[144,1024]{1,0:T(8,128)(2,1)S(1)}, u32[]{:S(2)}, u32[]{:S(2)}) collective-permute-start(bf16[144,1024]{1,0:T(8,128)(2,1)} %get-tuple-element.31), channel_id=1, source_target_pairs={{0,2},{1,3},{2,4},{3,5},{4,6},{5,7},{6,0},{7,1},{8,10},{9,11},{10,... | collective-permute-start | bytes 884744 | tf_op jit(solution)/shard_map/ppermute | solution.py:449
  24.2 9.3 %copy-start.2 = (bf16[16,32,512]{2,1,0:T(8,128)(2,1)S(1)}, bf16[16,32,512]{2,1,0:T(8,128)(2,1)}, u32[]{:S(2)}) copy-start(bf16[16,32,512]{2,1,0:T(8,128)(2,1)} %param.20) | copy-start | bytes 1572868
  24.2 20.3 %copy-start.1 = (bf16[16,32,1024]{2,1,0:T(8,128)(2,1)S(1)}, bf16[16,32,1024]{2,1,0:T(8,128)(2,1)}, u32[]{:S(2)}) copy-start(bf16[16,32,1024]{2,1,0:T(8,128)(2,1)} %param.21) | copy-start | bytes 3145732
  24.2 10.1 %collective-permute-start.3 = (bf16[144,1024]{1,0:T(8,128)(2,1)}, bf16[144,1024]{1,0:T(8,128)(2,1)S(1)}, u32[]{:S(2)}, u32[]{:S(2)}) collective-permute-start(bf16[144,1024]{1,0:T(8,128)(2,1)} %get-tuple-element.32), channel_id=1, source_target_pairs={{0,6},{1,7},{2,0},{3,1},{4,2},{5,3},{6,4},{7,5},{8,14},{9,15},{10,... | collective-permute-start | bytes 884744 | tf_op jit(solution)/shard_map/ppermute | solution.py:450
  31.0 22.8 %copy-start.3 = (bf16[144,1024]{1,0:T(8,128)(2,1)S(1)}, bf16[144,1024]{1,0:T(8,128)(2,1)}, u32[]{:S(2)}) copy-start(bf16[144,1024]{1,0:T(8,128)(2,1)} %get-tuple-element.39.up) | copy-start | bytes 884740
  34.3 19.6 %copy-start.4 = (bf16[144,1024]{1,0:T(8,128)(2,1)S(1)}, bf16[144,1024]{1,0:T(8,128)(2,1)}, u32[]{:S(2)}) copy-start(bf16[144,1024]{1,0:T(8,128)(2,1)} %get-tuple-element.40.down) | copy-start | bytes 884740
  34.3 1.4 %collective-permute-start.4 = (f32[32,640]{1,0:T(8,128)S(1)}, f32[32,640]{1,0:T(8,128)S(1)}, u32[]{:S(2)}, u32[]{:S(2)}) collective-permute-start(f32[32,640]{1,0:T(8,128)S(1)} %down_mix.1), channel_id=1, source_target_pairs={{0,1},{1,0},{2,3},{3,2},{4,5},{5,4},{6,7},{7,6},{8,9},{9,8},{10,11... | collective-permute-start | bytes 245768 | tf_op jit(solution)/shard_map/ppermute | solution.py:455
  35.7 4.8 %collective-permute-start.7 = (bf16[32,640]{1,0:T(8,128)(2,1)S(1)}, bf16[32,640]{1,0:T(8,128)(2,1)S(1)}, u32[]{:S(2)}, u32[]{:S(2)}) collective-permute-start(bf16[32,640]{1,0:T(8,128)(2,1)S(1)} %add_convert_fusion.mine), channel_id=1, source_target_pairs={{0,6},{1,7},{2,0},{3,1},{4,2},{5,3},{6,4},{7,5},{8,14},{9,15},{10,... | collective-permute-start | bytes 122888 | tf_op jit(solution)/shard_map/ppermute | solution.py:456
  38.5 5.5 %collective-permute-start.6 = (bf16[32,640]{1,0:T(8,128)(2,1)S(1)}, bf16[32,640]{1,0:T(8,128)(2,1)S(1)}, u32[]{:S(2)}, u32[]{:S(2)}) collective-permute-start(bf16[32,640]{1,0:T(8,128)(2,1)S(1)} %add_convert_fusion.mine), channel_id=1, source_target_pairs={{0,4},{1,5},{2,6},{3,7},{4,0},{5,1},{6,2},{7,3},{8,12},{9,13},{10,... | collective-permute-start | bytes 122888 | tf_op jit(solution)/shard_map/ppermute | solution.py:456
  39.3 5.2 %collective-permute-start.5 = (bf16[32,640]{1,0:T(8,128)(2,1)S(1)}, bf16[32,640]{1,0:T(8,128)(2,1)S(1)}, u32[]{:S(2)}, u32[]{:S(2)}) collective-permute-start(bf16[32,640]{1,0:T(8,128)(2,1)S(1)} %add_convert_fusion.mine), channel_id=1, source_target_pairs={{0,2},{1,3},{2,4},{3,5},{4,6},{5,7},{6,0},{7,1},{8,10},{9,11},{10,... | collective-permute-start | bytes 122888 | tf_op jit(solution)/shard_map/ppermute | solution.py:456
  46.7 22.7 %all-to-all-start.1 = ((bf16[16,40,1024]{2,1,0:T(8,128)(2,1)}), bf16[16,40,1024]{2,1,0:T(8,128)(2,1)S(1)}, u32[]{:S(2)}, u32[]{:S(2)}) async-start(bf16[16,40,1024]{2,1,0:T(8,128)(2,1)} %bitcast.7), calls=%async_computation.1 | async-start | bytes 2621440 | tf_op jit(solution)/shard_map/all_to_all | solution.py:467
  54.0 11.4 %collective-permute-start.8 = (bf16[144,1024]{1,0:T(8,128)(2,1)S(1)}, bf16[144,1024]{1,0:T(8,128)(2,1)S(1)}, u32[]{:S(2)}, u32[]{:S(2)}) collective-permute-start(bf16[144,1024]{1,0:T(8,128)(2,1)S(1)} %get-tuple-element.43), channel_id=1, source_target_pairs={{0,2},{1,3},{2,4},{3,5},{4,6},{5,7},{6,0},{7,1},{8,10},{9,11},{10,... | collective-permute-start | bytes 884744 | tf_op jit(solution)/shard_map/ppermute | solution.py:464
  54.3 15.1 %copy-start.5 = (s32[96,128]{1,0:T(8,128)S(1)}, s32[96,128]{1,0:T(8,128)}, u32[]{:S(2)}) copy-start(s32[96,128]{1,0:T(8,128)} %get-tuple-element.48.dest) | copy-start | bytes 147460
  54.3 11.1 %collective-permute-start.11 = (bf16[144,1024]{1,0:T(8,128)(2,1)S(1)}, bf16[144,1024]{1,0:T(8,128)(2,1)S(1)}, u32[]{:S(2)}, u32[]{:S(2)}) collective-permute-start(bf16[144,1024]{1,0:T(8,128)(2,1)S(1)} %get-tuple-element.46), channel_id=1, source_target_pairs={{0,6},{1,7},{2,0},{3,1},{4,2},{5,3},{6,4},{7,5},{8,14},{9,15},{10,... | collective-permute-start | bytes 884744 | tf_op jit(solution)/shard_map/ppermute | solution.py:465
  57.5 11.6 %collective-permute-start.9 = (bf16[144,1024]{1,0:T(8,128)(2,1)}, bf16[144,1024]{1,0:T(8,128)(2,1)S(1)}, u32[]{:S(2)}, u32[]{:S(2)}) collective-permute-start(bf16[144,1024]{1,0:T(8,128)(2,1)} %get-tuple-element.44), channel_id=1, source_target_pairs={{0,2},{1,3},{2,4},{3,5},{4,6},{5,7},{6,0},{7,1},{8,10},{9,11},{10,... | collective-permute-start | bytes 884744 | tf_op jit(solution)/shard_map/ppermute | solution.py:461
  57.5 11.6 %collective-permute-start.10 = (bf16[144,1024]{1,0:T(8,128)(2,1)}, bf16[144,1024]{1,0:T(8,128)(2,1)S(1)}, u32[]{:S(2)}, u32[]{:S(2)}) collective-permute-start(bf16[144,1024]{1,0:T(8,128)(2,1)} %get-tuple-element.45), channel_id=1, source_target_pairs={{0,6},{1,7},{2,0},{3,1},{4,2},{5,3},{6,4},{7,5},{8,14},{9,15},{10,... | collective-permute-start | bytes 884744 | tf_op jit(solution)/shard_map/ppermute | solution.py:462
  64.2 1.1 %copy-start = (bf16[288,1024]{1,0:T(8,128)(2,1)S(1)}, bf16[288,1024]{1,0:T(8,128)(2,1)}, u32[]{:S(2)}) copy-start(bf16[288,1024]{1,0:T(8,128)(2,1)} %project.5.own) | copy-start | bytes 1769476

commit v6 on v5

--- a/solution.py
+++ b/solution.py
@@ -453,7 +453,7 @@
     mine = down_mix(arrived, adapter_down)
     mine, far_up, far_down = lax.optimization_barrier((mine, far_up, far_down))
     pair = (mine + lax.ppermute(mine, "tensor", swap)).astype(jnp.bfloat16)
-    mixes = [pair] + [lax.ppermute(pair, "tensor", shift(k)) for k in range(1, chips)]
+    mixes = [pair] + [lax.ppermute(pair, "tensor", shift(k)) for k in range(chips - 1, 0, -1)]
     terms = up_terms(mixes, arrived, adapter_up, owner_rows)
     terms, up, down, near_up, near_down, attn = lax.optimization_barrier(
         (terms, up, down, near_up, near_down, attn)

time: 71.5 us -> 71 us (level)
  waiting for transfers between devices: 12 us -> 10.2 us
  starting transfers between devices: 30.5 us -> 31.8 us
    ppermute x3, waiting for transfers between devices: 4.32 us -> 2.56 us  [body(): lax.ppermute(pair, 'tensor', shift(k))]
    ppermute x3, starting transfers between devices: 4.52 us -> 5.73 us  [body(): lax.ppermute(pair, 'tensor', shift(k))]
  transfers between devices with their start and end apart: 14 -> 14, of which waited for: 8 -> 7; matrix products, arithmetic and copies ran while one was open for 0% -> 0% of each run, Pallas kernels for 32% -> 32%
where the time goes in v6:
time: 71 us; the launch traced here: 70.6 us
  starting transfers between devices  31.8 us (45%)
  Pallas kernels  26.6 us (37%)
  waiting for transfers between devices  10.2 us (14%)
  local copies, waits for them, and re-layouts  1.79 us (3%)
    pallas_call x3, Pallas kernels, project(): pl.pallas_call(functools.partial(project_kernel, first, cuts), in_specs=[...  12 us
    pallas_call x1, Pallas kernels, attend(): pl.pallas_call(functools.partial(attend_kernel, slots, owner_rows, span),...  9.72 us
    all_to_all x1, starting transfers between devices, body(): lax.all_to_all(payload.reshape(owners, owner_rows, -1), 'dp', 0, 0, tiled...  8.13 us
    all_to_all x1, starting transfers between devices, body(): lax.all_to_all(terms.reshape(owners, owner_rows, -1), 'dp', 0, 0, tiled=T...  7.25 us
    ppermute x3, starting transfers between devices, body(): lax.ppermute(pair, 'tensor', shift(k))  5.73 us
    ppermute x1, waiting for transfers between devices, body(): from_below = lax.ppermute(near_up, 'tensor', shift(1))  3.63 us
    ppermute x1, starting transfers between devices, body(): from_above = lax.ppermute(near_down, 'tensor', shift(-1))  3.23 us
    ppermute x1, starting transfers between devices, body(): down = lax.ppermute(down, 'tensor', shift(-1))  3.12 us
  transfers between devices with their start and end apart: 14, of which 7 were waited for; matrix products, arithmetic and copies ran while one was open for 0% of the time, Pallas kernels for 32%

profile of v6, /device:TPU:0, one launch (start us, length us, event | category | flops | bytes accessed | tf_op | source)
XLA Modules:
  0.0 70.6 jit_solution(17769847657310669309)
XLA Ops:
  0.0 0.0 collective-permute-start.1
  0.0 9.7 %attend.1 = (bf16[3,96,512]{2,1,0:T(8,128)(2,1)}, bf16[640,640]{1,0:T(8,128)(2,1)}, s32[96,128]{1,0:T(8,128)}) custom-call(s32[96]{0:T(128)} %lengths.1, s32[1,96]{1,0:T(1,128)} %bitcast.20, s32[1,256]{1,0:T(1,128)} %bitcast.19, bf16[3,96,512]{2,1,0:T(8,128)(2,1)} %q_hbm.1, bf16[3,96,128]{2,1,0:T(8,128)(2,1)} %dk_hbm.1, bf16[3,96,128]{2,1,0:T(8,128)(2,1)} %dv_hbm.1, ...), custom_call_target="tpu_custom_call" | custom-call | flops 301989888 | bytes 12582912 | tf_op jit(solution)/shard_map/attend/pallas_call | solution.py:166
  9.7 0.6 collective-permute-start
  10.3 8.1 %all-to-all-start = ((bf16[16,40,640]{2,1,0:T(8,128)(2,1)}), bf16[16,40,640]{2,1,0:T(8,128)(2,1)S(1)}, u32[]{:S(2)}, u32[]{:S(2)}) async-start(bf16[16,40,640]{2,1,0:T(8,128)(2,1)} %bitcast.18), calls=%async_computation | async-start | bytes 1638400 | tf_op jit(solution)/shard_map/all_to_all | solution.py:442
  18.5 0.0 collective-permute-done.attn_other
  18.5 0.0 copy-start.6
  18.5 0.0 collective-permute-done.1.weight_other
  18.5 0.7 copy-done.6
  19.2 3.5 %project.4 = (bf16[144,1024]{1,0:T(8,128)(2,1)}, bf16[144,1024]{1,0:T(8,128)(2,1)}) custom-call(bf16[288,512]{1,0:T(8,128)(2,1)} %bitcast.15, bf16[288,512]{1,0:T(8,128)(2,1)} %copy-done.6, bf16[512,8192]{1,0:T(8,128)(2,1)} %weight.5, bf16[512,8192]{1,0:T(8,128)(2,1)} %collective-permute-done.1.weight_other), custom_call_target="tpu_custom_call" | custom-call | flops 2415919104 | bytes 8388608 | tf_op jit(solution)/shard_map/project/pallas_call | solution.py:251
  22.7 1.6 %collective-permute-start.2 = (bf16[144,1024]{1,0:T(8,128)(2,1)}, bf16[144,1024]{1,0:T(8,128)(2,1)S(1)}, u32[]{:S(2)}, u32[]{:S(2)}) collective-permute-start(bf16[144,1024]{1,0:T(8,128)(2,1)} %get-tuple-element.31), channel_id=1, source_target_pairs={{0,2},{1,3},{2,4},{3,5},{4,6},{5,7},{6,0},{7,1},{8,10},{9,11},{10,... | collective-permute-start | bytes 884744 | tf_op jit(solution)/shard_map/ppermute | solution.py:449
  24.2 0.0 copy-start.2
  24.2 0.0 copy-start.1
  24.2 1.7 %collective-permute-start.3 = (bf16[144,1024]{1,0:T(8,128)(2,1)}, bf16[144,1024]{1,0:T(8,128)(2,1)S(1)}, u32[]{:S(2)}, u32[]{:S(2)}) collective-permute-start(bf16[144,1024]{1,0:T(8,128)(2,1)} %get-tuple-element.32), channel_id=1, source_target_pairs={{0,6},{1,7},{2,0},{3,1},{4,2},{5,3},{6,4},{7,5},{8,14},{9,15},{10,... | collective-permute-start | bytes 884744 | tf_op jit(solution)/shard_map/ppermute | solution.py:450
  26.0 5.0 %project.3 = (bf16[144,1024]{1,0:T(8,128)(2,1)}, bf16[144,1024]{1,0:T(8,128)(2,1)}, bf16[144,1024]{1,0:T(8,128)(2,1)}, bf16[144,1024]{1,0:T(8,128)(2,1)}) custom-call(bf16[288,512]{1,0:T(8,128)(2,1)} %bitcast.16, bf16[288,512]{1,0:T(8,128)(2,1)} %copy-done.6, bf16[512,8192]{1,0:T(8,128)(2,1)} %weight.5, bf16[512,8192]{1,0:T(8,128)(2,1)} %collective-permute-done.1.weight_other), custom_call_target="tpu_custom_call" | custom-call | flops 4831838208 | bytes 16777216 | tf_op jit(solution)/shard_map/project/pallas_call | solution.py:251
  31.0 0.0 copy-start.3
  31.0 2.5 %all-to-all-done = bf16[16,40,640]{2,1,0:T(8,128)(2,1)S(1)} async-done(((bf16[16,40,640]{2,1,0:T(8,128)(2,1)}), bf16[16,40,640]{2,1,0:T(8,128)(2,1)S(1)}, u32[]{:S(2)}, u32[]{:S(2)}) %all-to-all-start) | async-done | bytes 819232 | tf_op jit(solution)/shard_map/all_to_all | solution.py:442
  33.5 0.0 copy-done.2
  33.6 0.7 %down_mix.1 = f32[32,640]{1,0:T(8,128)S(1)} custom-call(bf16[640,640]{1,0:T(8,128)(2,1)S(1)} %bitcast.9, bf16[512,512]{1,0:T(8,128)(2,1)S(1)} %bitcast.13), custom_call_target="tpu_custom_call" | custom-call | flops 335544320 | bytes 1343488 | tf_op jit(solution)/shard_map/down_mix/pallas_call | solution.py:310
  34.3 0.0 copy-start.4
  34.3 0.0 collective-permute-done.2.far_up
  34.3 0.0 collective-permute-done.3.far_down
  34.3 0.1 collective-permute-start.4
  34.4 1.3 %collective-permute-done.4 = f32[32,640]{1,0:T(8,128)S(1)} collective-permute-done((f32[32,640]{1,0:T(8,128)S(1)}, f32[32,640]{1,0:T(8,128)S(1)}, u32[]{:S(2)}, u32[]{:S(2)}) %collective-permute-start.4) | collective-permute-done | bytes 81952 | tf_op jit(solution)/shard_map/ppermute | solution.py:455
  35.7 1.6 %collective-permute-start.7 = (bf16[32,640]{1,0:T(8,128)(2,1)S(1)}, bf16[32,640]{1,0:T(8,128)(2,1)S(1)}, u32[]{:S(2)}, u32[]{:S(2)}) collective-permute-start(bf16[32,640]{1,0:T(8,128)(2,1)S(1)} %add_convert_fusion.mine), channel_id=1, source_target_pairs={{0,2},{1,3},{2,4},{3,5},{4,6},{5,7},{6,0},{7,1},{8,10},{9,11},{10,... | collective-permute-start | bytes 122888 | tf_op jit(solution)/shard_map/ppermute | solution.py:456
  37.2 2.7 %collective-permute-start.6 = (bf16[32,640]{1,0:T(8,128)(2,1)S(1)}, bf16[32,640]{1,0:T(8,128)(2,1)S(1)}, u32[]{:S(2)}, u32[]{:S(2)}) collective-permute-start(bf16[32,640]{1,0:T(8,128)(2,1)S(1)} %add_convert_fusion.mine), channel_id=1, source_target_pairs={{0,4},{1,5},{2,6},{3,7},{4,0},{5,1},{6,2},{7,3},{8,12},{9,13},{10,... | collective-permute-start | bytes 122888 | tf_op jit(solution)/shard_map/ppermute | solution.py:456
  40.0 1.4 %collective-permute-start.5 = (bf16[32,640]{1,0:T(8,128)(2,1)S(1)}, bf16[32,640]{1,0:T(8,128)(2,1)S(1)}, u32[]{:S(2)}, u32[]{:S(2)}) collective-permute-start(bf16[32,640]{1,0:T(8,128)(2,1)S(1)} %add_convert_fusion.mine), channel_id=1, source_target_pairs={{0,6},{1,7},{2,0},{3,1},{4,2},{5,3},{6,4},{7,5},{8,14},{9,15},{10,... | collective-permute-start | bytes 122888 | tf_op jit(solution)/shard_map/ppermute | solution.py:456
  41.4 0.0 collective-permute-done.7.three
  41.4 1.3 %collective-permute-done.6.two = bf16[32,640]{1,0:T(8,128)(2,1)S(1)} collective-permute-done((bf16[32,640]{1,0:T(8,128)(2,1)S(1)}, bf16[32,640]{1,0:T(8,128)(2,1)S(1)}, u32[]{:S(2)}, u32[]{:S(2)}) %collective-permute-start.6) | collective-permute-done | bytes 40992 | tf_op jit(solution)/shard_map/ppermute | solution.py:456
  42.7 1.2 %collective-permute-done.5.one = bf16[32,640]{1,0:T(8,128)(2,1)S(1)} collective-permute-done((bf16[32,640]{1,0:T(8,128)(2,1)S(1)}, bf16[32,640]{1,0:T(8,128)(2,1)S(1)}, u32[]{:S(2)}, u32[]{:S(2)}) %collective-permute-start.5) | collective-permute-done | bytes 40992 | tf_op jit(solution)/shard_map/ppermute | solution.py:456
  44.0 0.0 copy-done.1
  44.0 2.2 %up_terms.1 = bf16[640,1024]{1,0:T(8,128)(2,1)} custom-call(bf16[32,640]{1,0:T(8,128)(2,1)S(1)} %add_convert_fusion.mine, bf16[32,640]{1,0:T(8,128)(2,1)S(1)} %collective-permute-done.5.one, bf16[32,640]{1,0:T(8,128)(2,1)S(1)} %collective-permute-done.6.two, bf16[32,640]{1,0:T(8,128)(2,1)S(1)} %collective-permute-done.7.three, ...), custom_call_target="tpu_custom_call" | custom-call | flops 671088640 | bytes 2359296 | tf_op jit(solution)/shard_map/up_terms/pallas_call | solution.py:349
  46.1 7.3 %all-to-all-start.1 = ((bf16[16,40,1024]{2,1,0:T(8,128)(2,1)}), bf16[16,40,1024]{2,1,0:T(8,128)(2,1)S(1)}, u32[]{:S(2)}, u32[]{:S(2)}) async-start(bf16[16,40,1024]{2,1,0:T(8,128)(2,1)} %bitcast.7), calls=%async_computation.1 | async-start | bytes 2621440 | tf_op jit(solution)/shard_map/all_to_all | solution.py:467
  53.4 0.0 copy-done.3
  53.4 0.0 copy-done.4
  53.4 0.1 merge.1
  53.6 0.4 collective-permute-start.8
  53.9 0.0 copy-start.5
  53.9 3.1 %collective-permute-start.11 = (bf16[144,1024]{1,0:T(8,128)(2,1)S(1)}, bf16[144,1024]{1,0:T(8,128)(2,1)S(1)}, u32[]{:S(2)}, u32[]{:S(2)}) collective-permute-start(bf16[144,1024]{1,0:T(8,128)(2,1)S(1)} %get-tuple-element.46), channel_id=1, source_target_pairs={{0,6},{1,7},{2,0},{3,1},{4,2},{5,3},{6,4},{7,5},{8,14},{9,15},{10,... | collective-permute-start | bytes 884744 | tf_op jit(solution)/shard_map/ppermute | solution.py:465
  57.0 0.0 collective-permute-start.9
  57.0 3.2 %collective-permute-start.10 = (bf16[144,1024]{1,0:T(8,128)(2,1)}, bf16[144,1024]{1,0:T(8,128)(2,1)S(1)}, u32[]{:S(2)}, u32[]{:S(2)}) collective-permute-start(bf16[144,1024]{1,0:T(8,128)(2,1)} %get-tuple-element.45), channel_id=1, source_target_pairs={{0,6},{1,7},{2,0},{3,1},{4,2},{5,3},{6,4},{7,5},{8,14},{9,15},{10,... | collective-permute-start | bytes 884744 | tf_op jit(solution)/shard_map/ppermute | solution.py:462
  60.3 3.5 %project.5.own = bf16[288,1024]{1,0:T(8,128)(2,1)} custom-call(bf16[288,512]{1,0:T(8,128)(2,1)} %bitcast.17, bf16[288,512]{1,0:T(8,128)(2,1)} %copy-done.6, bf16[512,8192]{1,0:T(8,128)(2,1)} %weight.5, bf16[512,8192]{1,0:T(8,128)(2,1)} %collective-permute-done.1.weight_other), custom_call_target="tpu_custom_call" | custom-call | flops 2415919104 | bytes 8388608 | tf_op jit(solution)/shard_map/project/pallas_call | solution.py:251
  63.8 0.0 copy-start
  63.8 1.1 %copy-done = bf16[288,1024]{1,0:T(8,128)(2,1)S(1)} copy-done((bf16[288,1024]{1,0:T(8,128)(2,1)S(1)}, bf16[288,1024]{1,0:T(8,128)(2,1)}, u32[]{:S(2)}) %copy-start) | copy-done | bytes 589848
  64.8 0.1 widen.1.own
  64.9 0.1 collective-permute-done.8.refs_0_
  65.0 0.0 collective-permute-done.11.refs_3_
  65.0 3.6 %collective-permute-done.9.refs_1_ = bf16[144,1024]{1,0:T(8,128)(2,1)S(1)} collective-permute-done((bf16[144,1024]{1,0:T(8,128)(2,1)}, bf16[144,1024]{1,0:T(8,128)(2,1)S(1)}, u32[]{:S(2)}, u32[]{:S(2)}) %collective-permute-start.9) | collective-permute-done | bytes 294944 | tf_op jit(solution)/shard_map/ppermute | solution.py:461
  68.6 0.0 collective-permute-done.10.refs_2_
  68.6 0.2 gather_base.1.base
  68.8 0.1 all-to-all-done.1
  68.9 0.0 copy-done.5
  68.9 1.7 %finish.1 = bf16[3,96,1024]{2,1,0:T(8,128)(2,1)} custom-call(f32[288,1024]{1,0:T(8,128)S(1)} %gather_base.1.base, bf16[640,1024]{1,0:T(8,128)(2,1)S(1)} %bitcast.11, s32[96,128]{1,0:T(8,128)S(1)} %copy-done.5), custom_call_target="tpu_custom_call" | custom-call | flops 377487360 | bytes 1310720 | tf_op jit(solution)/shard_map/finish/pallas_call | solution.py:402
  (1 shorter events, 0.0 us)
Async XLA Ops:
  0.0 18.5 %collective-permute-start.1 = (bf16[512,8192]{1,0:T(8,128)(2,1)}, bf16[512,8192]{1,0:T(8,128)(2,1)}, u32[]{:S(2)}, u32[]{:S(2)}) collective-permute-start(bf16[512,8192]{1,0:T(8,128)(2,1)} %weight.5), channel_id=1, source_target_pairs={{0,1},{1,0},{2,3},{3,2},{4,5},{5,4},{6,7},{7,6},{8,9},{9,8},{10,11... | collective-permute-start | bytes 25165832 | tf_op jit(solution)/shard_map/ppermute | solution.py:437
  9.7 8.7 %collective-permute-start = (bf16[288,512]{1,0:T(8,128)(2,1)}, bf16[288,512]{1,0:T(8,128)(2,1)S(1)}, u32[]{:S(2)}, u32[]{:S(2)}) collective-permute-start(bf16[288,512]{1,0:T(8,128)(2,1)} %bitcast.14), channel_id=1, source_target_pairs={{0,1},{1,0},{2,3},{3,2},{4,5},{5,4},{6,7},{7,6},{8,9},{9,8},{10,11... | collective-permute-start | bytes 884744 | tf_op jit(solution)/shard_map/ppermute | solution.py:446
  10.3 23.2 %all-to-all-start = ((bf16[16,40,640]{2,1,0:T(8,128)(2,1)}), bf16[16,40,640]{2,1,0:T(8,128)(2,1)S(1)}, u32[]{:S(2)}, u32[]{:S(2)}) async-start(bf16[16,40,640]{2,1,0:T(8,128)(2,1)} %bitcast.18), calls=%async_computation | async-start | bytes 1638400 | tf_op jit(solution)/shard_map/all_to_all | solution.py:442
  18.5 0.7 %copy-start.6 = (bf16[288,512]{1,0:T(8,128)(2,1)}, bf16[288,512]{1,0:T(8,128)(2,1)S(1)}, u32[]{:S(2)}) copy-start(bf16[288,512]{1,0:T(8,128)(2,1)S(1)} %collective-permute-done.attn_other) | copy-start | bytes 884740
  22.7 11.6 %collective-permute-start.2 = (bf16[144,1024]{1,0:T(8,128)(2,1)}, bf16[144,1024]{1,0:T(8,128)(2,1)S(1)}, u32[]{:S(2)}, u32[]{:S(2)}) collective-permute-start(bf16[144,1024]{1,0:T(8,128)(2,1)} %get-tuple-element.31), channel_id=1, source_target_pairs={{0,2},{1,3},{2,4},{3,5},{4,6},{5,7},{6,0},{7,1},{8,10},{9,11},{10,... | collective-permute-start | bytes 884744 | tf_op jit(solution)/shard_map/ppermute | solution.py:449
  24.2 9.3 %copy-start.2 = (bf16[16,32,512]{2,1,0:T(8,128)(2,1)S(1)}, bf16[16,32,512]{2,1,0:T(8,128)(2,1)}, u32[]{:S(2)}) copy-start(bf16[16,32,512]{2,1,0:T(8,128)(2,1)} %param.20) | copy-start | bytes 1572868
  24.2 19.7 %copy-start.1 = (bf16[16,32,1024]{2,1,0:T(8,128)(2,1)S(1)}, bf16[16,32,1024]{2,1,0:T(8,128)(2,1)}, u32[]{:S(2)}) copy-start(bf16[16,32,1024]{2,1,0:T(8,128)(2,1)} %param.21) | copy-start | bytes 3145732
  24.2 10.1 %collective-permute-start.3 = (bf16[144,1024]{1,0:T(8,128)(2,1)}, bf16[144,1024]{1,0:T(8,128)(2,1)S(1)}, u32[]{:S(2)}, u32[]{:S(2)}) collective-permute-start(bf16[144,1024]{1,0:T(8,128)(2,1)} %get-tuple-element.32), channel_id=1, source_target_pairs={{0,6},{1,7},{2,0},{3,1},{4,2},{5,3},{6,4},{7,5},{8,14},{9,15},{10,... | collective-permute-start | bytes 884744 | tf_op jit(solution)/shard_map/ppermute | solution.py:450
  31.0 22.4 %copy-start.3 = (bf16[144,1024]{1,0:T(8,128)(2,1)S(1)}, bf16[144,1024]{1,0:T(8,128)(2,1)}, u32[]{:S(2)}) copy-start(bf16[144,1024]{1,0:T(8,128)(2,1)} %get-tuple-element.39.up) | copy-start | bytes 884740
  34.3 19.1 %copy-start.4 = (bf16[144,1024]{1,0:T(8,128)(2,1)S(1)}, bf16[144,1024]{1,0:T(8,128)(2,1)}, u32[]{:S(2)}) copy-start(bf16[144,1024]{1,0:T(8,128)(2,1)} %get-tuple-element.40.down) | copy-start | bytes 884740
  34.3 1.4 %collective-permute-start.4 = (f32[32,640]{1,0:T(8,128)S(1)}, f32[32,640]{1,0:T(8,128)S(1)}, u32[]{:S(2)}, u32[]{:S(2)}) collective-permute-start(f32[32,640]{1,0:T(8,128)S(1)} %down_mix.1), channel_id=1, source_target_pairs={{0,1},{1,0},{2,3},{3,2},{4,5},{5,4},{6,7},{7,6},{8,9},{9,8},{10,11... | collective-permute-start | bytes 245768 | tf_op jit(solution)/shard_map/ppermute | solution.py:455
  35.7 5.7 %collective-permute-start.7 = (bf16[32,640]{1,0:T(8,128)(2,1)S(1)}, bf16[32,640]{1,0:T(8,128)(2,1)S(1)}, u32[]{:S(2)}, u32[]{:S(2)}) collective-permute-start(bf16[32,640]{1,0:T(8,128)(2,1)S(1)} %add_convert_fusion.mine), channel_id=1, source_target_pairs={{0,2},{1,3},{2,4},{3,5},{4,6},{5,7},{6,0},{7,1},{8,10},{9,11},{10,... | collective-permute-start | bytes 122888 | tf_op jit(solution)/shard_map/ppermute | solution.py:456
  37.2 5.5 %collective-permute-start.6 = (bf16[32,640]{1,0:T(8,128)(2,1)S(1)}, bf16[32,640]{1,0:T(8,128)(2,1)S(1)}, u32[]{:S(2)}, u32[]{:S(2)}) collective-permute-start(bf16[32,640]{1,0:T(8,128)(2,1)S(1)} %add_convert_fusion.mine), channel_id=1, source_target_pairs={{0,4},{1,5},{2,6},{3,7},{4,0},{5,1},{6,2},{7,3},{8,12},{9,13},{10,... | collective-permute-start | bytes 122888 | tf_op jit(solution)/shard_map/ppermute | solution.py:456
  40.0 4.0 %collective-permute-start.5 = (bf16[32,640]{1,0:T(8,128)(2,1)S(1)}, bf16[32,640]{1,0:T(8,128)(2,1)S(1)}, u32[]{:S(2)}, u32[]{:S(2)}) collective-permute-start(bf16[32,640]{1,0:T(8,128)(2,1)S(1)} %add_convert_fusion.mine), channel_id=1, source_target_pairs={{0,6},{1,7},{2,0},{3,1},{4,2},{5,3},{6,4},{7,5},{8,14},{9,15},{10,... | collective-permute-start | bytes 122888 | tf_op jit(solution)/shard_map/ppermute | solution.py:456
  46.1 22.7 %all-to-all-start.1 = ((bf16[16,40,1024]{2,1,0:T(8,128)(2,1)}), bf16[16,40,1024]{2,1,0:T(8,128)(2,1)S(1)}, u32[]{:S(2)}, u32[]{:S(2)}) async-start(bf16[16,40,1024]{2,1,0:T(8,128)(2,1)} %bitcast.7), calls=%async_computation.1 | async-start | bytes 2621440 | tf_op jit(solution)/shard_map/all_to_all | solution.py:467
  53.6 11.4 %collective-permute-start.8 = (bf16[144,1024]{1,0:T(8,128)(2,1)S(1)}, bf16[144,1024]{1,0:T(8,128)(2,1)S(1)}, u32[]{:S(2)}, u32[]{:S(2)}) collective-permute-start(bf16[144,1024]{1,0:T(8,128)(2,1)S(1)} %get-tuple-element.43), channel_id=1, source_target_pairs={{0,2},{1,3},{2,4},{3,5},{4,6},{5,7},{6,0},{7,1},{8,10},{9,11},{10,... | collective-permute-start | bytes 884744 | tf_op jit(solution)/shard_map/ppermute | solution.py:464
  53.9 15.0 %copy-start.5 = (s32[96,128]{1,0:T(8,128)S(1)}, s32[96,128]{1,0:T(8,128)}, u32[]{:S(2)}) copy-start(s32[96,128]{1,0:T(8,128)} %get-tuple-element.48.dest) | copy-start | bytes 147460
  53.9 11.0 %collective-permute-start.11 = (bf16[144,1024]{1,0:T(8,128)(2,1)S(1)}, bf16[144,1024]{1,0:T(8,128)(2,1)S(1)}, u32[]{:S(2)}, u32[]{:S(2)}) collective-permute-start(bf16[144,1024]{1,0:T(8,128)(2,1)S(1)} %get-tuple-element.46), channel_id=1, source_target_pairs={{0,6},{1,7},{2,0},{3,1},{4,2},{5,3},{6,4},{7,5},{8,14},{9,15},{10,... | collective-permute-start | bytes 884744 | tf_op jit(solution)/shard_map/ppermute | solution.py:465
  57.0 11.6 %collective-permute-start.9 = (bf16[144,1024]{1,0:T(8,128)(2,1)}, bf16[144,1024]{1,0:T(8,128)(2,1)S(1)}, u32[]{:S(2)}, u32[]{:S(2)}) collective-permute-start(bf16[144,1024]{1,0:T(8,128)(2,1)} %get-tuple-element.44), channel_id=1, source_target_pairs={{0,2},{1,3},{2,4},{3,5},{4,6},{5,7},{6,0},{7,1},{8,10},{9,11},{10,... | collective-permute-start | bytes 884744 | tf_op jit(solution)/shard_map/ppermute | solution.py:461
  57.0 11.6 %collective-permute-start.10 = (bf16[144,1024]{1,0:T(8,128)(2,1)}, bf16[144,1024]{1,0:T(8,128)(2,1)S(1)}, u32[]{:S(2)}, u32[]{:S(2)}) collective-permute-start(bf16[144,1024]{1,0:T(8,128)(2,1)} %get-tuple-element.45), channel_id=1, source_target_pairs={{0,6},{1,7},{2,0},{3,1},{4,2},{5,3},{6,4},{7,5},{8,14},{9,15},{10,... | collective-permute-start | bytes 884744 | tf_op jit(solution)/shard_map/ppermute | solution.py:462
  63.8 1.1 %copy-start = (bf16[288,1024]{1,0:T(8,128)(2,1)S(1)}, bf16[288,1024]{1,0:T(8,128)(2,1)}, u32[]{:S(2)}) copy-start(bf16[288,1024]{1,0:T(8,128)(2,1)} %project.5.own) | copy-start | bytes 1769476
